TPU v7x, 32 devices: a whole 2x2x4 slice. The times are simulated.
32 devices in a mesh: grp: 2 (over y), ao: 4 (over z), vir: 2 (over x), rep: 2 (over core).
Axes of the slice: x: 2, y: 2, z: 4, core: 2. Of those that a mesh axis runs over, the one named last changes fastest.
Arguments:
- half_ints: bfloat16 [8, 2, 24, 128, 128], P('grp', 'rep', 'ao'), parts along dimension 0, may hold values from -6 to 6
- coeff: bfloat16 [2560, 2048], P('rep', 'ao'), may hold values from -0.15625 to 0.15625
- eps_occ: float32 [400], replicated, may hold values from -1.5 to -0.5
- eps_vir: float32 [2048], replicated, may hold values from 0.5 to 2.5
- pair_occ: int32 [8, 2], P(('grp', 'ao')), parts along dimension 0, may hold values from 0 to 399
- tile_list: int32 [2, 24, 2], P('rep'), may hold values from 0 to 23, as said below
- shell_extra: int32 [2, 12], replicated, may hold values from 1 to 64, 512 in all within a row
Outputs:
- amplitudes: bfloat16 [8, 2048, 2048], P(('grp', 'ao'), 'rep', 'vir'), parts along dimension 0
There are 2 independent parts, one for each index of `grp`. A program takes and returns all parts, laid end to end along the dimension named above; an argument that names none is the same for every part. Nothing has to cross between parts.
Inputs may be any that keep to these rules, and one draw needn't show every extreme that they name: `tile_list`: column 0 is a row block within the half, below 12; column 1 is a block of all 24; every half has the tile (11, 23). `shell_extra`: each row sums to 512.
All inputs are finite; a program needn't handle non-finite values.
Results may differ from a plain program's by a relative error of at most 0.0085.
Values may be sent and summed in bfloat16 or wider, within the bound.
No kernel may reach another device: no remote copies, remote signals or barrier semaphores. Data moves between devices by JAX's collectives and lax.ppermute only.
A program may use at most 128 MiB of HBM per device.

v0:
```python
import jax
import jax.numpy as jnp
from jax import lax
from jax.sharding import PartitionSpec as P

NAO = 2560
TILE = 128
HALF_BLK = 12


def block_layout(shell_extra):
    shell_sizes = (TILE // 2 + shell_extra).reshape(-1)
    offsets = jnp.cumsum(shell_sizes) - shell_sizes
    columns = jnp.arange(TILE, dtype=jnp.int32)
    real_rows = offsets[:, None] + columns[None, :]
    valid_rows = columns[None, :] < shell_sizes[:, None]
    return (offsets, real_rows, valid_rows)


def padded_rows(matrix, real_rows, valid_rows):
    picked = jnp.take(matrix, jnp.minimum(real_rows, NAO - 1).reshape(-1), axis=0)
    picked = picked.reshape(real_rows.shape[0], TILE, matrix.shape[1])
    return jnp.where(valid_rows[:, :, None], picked, jnp.zeros_like(picked))


def packed_position(partial_starts, partial_length):
    positions = jnp.arange(partial_length, dtype=jnp.int32)
    block_of = (
        jnp.sum((partial_starts[None, :] <= positions[:, None]).astype(jnp.int32), axis=1) - 1
    )
    block_start = jnp.take(partial_starts, block_of)
    return block_of * TILE + positions - block_start


def local(half_ints, coeff, eps_occ, eps_vir, pair_occ, tile_list, shell_extra):
    vir_count = lax.axis_size("vir")
    rep_count = lax.axis_size("rep")
    vir_at = lax.axis_index("vir")
    rep_at = lax.axis_index("rep")
    partial_length = coeff.shape[0]
    full_width = coeff.shape[1] * lax.axis_size("ao")
    vir_width = full_width // vir_count
    local_tiles = lax.all_to_all(half_ints, "ao", split_axis=0, concat_axis=2, tiled=True)
    gathered = lax.all_gather(coeff, "ao", axis=1, tiled=True)
    own_cols = lax.dynamic_slice_in_dim(gathered, vir_at * vir_width, vir_width, 1)
    coeff_all = lax.all_gather(own_cols, "rep", axis=0, tiled=True)
    offsets, real_rows, valid_rows = block_layout(shell_extra)
    coeff_pad = padded_rows(coeff_all, real_rows, valid_rows)
    coeff_nu = jnp.take(coeff_pad, tile_list[0, :, 1], axis=0)
    products = jnp.einsum(
        "ptij,tjb->ptib", local_tiles[:, 0], coeff_nu, preferred_element_type=jnp.float32
    )
    blocks = jnp.arange(HALF_BLK, dtype=jnp.int32)
    one_hot = (tile_list[0, :, 0][:, None] == blocks[None, :]).astype(jnp.float32)
    padded_partial = jnp.einsum("tm,ptib->pmib", one_hot, products, precision=lax.Precision.HIGHEST)
    padded_partial = padded_partial.astype(jnp.bfloat16).reshape(
        products.shape[0], HALF_BLK * TILE, vir_width
    )
    partial_starts = (
        lax.dynamic_slice_in_dim(offsets, rep_at * HALF_BLK, HALF_BLK, 0) - rep_at * partial_length
    )
    packed_tile = jnp.take(padded_partial, packed_position(partial_starts, partial_length), axis=1)
    row_count = full_width // rep_count
    summed_block = lax.psum_scatter(
        jnp.einsum("ka,pkb->apb", gathered, packed_tile, preferred_element_type=jnp.float32).astype(
            jnp.bfloat16
        ),
        "rep",
        scatter_dimension=0,
        tiled=True,
    ).astype(jnp.float32)
    summed_block = jnp.transpose(summed_block, (1, 0, 2))
    energy_rows = lax.dynamic_slice_in_dim(eps_vir, rep_at * row_count, row_count, 0)
    energy_cols = lax.dynamic_slice_in_dim(eps_vir, vir_at * vir_width, vir_width, 0)
    pair_energy = jnp.take(eps_occ, pair_occ[:, 0]) + jnp.take(eps_occ, pair_occ[:, 1])
    denominator = (
        pair_energy[:, None, None] - energy_rows[None, :, None] - energy_cols[None, None, :]
    )
    return (summed_block / denominator).astype(jnp.bfloat16)


def solution(mesh):
    in_specs = (
        P("grp", "rep", "ao", None, None),
        P("rep", "ao"),
        P(),
        P(),
        P(("grp", "ao"), None),
        P("rep", None, None),
        P(),
    )
    out_specs = P(("grp", "ao"), "rep", "vir")
    return jax.shard_map(local, mesh=mesh, in_specs=in_specs, out_specs=out_specs, check_vma=False)
```

profile of v0, /device:TPU:9, one launch (start us, length us, event | category | flops | bytes accessed | tf_op | source)
XLA Modules:
  0.0 239.3 jit_solution(5328477057368363443)
XLA Ops:
  6.5 0.7 all-gather.3.cloned.1.call-update
  7.3 0.0 all-gather.5.cloned.1.call-start
  7.3 98.2 %all-gather.3.cloned.1.call-done = bf16[1280,2048]{1,0:T(8,128)(2,1)} async-done(((bf16[1280,512]{1,0:T(8,128)(2,1)}), bf16[1280,2048]{1,0:T(8,128)(2,1)}) %all-gather.3.cloned.1.call-update) | async-done | bytes 5242896 | tf_op jit(solution)/shard_map/all_gather | solution.py:44
  105.5 3.5 %constant_dynamic-slice_fusion = bf16[1280,1024]{1,0:T(8,128)(2,1)} fusion(bf16[1280,2048]{1,0:T(8,128)(2,1)} %all-gather.3.cloned.1.call-done, s32[]{:T(128)S(6)} %select_n.137), kind=kLoop, calls=%fused_computation.60 | loop fusion | bytes 5242884 | tf_op jit(solution)/shard_map/dynamic_slice | solution.py:45
  109.0 6.6 %all-to-all-start = ((bf16[4,1,6,128,128]{4,3,2,1,0:T(8,128)(2,1)}), bf16[4,1,6,128,128]{4,3,2,1,0:T(8,128)(2,1)S(1)}, u32[]{:S(2)}, u32[]{:S(2)}) async-start(bf16[4,1,6,128,128]{4,3,2,1,0:T(8,128)(2,1)} %param.7), calls=%async_computation | async-start | bytes 1572864 | tf_op jit(solution)/shard_map/all_to_all | solution.py:43
  115.6 0.1 reshape.455
  115.7 0.1 reshape.311
  115.8 0.1 reduce
  115.9 0.1 dynamic-slice_subtract_fusion.1
  116.0 0.7 fusion.22
  116.7 0.1 convert_reduce_fusion
  116.8 4.6 %fusion.13 = (s32[1280]{0:T(1024)S(1)}, s32[1280,1]{0,1:T(1,128)S(1)}) fusion(s32[]{:T(128)} %bitcast.5, s32[]{:T(128)} %bitcast.6, s32[]{:T(128)} %bitcast.7, s32[]{:T(128)} %bitcast.8, s32[]{:T(128)} %bitcast.9, s32[]{:T(128)} %bitcast.11, s32[]{:T(128)} %bitcast.10, s32[1280]{0:T(1024)S(1)} %get-tuple-element.39, s32[1280]{0:T(1024)S(1)} %get-tuple-element.38), kind=kLoop, calls=%fused_computation.45 | loop fusion | flops 17920 | bytes 20508 | tf_op jit(solution)/shard_map/jit(_take)/gather | solution.py:31
  121.5 0.1 compare_reduce_fusion.4
  121.6 3.2 %compare_and_fusion.1 = (pred[1280]{0:T(1024)(128)(4,1)S(1)}, s32[1280]{0:T(1024)S(1)}) fusion(s32[1280]{0:T(1024)S(1)} %convert_reduce_fusion, pred[1280]{0:T(1024)(128)(4,1)S(1)} %get-tuple-element.31, pred[1280]{0:T(1024)(128)(4,1)S(1)} %get-tuple-element.29, pred[1280]{0:T(1024)(128)(4,1)S(1)} %get-tuple-element.30, ...), kind=kLoop, calls=%fused_computation.43 | loop fusion | flops 28160 | bytes 23060 | tf_op jit(solution)/shard_map/jit(_take)/and | solution.py:62
  124.8 0.1 add_minimum_fusion
  125.0 0.1 iota_compare_fusion.1
  125.0 1.1 all-gather.5.cloned.1.call-done
  126.1 19.1 %gather_fusion = bf16[3072,1024]{1,0:T(8,128)(2,1)} fusion(bf16[2560,1024]{1,0:T(8,128)(2,1)} %all-gather.5.cloned.1.call-done, s32[3072]{0:T(1024)S(1)} %broadcast_clamp_fusion), kind=kCustom, calls=%fused_computation | custom fusion | bytes 12595200 | tf_op jit(solution)/shard_map/jit(_take)/gather | solution.py:21
  145.2 8.6 %copy.18 = bf16[24,128,1024]{1,2,0:T(8,128)(2,1)} copy(bf16[24,128,1024]{2,1,0:T(8,128)(2,1)} %bitcast.54) | data formatting | bytes 12582912 | tf_op jit(solution)/shard_map/jit(_take)/gather | solution.py:21
  153.9 6.2 %select_select_fusion = bf16[24,128,1024]{1,2,0:T(8,128)(2,1)} fusion(bf16[24,128,1024]{1,2,0:T(8,128)(2,1)} %copy.18, pred[24,128]{1,0:T(8,128)(4,1)S(1)} %get-tuple-element.57, pred[24,128]{1,0:T(8,128)(4,1)S(1)} %get-tuple-element.56), kind=kLoop, calls=%fused_computation.5 | loop fusion | flops 6291456 | bytes 12589056 | tf_op jit(solution)/shard_map/jit(_where)/select_n | solution.py:23
  160.0 7.2 %gather_fusion.1 = bf16[24,128,1024]{1,2,0:T(8,128)(2,1)} fusion(bf16[24,128,1024]{1,2,0:T(8,128)(2,1)} %select_select_fusion, s32[1024]{0:T(1024)S(1)} %pad_clamp_fusion.1), kind=kCustom, calls=%fused_computation.1 | custom fusion | bytes 12583008 | tf_op jit(solution)/shard_map/jit(_take)/gather | solution.py:49
  167.2 9.2 %fusion.3 = f32[24,128,1024]{1,2,0:T(8,128)} fusion(bf16[24,128,128]{2,1,0:T(8,128)(2,1)S(1)} %bitcast.55, bf16[24,128,1024]{1,2,0:T(8,128)(2,1)} %gather_fusion.1, pred[24]{0:T(512)(128)(4,1)S(1)} %compare_and_fusion.2), kind=kOutput, calls=%fused_computation.7 | convolution fusion | flops 808452096 | bytes 19660824 | tf_op jit(solution)/shard_map/ptij,tjb->ptib/dot_general | solution.py:50
  176.4 12.7 %copy.19 = f32[24,128,1024]{2,0,1:T(8,128)} copy(f32[24,128,1024]{1,2,0:T(8,128)} %fusion.3) | data formatting | bytes 25165824 | tf_op jit(solution)/shard_map/reshape.16
  189.1 8.1 %convert_bitcast_fusion.1 = bf16[1,12,128,1024]{3,1,2,0:T(8,128)(2,1)S(1)} fusion(f32[24,128,1024]{2,0,1:T(8,128)} %copy.19, s32[24]{0:T(128)S(1)} %slice_bitcast_fusion), kind=kOutput, calls=%fused_computation.11 | convolution fusion | flops 454557984 | bytes 15728736 | tf_op jit(solution)/shard_map/tm,ptib->pmib/dot_general | solution.py:55
  197.2 1.7 copy.20
  199.0 5.1 %gather_fusion.2 = bf16[1280,1024]{1,0:T(8,128)(2,1)} fusion(bf16[1536,1024]{1,0:T(8,128)(2,1)S(1)} %bitcast.53, s32[2048]{0:T(1024)S(1)} %pad_clamp_fusion), kind=kCustom, calls=%fused_computation.2 | custom fusion | bytes 5248000 | tf_op jit(solution)/shard_map/jit(_take)/gather | solution.py:62
  204.1 10.4 %convert_bitcast_fusion = bf16[2048,1,1024]{0,2,1:T(8,128)(2,1)} fusion(bf16[1280,2048]{1,0:T(8,128)(2,1)} %all-gather.3.cloned.1.call-done, bf16[1280,1024]{1,0:T(8,128)(2,1)} %gather_fusion.2, pred[1280]{0:T(1024)(128)(4,1)S(1)} %get-tuple-element.32), kind=kOutput, calls=%fused_computation.10 | convolution fusion | flops 5372116992 | bytes 12059904 | tf_op jit(solution)/shard_map/ka,pkb->apb/dot_general | solution.py:65
  214.5 0.6 fusion.21
  219.0 0.7 fusion.20
  220.9 6.9 %reduce-scatter.2.cloned.1.call-done = bf16[1024,1,1024]{0,2,1:T(8,128)(2,1)} async-done(((bf16[2048,1,1024]{0,2,1:T(8,128)(2,1)}), bf16[1024,1,1024]{0,2,1:T(8,128)(2,1)}) %reduce-scatter.2.cloned.1.call-update) | async-done | bytes 2097168 | tf_op jit(solution)/shard_map/reduce_scatter | solution.py:64
  227.9 2.3 fusion.6
  230.2 2.6 %copy.21 = bf16[1,1024,1024]{2,1,0:T(8,128)(2,1)} copy(bf16[1,1024,1024]{1,2,0:T(8,128)(2,1)S(1)} %fusion.6) | data formatting | bytes 4194304 | tf_op jit(solution)/shard_map/convert_element_type | solution.py:79
  (28 shorter events, 0.2 us)
Async XLA Ops:
  6.5 109.1 %copy-start.2 = (s32[2,12]{1,0:T(2,128)S(1)}, s32[2,12]{1,0:T(2,128)}, u32[]{:S(2)}) copy-start(s32[2,12]{1,0:T(2,128)} %param.13) | copy-start | bytes 292
  6.5 118.3 %copy-start.4 = (s32[1,24,2]{1,2,0:T(2,128)S(1)}, s32[1,24,2]{1,2,0:T(2,128)}, u32[]{:S(2)}) copy-start(s32[1,24,2]{1,2,0:T(2,128)} %param.12) | copy-start | bytes 580
  6.5 99.0 %all-gather.3.cloned.1.call-start = ((), (), s32[]{:S(2)}) async-start(), calls=%async_computation.2 | async-start | bytes 6553600 | tf_op jit(solution)/shard_map/all_gather | solution.py:44
  7.3 118.9 %all-gather.5.cloned.1.call-start = ((), (), s32[]{:S(2)}) async-start(), calls=%async_computation.3 | async-start | bytes 7864320 | tf_op jit(solution)/shard_map/all_gather | solution.py:46
  109.0 58.2 %all-to-all-start = ((bf16[4,1,6,128,128]{4,3,2,1,0:T(8,128)(2,1)}), bf16[4,1,6,128,128]{4,3,2,1,0:T(8,128)(2,1)S(1)}, u32[]{:S(2)}, u32[]{:S(2)}) async-start(bf16[4,1,6,128,128]{4,3,2,1,0:T(8,128)(2,1)} %param.7), calls=%async_computation | async-start | bytes 1572864 | tf_op jit(solution)/shard_map/all_to_all | solution.py:43
  115.6 112.3 %reduce-scatter.2.cloned.1.call-start = ((), (), s32[]{:S(2)}) async-start(), calls=%async_computation.4 | async-start | bytes 6291456 | tf_op jit(solution)/shard_map/reduce_scatter | solution.py:64
  204.0 10.5 %copy-start.1 = (s32[1,2]{1,0:T(1,128)S(1)}, s32[1,2]{1,0:T(1,128)}, u32[]{:S(2)}) copy-start(s32[1,2]{1,0:T(1,128)} %param.11) | copy-start | bytes 28
  204.0 14.9 %copy-start.3 = (f32[400]{0:T(512)S(1)}, f32[400]{0:T(512)}, u32[]{:S(2)}) copy-start(f32[400]{0:T(512)} %param.9) | copy-start | bytes 4804
  204.1 16.9 %copy-start = (f32[2048]{0:T(1024)S(1)}, f32[2048]{0:T(1024)}, u32[]{:S(2)}) copy-start(f32[2048]{0:T(1024)} %param.10) | copy-start | bytes 24580
Sparse Core Ops, SparseCore 0:
  8.9 96.5 all-gather.2
  109.1 16.9 all-gather.4
  214.6 13.2 reduce-scatter.1
where the time goes:
time: 241 us; the launch traced here: 239 us
  waiting for transfers between devices  107 us (44%)
  local copies, waits for them, and re-layouts  62.6 us (26%)
  matrix products  27.8 us (12%)
  between operations  18.4 us (8%)
  other arithmetic  17 us (7%)
  starting transfers between devices  6.61 us (3%)
    all_gather x1, waiting for transfers between devices, local(): gathered = lax.all_gather(coeff, 'ao', axis=1, tiled=True)  98.2 us
    gather x2, local copies, waits for them, and re-layouts, padded_rows(): jnp.take(matrix, jnp.minimum(real_rows, NAO - 1).reshape(-1), axis=0)  27.7 us
    another operation x2, local copies, waits for them, and re-layouts  12.8 us
    dot_general x1, matrix products, local(): jnp.einsum('ka,pkb->apb', gathered, packed_tile, preferred_element_type=j...  10.4 us
    dot_general x1, matrix products, local(): jnp.einsum('ptij,tjb->ptib', local_tiles[:, 0], coeff_nu, preferred_eleme...  9.2 us
    dot_general x1, matrix products, local(): jnp.einsum('tm,ptib->pmib', one_hot, products, precision=lax.Precision.HI...  8.14 us
    gather x1, local copies, waits for them, and re-layouts, local(): coeff_nu = jnp.take(coeff_pad, tile_list[0, :, 1], axis=0)  7.17 us
    reduce_scatter x1, waiting for transfers between devices, local(): lax.psum_scatter(jnp.einsum('ka,pkb->apb', gathered, packed_tile, preferr...  6.95 us
  transfers between devices with their start and end apart: 4, of which 3 were waited for; matrix products, arithmetic and copies ran while one was open for 22% of the time, Pallas kernels for 0%

commit v1 on v0

v1 whole, which is shorter than its diff:
```python
import functools

import jax
import jax.numpy as jnp
from jax import lax
from jax.experimental import pallas as pl
from jax.experimental.pallas import tpu as pltpu
from jax.sharding import PartitionSpec as P

TILE = 128
HALF_BLK = 12
LANES = 128
ROWS_WIN = 144
COLS_WIN = 256
RING = (0, 1, 3, 2)
SWAP = ((0, 1), (1, 0))
F32 = jnp.float32
BF16 = jnp.bfloat16


def shift_kernel(per_slot, n_refs, n_ao, row_total, *refs):
    place, list_own, list_other, extra = refs[:4]
    tiles = refs[4 : 4 + n_refs]
    shifted, row_base, col_base, offsets = refs[4 + n_refs :]
    blocks = 2 * HALF_BLK

    def lay(k, start):
        offsets[k] = start
        return start + TILE // 2 + extra[k // HALF_BLK, lax.rem(k, HALF_BLK)]

    lax.fori_loop(0, blocks, lay, jnp.int32(0))
    rows = lax.broadcasted_iota(jnp.int32, (TILE, TILE), 0)
    cols = lax.broadcasted_iota(jnp.int32, (TILE, TILE), 1)
    for r in range(n_refs):
        other, slot = r // (n_refs // 2), r % (n_refs // 2)
        listed = list_other if other else list_own
        half = place[0] if not other else 1 - place[0]
        ref = tiles[r]
        count = ref.shape[0]

        def one(i, carry, ref=ref, listed=listed, half=half, slot=slot, r=r, count=count):
            n = place[1 + slot] * count + i
            m = listed[0, n, 0] + HALF_BLK * half
            k = listed[0, n, 1]
            size_m = TILE // 2 + extra[m // HALF_BLK, lax.rem(m, HALF_BLK)]
            size_k = TILE // 2 + extra[k // HALF_BLK, lax.rem(k, HALF_BLK)]
            off_m = offsets[m]
            off_k = offsets[k]
            base_m = (off_m // 16) * 16
            base_k = jnp.minimum((off_k // LANES) * LANES, row_total - COLS_WIN)
            value = jnp.where((rows < size_m) & (cols < size_k), ref[i].astype(F32), 0.0)
            value = jnp.concatenate([value, jnp.zeros((TILE, COLS_WIN - TILE), F32)], axis=1)
            value = jnp.concatenate(
                [value, jnp.zeros((ROWS_WIN - TILE, COLS_WIN), F32)], axis=0
            )
            value = pltpu.roll(value, off_k - base_k, 1)
            value = pltpu.roll(value, off_m - base_m, 0)
            at = r * count + i
            shifted[at] = value.astype(BF16)
            row_base[at] = base_m
            col_base[at] = base_k
            return carry

        lax.fori_loop(0, count, one, 0)


def shift_tiles(place, list_own, list_other, shell_extra, tiles, row_total):
    count = tiles[0].shape[0]
    total = len(tiles) * count
    smem = pl.BlockSpec(memory_space=pltpu.SMEM)
    vmem = pl.BlockSpec(memory_space=pltpu.VMEM)
    return pl.pallas_call(
        functools.partial(shift_kernel, count, len(tiles), len(tiles) // 2, row_total),
        out_shape=(
            jax.ShapeDtypeStruct((total, ROWS_WIN, COLS_WIN), BF16),
            jax.ShapeDtypeStruct((total,), jnp.int32),
            jax.ShapeDtypeStruct((total,), jnp.int32),
        ),
        in_specs=[smem] * 4 + [vmem] * len(tiles),
        out_specs=(vmem, smem, smem),
        scratch_shapes=[pltpu.SMEM((2 * HALF_BLK,), jnp.int32)],
        compiler_params=pltpu.CompilerParams(vmem_limit_bytes=32 << 20),
        name="shift_tiles",
    )(place, list_own, list_other, shell_extra, *tiles)


def transform_kernel(layout, n_tiles, a_panels, b_panels, step_panels, *refs):
    place, row_base, col_base, pair_occ, eps_occ = refs[:5]
    shifted, eps_rows, eps_cols = refs[5:8]
    pieces = refs[8 : 8 + len(layout)]
    out, panels, total, held, sems = refs[8 + len(layout) :]
    step = pl.program_id(0)
    width = b_panels * LANES
    b_first = place[1] * b_panels
    row_total = panels.shape[1]

    @pl.when(step == 0)
    def _():
        copies = []
        for ref, (at, column, half_at, row) in zip(pieces, layout):
            rows = ref.shape[0]
            start = pl.multiple_of(place[half_at] * (row_total // 2) + row, 16)
            copies.append(
                pltpu.make_async_copy(
                    ref.at[:, pl.ds(column * LANES, LANES)],
                    panels.at[place[at], pl.ds(start, rows), :],
                    sems.at[len(copies)],
                )
            )
        for copy in copies:
            copy.start()
        total[...] = jnp.zeros_like(total)
        for copy in copies:
            copy.wait()

        def add(n, carry):
            base_m = pl.multiple_of(row_base[n], 16)
            base_k = pl.multiple_of(col_base[n], LANES)
            window = jnp.concatenate(
                [panels[b_first + j, pl.ds(base_k, COLS_WIN), :] for j in range(b_panels)], axis=1
            )
            total[pl.ds(base_m, ROWS_WIN), :] += jnp.dot(
                shifted[n], window, preferred_element_type=F32
            )
            return carry

        lax.fori_loop(0, n_tiles, add, 0)
        held[...] = total[pl.ds(0, row_total), :].astype(BF16)

    a_first = place[0] * a_panels + step * step_panels
    left = jnp.concatenate([panels[a_first + j] for j in range(step_panels)], axis=1)
    product = lax.dot_general(
        left, held[...], (((0,), (0,)), ((), ())), preferred_element_type=F32
    )
    energy = eps_occ[pair_occ[0, 0]] + eps_occ[pair_occ[0, 1]]
    denominator = energy - eps_rows[...] - eps_cols[pl.ds(place[1], 1), :]
    out[0] = (product / denominator).astype(BF16)


def transform(place, layout, bases, pair_occ, eps_occ, shifted, eps_vir, pieces, sizes):
    row_total, a_width, b_width, full_width = sizes
    a_panels, b_panels = a_width // LANES, b_width // LANES
    step_panels = 2
    steps = a_panels // step_panels
    n_tiles = shifted.shape[0]
    row_base, col_base = bases
    smem = pl.BlockSpec(memory_space=pltpu.SMEM)
    vmem = pl.BlockSpec(memory_space=pltpu.VMEM)
    refs = [pieces[piece[0]] for piece in layout]
    own_rows = lax.dynamic_slice_in_dim(eps_vir, lax.axis_index("rep") * a_width, a_width, 0)
    return pl.pallas_call(
        functools.partial(
            transform_kernel, [piece[1:] for piece in layout], n_tiles, a_panels, b_panels,
            step_panels,
        ),
        grid=(steps,),
        out_shape=jax.ShapeDtypeStruct((1, a_width, b_width), BF16),
        in_specs=[smem] * 5
        + [vmem, pl.BlockSpec((step_panels * LANES, 1), lambda i: (i, 0)), vmem]
        + [pl.BlockSpec(memory_space=pl.ANY)] * len(refs),
        out_specs=pl.BlockSpec((1, step_panels * LANES, b_width), lambda i: (0, i, 0)),
        scratch_shapes=[
            pltpu.VMEM((full_width // LANES, row_total, LANES), BF16),
            pltpu.VMEM((row_total + TILE, b_width), F32),
            pltpu.VMEM((row_total, b_width), BF16),
            pltpu.SemaphoreType.DMA((len(refs),)),
        ],
        compiler_params=pltpu.CompilerParams(vmem_limit_bytes=48 << 20),
        name="transform",
    )(
        place, row_base, col_base, pair_occ, eps_occ,
        shifted, own_rows.reshape(a_width, 1), eps_vir.reshape(-1, b_width), *refs,
    )


def ring_pairs(distance):
    return [(RING[i], RING[(i + distance) % 4]) for i in range(4)]


def other_core(value):
    return lax.ppermute(value, "rep", SWAP)


def exchange_small(half_ints, coeff):
    z, x, y = lax.axis_index("ao"), lax.axis_index("vir"), lax.axis_index("grp")
    ring = jnp.asarray(RING, jnp.int32)
    spot = jnp.where(z == 3, 2, jnp.where(z == 2, 3, z))
    quarter = y * 2 + x
    shards = [ring[(spot - k) % 4] for k in range(4)]
    rows, width = coeff.shape
    part = width // LANES
    middle = rows // 2
    moving = lax.dynamic_slice_in_dim(coeff, quarter * LANES, LANES, 1)
    pieces = [(coeff, 4 * shards[0] + j, j, 0) for j in range(part)]
    tiles = [lax.dynamic_index_in_dim(half_ints[:, 0], z, 0, False)]
    for k in (1, 2, 3):
        moving = lax.ppermute(moving, "ao", ring_pairs(1))
        leaving = lax.dynamic_index_in_dim(half_ints[:, 0], ring[(spot + k) % 4], 0, False)
        tiles.append(lax.ppermute(leaving, "ao", ring_pairs(k)))
        by_x = lax.ppermute(moving, "vir", SWAP)
        by_y = lax.ppermute(moving, "grp", SWAP)
        far_x = lax.ppermute(by_y[:middle], "vir", SWAP)
        far_y = lax.ppermute(by_x[middle:], "grp", SWAP)
        first = part * shards[k]
        pieces += [
            (moving, first + quarter, 0, 0),
            (by_x, first + (quarter ^ 1), 0, 0),
            (by_y, first + (quarter ^ 2), 0, 0),
            (far_x, first + (quarter ^ 3), 0, 0),
            (far_y, first + (quarter ^ 3), 0, middle),
        ]
    return pieces, tiles, shards


def exchange_any(half_ints, coeff):
    count = lax.axis_size("ao")
    part = coeff.shape[1] // LANES
    gathered = lax.all_gather(coeff, "ao", axis=0, tiled=False)
    tiles = lax.all_to_all(half_ints, "ao", split_axis=0, concat_axis=2, tiled=True)[0, 0]
    tiles = tiles.reshape((count, -1) + tiles.shape[1:])
    pieces = [
        (gathered[s], jnp.int32(s * part + j), j, 0) for s in range(count) for j in range(part)
    ]
    return pieces, [tiles[s] for s in range(count)], [jnp.int32(s) for s in range(count)]


def local(half_ints, coeff, eps_occ, eps_vir, pair_occ, tile_list, shell_extra):
    sizes = tuple(lax.axis_size(name) for name in ("grp", "ao", "vir"))
    rows, width = coeff.shape
    row_total = rows * lax.axis_size("rep")
    full_width = width * sizes[1]
    small = sizes == (2, 4, 2) and width == 4 * LANES
    pieces, tiles, order = (exchange_small if small else exchange_any)(half_ints, coeff)
    core = lax.axis_index("rep").astype(jnp.int32)
    vir = lax.axis_index("vir").astype(jnp.int32)

    swapped = {}
    arrays, layout, ids = [], [], []
    for piece, panel, column, row in pieces:
        if id(piece) not in swapped:
            swapped[id(piece)] = len(arrays)
            arrays += [piece, other_core(piece)]
        at = swapped[id(piece)]
        ids.append(panel)
        layout.append((at, 3 + len(ids), column, 2, row))
        layout.append((at + 1, 3 + len(ids), column, 3, row))
    place = jnp.stack([core, vir, core, 1 - core] + [jnp.asarray(i, jnp.int32) for i in ids])

    tile_place = jnp.stack([core] + [jnp.asarray(s, jnp.int32) for s in order])
    all_tiles = tiles + [other_core(t) for t in tiles]
    shifted, row_base, col_base = shift_tiles(
        tile_place, tile_list, other_core(tile_list), shell_extra, all_tiles, row_total
    )
    return transform(
        place, layout, (row_base, col_base), pair_occ, eps_occ, shifted, eps_vir, arrays,
        (row_total, full_width // lax.axis_size("rep"), full_width // sizes[2], full_width),
    )


def solution(mesh):
    in_specs = (
        P("grp", "rep", "ao", None, None),
        P("rep", "ao"),
        P(),
        P(),
        P(("grp", "ao"), None),
        P("rep", None, None),
        P(),
    )
    out_specs = P(("grp", "ao"), "rep", "vir")
    return jax.shard_map(local, mesh=mesh, in_specs=in_specs, out_specs=out_specs, check_vma=False)
```

time: 241 us -> 138 us (0.57)
  waiting for transfers between devices: 107 us -> 21 us
  starting transfers between devices: 6.61 us -> 43.7 us
  Pallas kernels: 0 us -> 36.5 us
  local copies, waits for them, and re-layouts: 62.6 us -> 26.3 us
  matrix products: 27.8 us -> 0 us
  other arithmetic: 17 us -> 0 us
  between operations: 18.4 us -> 8.32 us
    all_gather x2 -> x0, waiting for transfers between devices: 99.3 us -> none  [the longest x1 98.2 us: local(): gathered = lax.all_gather(coeff, 'ao', axis=1, tiled=True)]
    ppermute x0 -> x39, starting transfers between devices: none -> 43.7 us  [the longest x21 27.5 us: other_core(): return lax.ppermute(value, 'rep', SWAP)]
    gather x6 -> x0, local copies, waits for them, and re-layouts: 41.4 us -> none  [the longest x2 27.7 us: padded_rows(): jnp.take(matrix, jnp.minimum(real_rows, NAO - 1).reshape(-1), axis=0)]
    pallas_call x0 -> x2, Pallas kernels: none -> 36.5 us  [the longest x1 27.2 us: transform(): pl.pallas_call(functools.partial(transform_kernel, [piece[1:] for piece i...]
    dot_general x3 -> x0, matrix products: 27.8 us -> none  [the longest x1 10.4 us: local(): jnp.einsum('ka,pkb->apb', gathered, packed_tile, preferred_element_type=j...]
    ppermute x0 -> x39, waiting for transfers between devices: none -> 21 us  [the longest x3 7.58 us: exchange_small(): moving = lax.ppermute(moving, 'ao', ring_pairs(1))]
    unnamed x10 -> x87, local copies, waits for them, and re-layouts: 0.02 us -> 18 us
    another operation x2, local copies, waits for them, and re-layouts: 12.8 us -> 2.64 us  [the longest x1 2.54 us: local(): tile_place = jnp.stack([core] + [jnp.asarray(s, jnp.int32) for s in order])]
  transfers between devices with their start and end apart: 4 -> 39, of which waited for: 3 -> 9; matrix products, arithmetic and copies ran while one was open for 22% -> 5% of each run, Pallas kernels for 0% -> 7%
where the time goes in v1:
time: 138 us; the launch traced here: 136 us
  starting transfers between devices  43.7 us (32%)
  Pallas kernels  36.5 us (26%)
  local copies, waits for them, and re-layouts  26.3 us (19%)
  waiting for transfers between devices  21 us (15%)
  between operations  8.32 us (6%)
    ppermute x21, starting transfers between devices, other_core(): return lax.ppermute(value, 'rep', SWAP)  27.5 us
    pallas_call x1, Pallas kernels, transform(): pl.pallas_call(functools.partial(transform_kernel, [piece[1:] for piece i...  27.2 us
    unnamed x87, local copies, waits for them, and re-layouts  18 us
    pallas_call x1, Pallas kernels, shift_tiles(): pl.pallas_call(functools.partial(shift_kernel, count, len(tiles), len(til...  9.31 us
    ppermute x3, waiting for transfers between devices, exchange_small(): moving = lax.ppermute(moving, 'ao', ring_pairs(1))  7.58 us
    ppermute x3, waiting for transfers between devices, exchange_small(): far_y = lax.ppermute(by_x[middle:], 'grp', SWAP)  4.66 us
    ppermute x3, waiting for transfers between devices, exchange_small(): tiles.append(lax.ppermute(leaving, 'ao', ring_pairs(k)))  4.48 us
    ppermute x3, starting transfers between devices, exchange_small(): moving = lax.ppermute(moving, 'ao', ring_pairs(1))  3.47 us
  transfers between devices with their start and end apart: 39, of which 9 were waited for; matrix products, arithmetic and copies ran while one was open for 5% of the time, Pallas kernels for 7%

profile of v1, /device:TPU:9, one launch (start us, length us, event | category | flops | bytes accessed | tf_op | source)
XLA Modules:
  0.0 135.8 jit_solution(4379085848708100126)
XLA Ops:
  0.0 1.1 constant_dynamic-slice_fusion
  1.1 2.4 %collective-permute-start.9 = (bf16[1280,128]{1,0:T(8,128)(2,1)S(1)}, bf16[1280,128]{1,0:T(8,128)(2,1)S(1)}, u32[]{:S(2)}, u32[]{:S(2)}) collective-permute-start(bf16[1280,128]{1,0:T(8,128)(2,1)S(1)} %constant_dynamic-slice_fusion), channel_id=1, source_target_pairs={{0,4},{4,12},{12,8},{8,0},{1,5},{5,13},{13,9},{9,1},{2,6},{6,14},{... | collective-permute-start | bytes 983048 | tf_op jit(solution)/shard_map/ppermute | solution.py:197
  3.4 1.6 %fusion = (s32[1]{0:T(128)}, s32[1]{0:T(128)}, s32[1]{0:T(128)}, s32[1]{0:T(128)}, s32[1]{0:T(128)}, /*index=5*/s32[1]{0:T(128)}, s32[1]{0:T(128)}) fusion(s32[4]{0:T(128)} %constant.99.clone, s32[]{:T(128)S(6)} %select_n.96, s32[]{:T(128)S(6)} %select_n.90, s32[]{:T(128)S(6)} %select_n.87, s32[]{:T(128)S(6)} %select_n.85, s32[]{:T(128)S(6)} %select_n.83, ...), kind=kLoop, calls=%fused_computation.5 | loop fusion | bytes 84 | tf_op jit(solution)/shard_map/dynamic_slice | solution.py:198
  10.5 1.3 collective-permute-start.13
  12.2 2.2 %collective-permute-start.1 = (bf16[6,128,128]{2,1,0:T(8,128)(2,1)S(1)}, bf16[6,128,128]{2,1,0:T(8,128)(2,1)S(1)}, u32[]{:S(2)}, u32[]{:S(2)}) collective-permute-start(bf16[6,128,128]{2,1,0:T(8,128)(2,1)S(1)} %get-tuple-element.12), channel_id=1, source_target_pairs={{0,4},{4,12},{12,8},{8,0},{1,5},{5,13},{13,9},{9,1},{2,6},{6,14},{... | collective-permute-start | bytes 589832 | tf_op jit(solution)/shard_map/ppermute | solution.py:199
  14.8 2.7 %collective-permute-start = (s32[1,24,2]{2,1,0:T(8,128)S(1)}, s32[1,24,2]{2,1,0:T(8,128)S(1)}, u32[]{:S(2)}, u32[]{:S(2)}) collective-permute-start(s32[1,24,2]{2,1,0:T(8,128)S(1)} %copy.12.refs_1_), channel_id=1, source_target_pairs={{0,1},{1,0},{2,3},{3,2},{4,5},{5,4},{6,7},{7,6},{8,9},{9,8},{10,11... | collective-permute-start | bytes 584 | tf_op jit(solution)/shard_map/ppermute | solution.py:181
  18.3 1.2 collective-permute-start.11
  19.6 2.7 %collective-permute-start.4 = (bf16[6,128,128]{2,1,0:T(8,128)(2,1)S(1)}, bf16[6,128,128]{2,1,0:T(8,128)(2,1)S(1)}, u32[]{:S(2)}, u32[]{:S(2)}) collective-permute-start(bf16[6,128,128]{2,1,0:T(8,128)(2,1)S(1)} %get-tuple-element.13.refs_4_), channel_id=1, source_target_pairs={{0,1},{1,0},{2,3},{3,2},{4,5},{5,4},{6,7},{7,6},{8,9},{9,8},{10,11... | collective-permute-start | bytes 589832 | tf_op jit(solution)/shard_map/ppermute | solution.py:181
  22.4 5.2 %collective-permute-start.7 = (bf16[6,128,128]{2,1,0:T(8,128)(2,1)S(1)}, bf16[6,128,128]{2,1,0:T(8,128)(2,1)S(1)}, u32[]{:S(2)}, u32[]{:S(2)}) collective-permute-start(bf16[6,128,128]{2,1,0:T(8,128)(2,1)S(1)} %collective-permute-done.3.refs_7_), channel_id=1, source_target_pairs={{0,1},{1,0},{2,3},{3,2},{4,5},{5,4},{6,7},{7,6},{8,9},{9,8},{10,11... | collective-permute-start | bytes 589832 | tf_op jit(solution)/shard_map/ppermute | solution.py:181
  27.6 4.3 %collective-permute-done.2.refs_6_ = bf16[6,128,128]{2,1,0:T(8,128)(2,1)S(1)} collective-permute-done((bf16[6,128,128]{2,1,0:T(8,128)(2,1)S(1)}, bf16[6,128,128]{2,1,0:T(8,128)(2,1)S(1)}, u32[]{:S(2)}, u32[]{:S(2)}) %collective-permute-start.2) | collective-permute-done | bytes 196640 | tf_op jit(solution)/shard_map/ppermute | solution.py:199
  33.5 1.2 collective-permute-start.15
  35.0 7.1 %collective-permute-done.19.refs_26_ = bf16[1280,128]{1,0:T(8,128)(2,1)S(1)} collective-permute-done((bf16[1280,128]{1,0:T(8,128)(2,1)S(1)}, bf16[1280,128]{1,0:T(8,128)(2,1)S(1)}, u32[]{:S(2)}, u32[]{:S(2)}) %collective-permute-start.19) | collective-permute-done | bytes 327712 | tf_op jit(solution)/shard_map/ppermute | solution.py:197
  42.1 1.1 collective-permute-start.29
  44.1 1.2 collective-permute-start.16
  46.7 1.2 collective-permute-start.21
  50.5 1.7 %collective-permute-start.14 = (bf16[1280,128]{1,0:T(8,128)(2,1)S(1)}, bf16[1280,128]{1,0:T(8,128)(2,1)S(1)}, u32[]{:S(2)}, u32[]{:S(2)}) collective-permute-start(bf16[1280,128]{1,0:T(8,128)(2,1)S(1)} %collective-permute-done.13.refs_20_), channel_id=1, source_target_pairs={{0,1},{1,0},{2,3},{3,2},{4,5},{5,4},{6,7},{7,6},{8,9},{9,8},{10,11... | collective-permute-start | bytes 983048 | tf_op jit(solution)/shard_map/ppermute | solution.py:181
  52.2 1.8 %collective-permute-start.12 = (bf16[1280,128]{1,0:T(8,128)(2,1)S(1)}, bf16[1280,128]{1,0:T(8,128)(2,1)S(1)}, u32[]{:S(2)}, u32[]{:S(2)}) collective-permute-start(bf16[1280,128]{1,0:T(8,128)(2,1)S(1)} %collective-permute-done.11.refs_18_), channel_id=1, source_target_pairs={{0,1},{1,0},{2,3},{3,2},{4,5},{5,4},{6,7},{7,6},{8,9},{9,8},{10,11... | collective-permute-start | bytes 983048 | tf_op jit(solution)/shard_map/ppermute | solution.py:181
  54.0 1.4 %collective-permute-done.21.refs_28_ = bf16[1280,128]{1,0:T(8,128)(2,1)S(1)} collective-permute-done((bf16[1280,128]{1,0:T(8,128)(2,1)S(1)}, bf16[1280,128]{1,0:T(8,128)(2,1)S(1)}, u32[]{:S(2)}, u32[]{:S(2)}) %collective-permute-start.21) | collective-permute-done | bytes 327712 | tf_op jit(solution)/shard_map/ppermute | solution.py:200
  55.4 1.2 collective-permute-start.25
  56.7 1.2 collective-permute-start.33
  58.5 1.1 collective-permute-done.25.refs_32_
  59.6 3.6 %collective-permute-start.30 = (bf16[1280,128]{1,0:T(8,128)(2,1)S(1)}, bf16[1280,128]{1,0:T(8,128)(2,1)S(1)}, u32[]{:S(2)}, u32[]{:S(2)}) collective-permute-start(bf16[1280,128]{1,0:T(8,128)(2,1)S(1)} %collective-permute-done.29.refs_36_), channel_id=1, source_target_pairs={{0,1},{1,0},{2,3},{3,2},{4,5},{5,4},{6,7},{7,6},{8,9},{9,8},{10,11... | collective-permute-start | bytes 983048 | tf_op jit(solution)/shard_map/ppermute | solution.py:181
  63.2 4.7 %collective-permute-done.27.refs_34_ = bf16[640,128]{1,0:T(8,128)(2,1)S(1)} collective-permute-done((bf16[640,128]{1,0:T(8,128)(2,1)S(1)}, bf16[640,128]{1,0:T(8,128)(2,1)S(1)}, u32[]{:S(2)}, u32[]{:S(2)}) %collective-permute-start.27) | collective-permute-done | bytes 163872 | tf_op jit(solution)/shard_map/ppermute | solution.py:203
  67.9 2.5 %collective-permute-start.24 = (bf16[1280,128]{1,0:T(8,128)(2,1)S(1)}, bf16[1280,128]{1,0:T(8,128)(2,1)S(1)}, u32[]{:S(2)}, u32[]{:S(2)}) collective-permute-start(bf16[1280,128]{1,0:T(8,128)(2,1)S(1)} %collective-permute-done.23.refs_30_), channel_id=1, source_target_pairs={{0,1},{1,0},{2,3},{3,2},{4,5},{5,4},{6,7},{7,6},{8,9},{9,8},{10,11... | collective-permute-start | bytes 983048 | tf_op jit(solution)/shard_map/ppermute | solution.py:181
  75.2 1.2 collective-permute-start.37
  77.1 1.0 collective-permute-start.34
  79.7 1.3 collective-permute-start.36
  84.4 2.5 %stack.76.refs_0_ = s32[5]{0:T(128)S(1)} concatenate(s32[1]{0:T(128)} %bitcast, s32[1]{0:T(128)} %get-tuple-element.20, s32[1]{0:T(128)} %get-tuple-element.19, s32[1]{0:T(128)} %get-tuple-element.18, s32[1]{0:T(128)} %get-tuple-element.17), dimensions={0} | concatenate | bytes 40 | tf_op jit(solution)/shard_map/stack | solution.py:249
  87.0 1.0 copy.13.refs_6_
  94.7 9.3 %shift_tiles.1 = (bf16[48,144,256]{2,1,0:T(8,128)(2,1)S(1)}, s32[48]{0:T(128)S(1)}, s32[48]{0:T(128)S(1)}) custom-call(s32[5]{0:T(128)S(1)} %stack.76.refs_0_, s32[1,24,2]{2,1,0:T(8,128)S(1)} %copy.12.refs_1_, s32[1,24,2]{2,1,0:T(8,128)S(1)} %collective-permute-done.refs_2_, s32[2,12]{1,0:T(2,128)S(1)} %copy-done.36, ...), custom_call_target="tpu_custom_call" | custom-call | tf_op jit(solution)/shard_map/shift_tiles/pallas_call | solution.py:72
  104.0 1.8 %copy-done = bf16[48,144,256]{2,1,0:T(8,128)(2,1)} copy-done((bf16[48,144,256]{2,1,0:T(8,128)(2,1)}, bf16[48,144,256]{2,1,0:T(8,128)(2,1)S(1)}, u32[]{:S(2)}) %copy-start) | copy-done | bytes 3538968
  108.6 27.2 %transform.1 = bf16[1,1024,1024]{2,1,0:T(8,128)(2,1)} custom-call(s32[23]{0:T(128)S(1)} %stack.75.refs_0_, s32[48]{0:T(128)S(1)} %get-tuple-element.8.refs_1_, s32[48]{0:T(128)S(1)} %get-tuple-element.9.refs_2_, s32[1,2]{1,0:T(1,128)S(1)} %copy-done.37, f32[400]{0:T(512)S(1)} %copy-done.35, bf16[48,144,256]{2,1,0:T(8,128)(2,1)} %copy-done, ...), custom_call_target="tpu_custom_call" | custom-call | tf_op jit(solution)/shard_map/transform/pallas_call | solution.py:151
  (149 shorter events, 26.5 us)
Async XLA Ops:
  1.1 9.4 %collective-permute-start.9 = (bf16[1280,128]{1,0:T(8,128)(2,1)S(1)}, bf16[1280,128]{1,0:T(8,128)(2,1)S(1)}, u32[]{:S(2)}, u32[]{:S(2)}) collective-permute-start(bf16[1280,128]{1,0:T(8,128)(2,1)S(1)} %constant_dynamic-slice_fusion), channel_id=1, source_target_pairs={{0,4},{4,12},{12,8},{8,0},{1,5},{5,13},{13,9},{9,1},{2,6},{6,14},{... | collective-permute-start | bytes 983048 | tf_op jit(solution)/shard_map/ppermute | solution.py:197
  10.5 22.3 %collective-permute-start.13 = (bf16[1280,128]{1,0:T(8,128)(2,1)S(1)}, bf16[1280,128]{1,0:T(8,128)(2,1)S(1)}, u32[]{:S(2)}, u32[]{:S(2)}) collective-permute-start(bf16[1280,128]{1,0:T(8,128)(2,1)S(1)} %collective-permute-done.9.refs_16_), channel_id=1, source_target_pairs={{0,16},{16,0},{1,17},{17,1},{2,18},{18,2},{3,19},{19,3},{4,20},{20... | collective-permute-start | bytes 983048 | tf_op jit(solution)/shard_map/ppermute | solution.py:201
  11.9 7.6 %collective-permute-start.3 = (bf16[6,128,128]{2,1,0:T(8,128)(2,1)S(1)}, bf16[6,128,128]{2,1,0:T(8,128)(2,1)S(1)}, u32[]{:S(2)}, u32[]{:S(2)}) collective-permute-start(bf16[6,128,128]{2,1,0:T(8,128)(2,1)S(1)} %get-tuple-element.11), channel_id=1, source_target_pairs={{0,8},{4,0},{12,4},{8,12},{1,9},{5,1},{13,5},{9,13},{2,10},{6,2},{... | collective-permute-start | bytes 589832 | tf_op jit(solution)/shard_map/ppermute | solution.py:199
  12.2 10.3 %collective-permute-start.1 = (bf16[6,128,128]{2,1,0:T(8,128)(2,1)S(1)}, bf16[6,128,128]{2,1,0:T(8,128)(2,1)S(1)}, u32[]{:S(2)}, u32[]{:S(2)}) collective-permute-start(bf16[6,128,128]{2,1,0:T(8,128)(2,1)S(1)} %get-tuple-element.12), channel_id=1, source_target_pairs={{0,4},{4,12},{12,8},{8,0},{1,5},{5,13},{13,9},{9,1},{2,6},{6,14},{... | collective-permute-start | bytes 589832 | tf_op jit(solution)/shard_map/ppermute | solution.py:199
  14.4 17.6 %collective-permute-start.2 = (bf16[6,128,128]{2,1,0:T(8,128)(2,1)S(1)}, bf16[6,128,128]{2,1,0:T(8,128)(2,1)S(1)}, u32[]{:S(2)}, u32[]{:S(2)}) collective-permute-start(bf16[6,128,128]{2,1,0:T(8,128)(2,1)S(1)} %get-tuple-element.14), channel_id=1, source_target_pairs={{0,12},{4,8},{12,0},{8,4},{1,13},{5,9},{13,1},{9,5},{2,14},{6,10},... | collective-permute-start | bytes 589832 | tf_op jit(solution)/shard_map/ppermute | solution.py:199
  18.3 14.5 %collective-permute-start.11 = (bf16[1280,128]{1,0:T(8,128)(2,1)S(1)}, bf16[1280,128]{1,0:T(8,128)(2,1)S(1)}, u32[]{:S(2)}, u32[]{:S(2)}) collective-permute-start(bf16[1280,128]{1,0:T(8,128)(2,1)S(1)} %collective-permute-done.9.refs_16_), channel_id=1, source_target_pairs={{0,2},{2,0},{1,3},{3,1},{4,6},{6,4},{5,7},{7,5},{8,10},{10,8},{9,1... | collective-permute-start | bytes 983048 | tf_op jit(solution)/shard_map/ppermute | solution.py:200
  19.6 13.4 %collective-permute-start.4 = (bf16[6,128,128]{2,1,0:T(8,128)(2,1)S(1)}, bf16[6,128,128]{2,1,0:T(8,128)(2,1)S(1)}, u32[]{:S(2)}, u32[]{:S(2)}) collective-permute-start(bf16[6,128,128]{2,1,0:T(8,128)(2,1)S(1)} %get-tuple-element.13.refs_4_), channel_id=1, source_target_pairs={{0,1},{1,0},{2,3},{3,2},{4,5},{5,4},{6,7},{7,6},{8,9},{9,8},{10,11... | collective-permute-start | bytes 589832 | tf_op jit(solution)/shard_map/ppermute | solution.py:181
  22.4 11.1 %collective-permute-start.7 = (bf16[6,128,128]{2,1,0:T(8,128)(2,1)S(1)}, bf16[6,128,128]{2,1,0:T(8,128)(2,1)S(1)}, u32[]{:S(2)}, u32[]{:S(2)}) collective-permute-start(bf16[6,128,128]{2,1,0:T(8,128)(2,1)S(1)} %collective-permute-done.3.refs_7_), channel_id=1, source_target_pairs={{0,1},{1,0},{2,3},{3,2},{4,5},{5,4},{6,7},{7,6},{8,9},{9,8},{10,11... | collective-permute-start | bytes 589832 | tf_op jit(solution)/shard_map/ppermute | solution.py:181
  32.8 9.3 %collective-permute-start.19 = (bf16[1280,128]{1,0:T(8,128)(2,1)S(1)}, bf16[1280,128]{1,0:T(8,128)(2,1)S(1)}, u32[]{:S(2)}, u32[]{:S(2)}) collective-permute-start(bf16[1280,128]{1,0:T(8,128)(2,1)S(1)} %collective-permute-done.9.refs_16_), channel_id=1, source_target_pairs={{0,4},{4,12},{12,8},{8,0},{1,5},{5,13},{13,9},{9,1},{2,6},{6,14},{... | collective-permute-start | bytes 983048 | tf_op jit(solution)/shard_map/ppermute | solution.py:197
  32.8 10.4 %collective-permute-start.6 = (bf16[6,128,128]{2,1,0:T(8,128)(2,1)S(1)}, bf16[6,128,128]{2,1,0:T(8,128)(2,1)S(1)}, u32[]{:S(2)}, u32[]{:S(2)}) collective-permute-start(bf16[6,128,128]{2,1,0:T(8,128)(2,1)S(1)} %collective-permute-done.2.refs_6_), channel_id=1, source_target_pairs={{0,1},{1,0},{2,3},{3,2},{4,5},{5,4},{6,7},{7,6},{8,9},{9,8},{10,11... | collective-permute-start | bytes 589832 | tf_op jit(solution)/shard_map/ppermute | solution.py:181
  33.0 13.7 %collective-permute-start.10 = (bf16[1280,128]{1,0:T(8,128)(2,1)S(1)}, bf16[1280,128]{1,0:T(8,128)(2,1)S(1)}, u32[]{:S(2)}, u32[]{:S(2)}) collective-permute-start(bf16[1280,128]{1,0:T(8,128)(2,1)S(1)} %collective-permute-done.9.refs_16_), channel_id=1, source_target_pairs={{0,1},{1,0},{2,3},{3,2},{4,5},{5,4},{6,7},{7,6},{8,9},{9,8},{10,11... | collective-permute-start | bytes 983048 | tf_op jit(solution)/shard_map/ppermute | solution.py:181
  33.5 10.6 %collective-permute-start.15 = (bf16[640,128]{1,0:T(8,128)(2,1)S(1)}, bf16[640,128]{1,0:T(8,128)(2,1)S(1)}, u32[]{:S(2)}, u32[]{:S(2)}) collective-permute-start(bf16[640,128]{1,0:T(8,128)(2,1)S(1)} %slice.24), channel_id=1, source_target_pairs={{0,2},{2,0},{1,3},{3,1},{4,6},{6,4},{5,7},{7,5},{8,10},{10,8},{9,1... | collective-permute-start | bytes 491528 | tf_op jit(solution)/shard_map/ppermute | solution.py:202
  34.8 11.2 %collective-permute-start.17 = (bf16[640,128]{1,0:T(8,128)(2,1)S(1)}, bf16[640,128]{1,0:T(8,128)(2,1)S(1)}, u32[]{:S(2)}, u32[]{:S(2)}) collective-permute-start(bf16[640,128]{1,0:T(8,128)(2,1)S(1)} %slice.25), channel_id=1, source_target_pairs={{0,16},{16,0},{1,17},{17,1},{2,18},{18,2},{3,19},{19,3},{4,20},{20... | collective-permute-start | bytes 491528 | tf_op jit(solution)/shard_map/ppermute | solution.py:203
  42.1 8.4 %collective-permute-start.29 = (bf16[1280,128]{1,0:T(8,128)(2,1)S(1)}, bf16[1280,128]{1,0:T(8,128)(2,1)S(1)}, u32[]{:S(2)}, u32[]{:S(2)}) collective-permute-start(bf16[1280,128]{1,0:T(8,128)(2,1)S(1)} %collective-permute-done.19.refs_26_), channel_id=1, source_target_pairs={{0,4},{4,12},{12,8},{8,0},{1,5},{5,13},{13,9},{9,1},{2,6},{6,14},{... | collective-permute-start | bytes 983048 | tf_op jit(solution)/shard_map/ppermute | solution.py:197
  43.9 8.3 %collective-permute-start.23 = (bf16[1280,128]{1,0:T(8,128)(2,1)S(1)}, bf16[1280,128]{1,0:T(8,128)(2,1)S(1)}, u32[]{:S(2)}, u32[]{:S(2)}) collective-permute-start(bf16[1280,128]{1,0:T(8,128)(2,1)S(1)} %collective-permute-done.19.refs_26_), channel_id=1, source_target_pairs={{0,16},{16,0},{1,17},{17,1},{2,18},{18,2},{3,19},{19,3},{4,20},{20... | collective-permute-start | bytes 983048 | tf_op jit(solution)/shard_map/ppermute | solution.py:201
  46.7 8.8 %collective-permute-start.21 = (bf16[1280,128]{1,0:T(8,128)(2,1)S(1)}, bf16[1280,128]{1,0:T(8,128)(2,1)S(1)}, u32[]{:S(2)}, u32[]{:S(2)}) collective-permute-start(bf16[1280,128]{1,0:T(8,128)(2,1)S(1)} %collective-permute-done.19.refs_26_), channel_id=1, source_target_pairs={{0,2},{2,0},{1,3},{3,1},{4,6},{6,4},{5,7},{7,5},{8,10},{10,8},{9,1... | collective-permute-start | bytes 983048 | tf_op jit(solution)/shard_map/ppermute | solution.py:200
  48.6 57.2 %collective-permute-start.8 = (bf16[1280,512]{1,0:T(8,128)(2,1)}, bf16[1280,512]{1,0:T(8,128)(2,1)}, u32[]{:S(2)}, u32[]{:S(2)}) collective-permute-start(bf16[1280,512]{1,0:T(8,128)(2,1)} %refs_14_.1), channel_id=1, source_target_pairs={{0,1},{1,0},{2,3},{3,2},{4,5},{5,4},{6,7},{7,6},{8,9},{9,8},{10,11... | collective-permute-start | bytes 3932168 | tf_op jit(solution)/shard_map/ppermute | solution.py:181
  50.0 6.6 %collective-permute-start.20 = (bf16[1280,128]{1,0:T(8,128)(2,1)S(1)}, bf16[1280,128]{1,0:T(8,128)(2,1)S(1)}, u32[]{:S(2)}, u32[]{:S(2)}) collective-permute-start(bf16[1280,128]{1,0:T(8,128)(2,1)S(1)} %collective-permute-done.19.refs_26_), channel_id=1, source_target_pairs={{0,1},{1,0},{2,3},{3,2},{4,5},{5,4},{6,7},{7,6},{8,9},{9,8},{10,11... | collective-permute-start | bytes 983048 | tf_op jit(solution)/shard_map/ppermute | solution.py:181
  50.5 7.4 %collective-permute-start.14 = (bf16[1280,128]{1,0:T(8,128)(2,1)S(1)}, bf16[1280,128]{1,0:T(8,128)(2,1)S(1)}, u32[]{:S(2)}, u32[]{:S(2)}) collective-permute-start(bf16[1280,128]{1,0:T(8,128)(2,1)S(1)} %collective-permute-done.13.refs_20_), channel_id=1, source_target_pairs={{0,1},{1,0},{2,3},{3,2},{4,5},{5,4},{6,7},{7,6},{8,9},{9,8},{10,11... | collective-permute-start | bytes 983048 | tf_op jit(solution)/shard_map/ppermute | solution.py:181
  52.2 6.0 %collective-permute-start.12 = (bf16[1280,128]{1,0:T(8,128)(2,1)S(1)}, bf16[1280,128]{1,0:T(8,128)(2,1)S(1)}, u32[]{:S(2)}, u32[]{:S(2)}) collective-permute-start(bf16[1280,128]{1,0:T(8,128)(2,1)S(1)} %collective-permute-done.11.refs_18_), channel_id=1, source_target_pairs={{0,1},{1,0},{2,3},{3,2},{4,5},{5,4},{6,7},{7,6},{8,9},{9,8},{10,11... | collective-permute-start | bytes 983048 | tf_op jit(solution)/shard_map/ppermute | solution.py:181
  56.7 13.6 %collective-permute-start.33 = (bf16[1280,128]{1,0:T(8,128)(2,1)S(1)}, bf16[1280,128]{1,0:T(8,128)(2,1)}, u32[]{:S(2)}, u32[]{:S(2)}) collective-permute-start(bf16[1280,128]{1,0:T(8,128)(2,1)S(1)} %collective-permute-done.29.refs_36_), channel_id=1, source_target_pairs={{0,16},{16,0},{1,17},{17,1},{2,18},{18,2},{3,19},{19,3},{4,20},{20... | collective-permute-start | bytes 983048 | tf_op jit(solution)/shard_map/ppermute | solution.py:201
  57.9 12.5 %collective-permute-start.31 = (bf16[1280,128]{1,0:T(8,128)(2,1)S(1)}, bf16[1280,128]{1,0:T(8,128)(2,1)}, u32[]{:S(2)}, u32[]{:S(2)}) collective-permute-start(bf16[1280,128]{1,0:T(8,128)(2,1)S(1)} %collective-permute-done.29.refs_36_), channel_id=1, source_target_pairs={{0,2},{2,0},{1,3},{3,1},{4,6},{6,4},{5,7},{7,5},{8,10},{10,8},{9,1... | collective-permute-start | bytes 983048 | tf_op jit(solution)/shard_map/ppermute | solution.py:200
  58.3 9.6 %collective-permute-start.27 = (bf16[640,128]{1,0:T(8,128)(2,1)S(1)}, bf16[640,128]{1,0:T(8,128)(2,1)S(1)}, u32[]{:S(2)}, u32[]{:S(2)}) collective-permute-start(bf16[640,128]{1,0:T(8,128)(2,1)S(1)} %slice.27), channel_id=1, source_target_pairs={{0,16},{16,0},{1,17},{17,1},{2,18},{18,2},{3,19},{19,3},{4,20},{20... | collective-permute-start | bytes 491528 | tf_op jit(solution)/shard_map/ppermute | solution.py:203
  59.6 11.2 %collective-permute-start.30 = (bf16[1280,128]{1,0:T(8,128)(2,1)S(1)}, bf16[1280,128]{1,0:T(8,128)(2,1)S(1)}, u32[]{:S(2)}, u32[]{:S(2)}) collective-permute-start(bf16[1280,128]{1,0:T(8,128)(2,1)S(1)} %collective-permute-done.29.refs_36_), channel_id=1, source_target_pairs={{0,1},{1,0},{2,3},{3,2},{4,5},{5,4},{6,7},{7,6},{8,9},{9,8},{10,11... | collective-permute-start | bytes 983048 | tf_op jit(solution)/shard_map/ppermute | solution.py:181
  67.9 6.6 %collective-permute-start.24 = (bf16[1280,128]{1,0:T(8,128)(2,1)S(1)}, bf16[1280,128]{1,0:T(8,128)(2,1)S(1)}, u32[]{:S(2)}, u32[]{:S(2)}) collective-permute-start(bf16[1280,128]{1,0:T(8,128)(2,1)S(1)} %collective-permute-done.23.refs_30_), channel_id=1, source_target_pairs={{0,1},{1,0},{2,3},{3,2},{4,5},{5,4},{6,7},{7,6},{8,9},{9,8},{10,11... | collective-permute-start | bytes 983048 | tf_op jit(solution)/shard_map/ppermute | solution.py:181
  70.3 7.8 %collective-permute-start.22 = (bf16[1280,128]{1,0:T(8,128)(2,1)S(1)}, bf16[1280,128]{1,0:T(8,128)(2,1)S(1)}, u32[]{:S(2)}, u32[]{:S(2)}) collective-permute-start(bf16[1280,128]{1,0:T(8,128)(2,1)S(1)} %collective-permute-done.21.refs_28_), channel_id=1, source_target_pairs={{0,1},{1,0},{2,3},{3,2},{4,5},{5,4},{6,7},{7,6},{8,9},{9,8},{10,11... | collective-permute-start | bytes 983048 | tf_op jit(solution)/shard_map/ppermute | solution.py:181
  74.2 5.4 %collective-permute-start.35 = (bf16[640,128]{1,0:T(8,128)(2,1)S(1)}, bf16[640,128]{1,0:T(8,128)(2,1)}, u32[]{:S(2)}, u32[]{:S(2)}) collective-permute-start(bf16[640,128]{1,0:T(8,128)(2,1)S(1)} %slice.28), channel_id=1, source_target_pairs={{0,2},{2,0},{1,3},{3,1},{4,6},{6,4},{5,7},{7,5},{8,10},{10,8},{9,1... | collective-permute-start | bytes 491528 | tf_op jit(solution)/shard_map/ppermute | solution.py:202
  75.2 5.7 %collective-permute-start.37 = (bf16[640,128]{1,0:T(8,128)(2,1)S(1)}, bf16[640,128]{1,0:T(8,128)(2,1)}, u32[]{:S(2)}, u32[]{:S(2)}) collective-permute-start(bf16[640,128]{1,0:T(8,128)(2,1)S(1)} %slice.29), channel_id=1, source_target_pairs={{0,16},{16,0},{1,17},{17,1},{2,18},{18,2},{3,19},{19,3},{4,20},{20... | collective-permute-start | bytes 491528 | tf_op jit(solution)/shard_map/ppermute | solution.py:203
  77.1 28.6 %collective-permute-start.34 = (bf16[1280,128]{1,0:T(8,128)(2,1)}, bf16[1280,128]{1,0:T(8,128)(2,1)}, u32[]{:S(2)}, u32[]{:S(2)}) collective-permute-start(bf16[1280,128]{1,0:T(8,128)(2,1)} %collective-permute-done.33.refs_40_), channel_id=1, source_target_pairs={{0,1},{1,0},{2,3},{3,2},{4,5},{5,4},{6,7},{7,6},{8,9},{9,8},{10,11... | collective-permute-start | bytes 983048 | tf_op jit(solution)/shard_map/ppermute | solution.py:181
  78.9 26.9 %collective-permute-start.32 = (bf16[1280,128]{1,0:T(8,128)(2,1)}, bf16[1280,128]{1,0:T(8,128)(2,1)}, u32[]{:S(2)}, u32[]{:S(2)}) collective-permute-start(bf16[1280,128]{1,0:T(8,128)(2,1)} %collective-permute-done.31.refs_38_), channel_id=1, source_target_pairs={{0,1},{1,0},{2,3},{3,2},{4,5},{5,4},{6,7},{7,6},{8,9},{9,8},{10,11... | collective-permute-start | bytes 983048 | tf_op jit(solution)/shard_map/ppermute | solution.py:181
  79.7 26.1 %collective-permute-start.36 = (bf16[640,128]{1,0:T(8,128)(2,1)}, bf16[640,128]{1,0:T(8,128)(2,1)}, u32[]{:S(2)}, u32[]{:S(2)}) collective-permute-start(bf16[640,128]{1,0:T(8,128)(2,1)} %collective-permute-done.35.refs_42_), channel_id=1, source_target_pairs={{0,1},{1,0},{2,3},{3,2},{4,5},{5,4},{6,7},{7,6},{8,9},{9,8},{10,11... | collective-permute-start | bytes 491528 | tf_op jit(solution)/shard_map/ppermute | solution.py:181
  80.9 24.8 %collective-permute-start.38 = (bf16[640,128]{1,0:T(8,128)(2,1)}, bf16[640,128]{1,0:T(8,128)(2,1)}, u32[]{:S(2)}, u32[]{:S(2)}) collective-permute-start(bf16[640,128]{1,0:T(8,128)(2,1)} %collective-permute-done.37.refs_44_), channel_id=1, source_target_pairs={{0,1},{1,0},{2,3},{3,2},{4,5},{5,4},{6,7},{7,6},{8,9},{9,8},{10,11... | collective-permute-start | bytes 491528 | tf_op jit(solution)/shard_map/ppermute | solution.py:181
  (50 other events, 571.1 us)

commit v2 on v0

v2 whole, which is shorter than its diff:
```python
import functools

import jax
import jax.numpy as jnp
from jax import lax
from jax.experimental import pallas as pl
from jax.experimental.pallas import tpu as pltpu
from jax.sharding import PartitionSpec as P

TILE = 128
HALF_BLK = 12
LANES = 128
ROWS_WIN = 144
COLS_WIN = 256
GROUPS = 4
RING = (0, 1, 3, 2)
SWAP = ((0, 1), (1, 0))
F32 = jnp.float32
BF16 = jnp.bfloat16
SMEM = pl.BlockSpec(memory_space=pltpu.SMEM)
VMEM = pl.BlockSpec(memory_space=pltpu.VMEM)
MIB = 1 << 20


def shift_kernel(rows_half, n_refs, *refs):
    place, listed, extra = refs[:3]
    tiles = refs[3 : 3 + n_refs]
    shifted, where, offsets = refs[3 + n_refs :]

    def lay(k, start):
        start = jnp.where(k == HALF_BLK, 0, start)
        offsets[k] = start
        return start + TILE // 2 + extra[k // HALF_BLK, lax.rem(k, HALF_BLK)]

    lax.fori_loop(0, 2 * HALF_BLK, lay, jnp.int32(0))
    rows = lax.broadcasted_iota(jnp.int32, (TILE, TILE), 0)
    cols = lax.broadcasted_iota(jnp.int32, (TILE, TILE), 1)
    for r in range(n_refs):
        ref = tiles[r]
        count = ref.shape[0]

        def one(i, carry, ref=ref, r=r, count=count):
            n = place[1 + r] * count + i
            m = listed[0, n, 0]
            k = listed[0, n, 1]
            half_k = k // HALF_BLK
            size_m = TILE // 2 + extra[place[0], m]
            size_k = TILE // 2 + extra[half_k, lax.rem(k, HALF_BLK)]
            off_m = offsets[place[0] * HALF_BLK + m]
            off_k = offsets[k]
            base_m = (off_m // 16) * 16
            base_k = jnp.minimum((off_k // LANES) * LANES, rows_half - COLS_WIN)
            value = jnp.where((rows < size_m) & (cols < size_k), ref[i].astype(F32), 0.0)
            value = jnp.concatenate([value, jnp.zeros((TILE, COLS_WIN - TILE), F32)], axis=1)
            value = jnp.concatenate(
                [value, jnp.zeros((ROWS_WIN - TILE, COLS_WIN), F32)], axis=0
            )
            value = pltpu.roll(value, off_k - base_k, 1)
            value = pltpu.roll(value, off_m - base_m, 0)
            at = r * count + i
            shifted[at] = value.astype(BF16)
            where[0, at] = base_m
            where[1, at] = base_k
            where[2, at] = jnp.where(half_k == place[0], 0, 1)
            return carry

        lax.fori_loop(0, count, one, 0)


def shift_tiles(place, listed, shell_extra, tiles, rows_half):
    total = sum(t.shape[0] for t in tiles)
    return pl.pallas_call(
        functools.partial(shift_kernel, rows_half, len(tiles)),
        out_shape=(
            jax.ShapeDtypeStruct((total, ROWS_WIN, COLS_WIN), BF16),
            jax.ShapeDtypeStruct((3, total), jnp.int32),
        ),
        in_specs=[SMEM] * 3 + [VMEM] * len(tiles),
        out_specs=(VMEM, SMEM),
        scratch_shapes=[pltpu.SMEM((2 * HALF_BLK,), jnp.int32)],
        compiler_params=pltpu.CompilerParams(vmem_limit_bytes=12 * MIB),
        cost_estimate=pl.CostEstimate(flops=0, bytes_accessed=8 * MIB, transcendentals=0),
        name="shift_tiles",
    )(place, listed, shell_extra, *tiles)


def assemble_kernel(quarter, own, by_x, by_y, far_x, far_y, out):
    rows = own.shape[0]

    def put(at, value, first):
        start = pl.multiple_of(at * LANES, LANES)
        out[first : first + value.shape[0], pl.ds(start, LANES)] = value

    q = quarter[0]
    put(q, own[...], 0)
    put(q ^ 1, by_x[:rows], 0)
    put(q ^ 2, by_y[:rows], 0)
    half = rows // 2
    put(q ^ 3, far_x[far_x.shape[0] - half :], 0)
    put(q ^ 3, far_y[far_y.shape[0] - half :], half)


def assemble(quarter, *pieces):
    rows = pieces[0].shape[0]
    return pl.pallas_call(
        assemble_kernel,
        out_shape=jax.ShapeDtypeStruct((rows, 4 * LANES), BF16),
        in_specs=[SMEM] + [VMEM] * 5,
        out_specs=VMEM,
        compiler_params=pltpu.CompilerParams(vmem_limit_bytes=8 * MIB),
        cost_estimate=pl.CostEstimate(flops=0, bytes_accessed=3 * MIB, transcendentals=0),
        name="assemble",
    )(quarter, *pieces)


def first_kernel(n_refs, n_tiles, ids, where, shifted, *refs):
    own = refs[:n_refs]
    other = refs[n_refs : 2 * n_refs]
    out, held, total = refs[2 * n_refs :]
    blocks = held.shape[1]
    for s in range(n_refs):
        at = ids[s]

        @pl.when((at >= 0) & (at < blocks))
        def _(s=s, at=at):
            held[0, at] = own[s][...]
            held[1, at] = other[s][...]

    total[...] = jnp.zeros_like(total)

    def add(n, carry):
        base_m = pl.multiple_of(where[0, n], 16)
        base_k = pl.multiple_of(where[1, n], LANES)
        half = where[2, n]
        for j in range(blocks):
            total[j, pl.ds(base_m, ROWS_WIN), :] += jnp.dot(
                shifted[n], held[half, j, pl.ds(base_k, COLS_WIN), :],
                preferred_element_type=F32,
            )
        return carry

    lax.fori_loop(0, n_tiles, add, 0)
    out[...] = total[:, : out.shape[1], :].astype(BF16)


def first_product(ids, where, shifted, own, other, blocks):
    rows, width = own[0].shape
    n_tiles = shifted.shape[0]
    return pl.pallas_call(
        functools.partial(first_kernel, len(own), n_tiles),
        out_shape=jax.ShapeDtypeStruct((blocks, rows, width), BF16),
        in_specs=[SMEM] * 2 + [VMEM] * (1 + 2 * len(own)),
        out_specs=VMEM,
        scratch_shapes=[
            pltpu.VMEM((2, blocks, rows, width), BF16),
            pltpu.VMEM((blocks, rows + TILE, width), F32),
        ],
        compiler_params=pltpu.CompilerParams(vmem_limit_bytes=20 * MIB),
        cost_estimate=pl.CostEstimate(
            flops=n_tiles * 2 * ROWS_WIN * COLS_WIN * width * blocks, bytes_accessed=20 * MIB,
            transcendentals=0,
        ),
        name="first_product",
    )(ids, where, shifted, *own, *other)


def pick(ids, wanted, refs, held):
    for s, ref in enumerate(refs):

        @pl.when(ids[s] == wanted)
        def _(ref=ref):
            held[...] = ref[...]


def second(held, middle):
    dims = (((0,), (0,)), ((), ()))
    return jnp.concatenate(
        [
            lax.dot_general(held[...], middle[j], dims, preferred_element_type=F32)
            for j in range(middle.shape[0])
        ],
        axis=1,
    )


def send_kernel(chunk, ids, place, middle, *refs):
    groups = refs[:GROUPS]
    out, held = refs[GROUPS:]
    pick(ids, (1 - place[0]) * (GROUPS // 2) + chunk, groups, held)
    out[...] = second(held, middle).astype(BF16)


def keep_kernel(chunk, ids, place, pair_occ, eps_occ, middle, eps_rows, eps_cols, got, *refs):
    groups = refs[:GROUPS]
    out, held = refs[-2:]
    pick(ids, place[0] * (GROUPS // 2) + chunk, groups, held)
    total = second(held, middle) + got[...].astype(F32)
    energy = eps_occ[pair_occ[0, 0]] + eps_occ[pair_occ[0, 1]]
    out[0] = (total / (energy - eps_rows[...] - eps_cols[...])).astype(BF16)


def second_cost(rows, width, columns):
    return pl.CostEstimate(
        flops=2 * rows * width * columns, bytes_accessed=8 * MIB, transcendentals=0
    )


def send_product(chunk, ids, place, middle, groups):
    rows, width = groups[0].shape
    columns = middle.shape[0] * middle.shape[2]
    return pl.pallas_call(
        functools.partial(send_kernel, chunk),
        out_shape=jax.ShapeDtypeStruct((width, columns), BF16),
        in_specs=[SMEM] * 2 + [VMEM] * (1 + GROUPS),
        out_specs=VMEM,
        scratch_shapes=[pltpu.VMEM((rows, width), BF16)],
        compiler_params=pltpu.CompilerParams(vmem_limit_bytes=16 * MIB),
        cost_estimate=second_cost(rows, width, columns),
        name="send_product",
    )(ids, place, middle, *groups)


def keep_product(chunk, ids, place, pair_occ, eps_occ, middle, eps_rows, eps_cols, got, groups, before):
    rows, width = groups[0].shape
    columns = middle.shape[0] * middle.shape[2]
    extra = [] if before is None else [before]
    fixed = [ids, place, pair_occ, eps_occ, middle, eps_rows, eps_cols, got, *groups]
    whole = lambda a: pl.BlockSpec(a.shape, lambda i, n=a.ndim: (0,) * n)
    return pl.pallas_call(
        functools.partial(keep_kernel, chunk),
        grid=(1,),
        out_shape=jax.ShapeDtypeStruct((1, GROUPS // 2 * width, columns), BF16),
        in_specs=[SMEM] * 4
        + [VMEM, pl.BlockSpec((width, 1), lambda i: (chunk, 0)), VMEM, VMEM]
        + [VMEM] * GROUPS
        + [pl.BlockSpec(memory_space=pl.ANY)] * len(extra),
        out_specs=pl.BlockSpec((1, width, columns), lambda i: (0, chunk, 0)),
        scratch_shapes=[pltpu.VMEM((rows, width), BF16)],
        input_output_aliases={len(fixed): 0} if extra else {},
        compiler_params=pltpu.CompilerParams(vmem_limit_bytes=20 * MIB),
        cost_estimate=second_cost(rows, width, columns),
        name="keep_product",
    )(*fixed, *extra)


def ring_pairs(distance):
    return [(RING[i], RING[(i + distance) % 4]) for i in range(4)]


def other_core(value):
    return lax.ppermute(value, "rep", SWAP)


def to_x(value):
    return lax.ppermute(value, "vir", SWAP)


def to_y(value):
    return lax.ppermute(value, "grp", SWAP)


def to_z(value, distance=1):
    return lax.ppermute(value, "ao", ring_pairs(distance))


def exchange_small(half_ints, coeff):
    z, x, y = lax.axis_index("ao"), lax.axis_index("vir"), lax.axis_index("grp")
    ring = jnp.asarray(RING, jnp.int32)
    spot = jnp.where(z == 3, 2, jnp.where(z == 2, 3, z))
    quarter = y * 2 + x
    order = [ring[(spot - k) % 4] for k in range(4)]
    rows = coeff.shape[0]
    half = rows // 2
    together = lax.optimization_barrier
    join = lambda a, b: jnp.concatenate([a, b], axis=0)

    own = lax.dynamic_slice_in_dim(coeff, quarter * LANES, LANES, 1)
    t = [
        lax.dynamic_index_in_dim(half_ints[:, 0], ring[(spot + k) % 4], 0, False)
        for k in range(4)
    ]
    z1, t = together((to_z(own), t))
    x1, y1, z2, t = together((to_x(z1), to_y(z1), to_z(z1), t))
    x2, y2, z3, t1, t = together(
        (to_x(join(z2, y1[:half])), to_y(join(z2, x1[half:])), to_z(z2), to_z(t[1], 1), t)
    )
    x3, y3, t2, t3 = together(
        (
            to_x(join(z3, y2[:half])), to_y(join(z3, x2[half:rows])),
            to_z(t[2], 2), to_z(t[3], 3),
        )
    )
    x4, y4 = to_x(y3[:half]), to_y(x3[half:rows])
    q = quarter.astype(jnp.int32).reshape(1)
    groups = [
        coeff,
        assemble(q, z1, x1, y1, x2, y2),
        assemble(q, z2, x2, y2, x3, y3),
        assemble(q, z3, x3, y3, x4, y4),
    ]
    return groups, [t[0], t1, t2, t3], order


def exchange_any(half_ints, coeff):
    count = lax.axis_size("ao")
    gathered = lax.all_gather(coeff, "ao", axis=1, tiled=True)
    width = gathered.shape[1] // GROUPS
    tiles = lax.all_to_all(half_ints, "ao", split_axis=0, concat_axis=2, tiled=True)[0, 0]
    groups = [gathered[:, g * width : (g + 1) * width] for g in range(GROUPS)]
    return gathered, groups, [tiles], count


def local(half_ints, coeff, eps_occ, eps_vir, pair_occ, tile_list, shell_extra):
    sizes = tuple(lax.axis_size(name) for name in ("grp", "ao", "vir"))
    rows, width = coeff.shape
    full_width = width * sizes[1]
    a_width, b_width = full_width // lax.axis_size("rep"), full_width // sizes[2]
    core = lax.axis_index("rep").astype(jnp.int32)
    vir = lax.axis_index("vir").astype(jnp.int32)
    ints = lambda values: jnp.stack([jnp.asarray(v, jnp.int32) for v in values])
    if sizes == (2, 4, 2) and width == 4 * LANES:
        groups, tiles, order = exchange_small(half_ints, coeff)
        ids = ints(order)
        blocks = b_width // width
        b_ids = ids - vir * blocks
        own, tile_order = groups, order
    else:
        gathered, groups, tiles, _ = exchange_any(half_ints, coeff)
        ids = ints(range(GROUPS))
        blocks, b_ids = 1, ints([0])
        own = [lax.dynamic_slice_in_dim(gathered, vir * b_width, b_width, 1)]
        tile_order = [0]
    other = [other_core(g) for g in own]
    place = ints([core])
    shifted, where = shift_tiles(ints([core] + tile_order), tile_list, shell_extra, tiles, rows)
    middle = first_product(b_ids, where, shifted, own, other, blocks)
    rows_energy = lax.dynamic_slice_in_dim(eps_vir, core * a_width, a_width, 0).reshape(-1, 1)
    cols_energy = lax.dynamic_slice_in_dim(eps_vir, vir * b_width, b_width, 0).reshape(1, -1)
    got = [
        other_core(send_product(chunk, ids, place, middle, groups)) for chunk in range(GROUPS // 2)
    ]
    out = None
    for chunk in range(GROUPS // 2):
        out = keep_product(
            chunk, ids, place, pair_occ, eps_occ, middle, rows_energy, cols_energy, got[chunk],
            groups, out,
        )
    return out


def solution(mesh):
    in_specs = (
        P("grp", "rep", "ao", None, None),
        P("rep", "ao"),
        P(),
        P(),
        P(("grp", "ao"), None),
        P("rep", None, None),
        P(),
    )
    out_specs = P(("grp", "ao"), "rep", "vir")
    return jax.shard_map(local, mesh=mesh, in_specs=in_specs, out_specs=out_specs, check_vma=False)
```

time: 241 us -> 105 us (0.44)
  waiting for transfers between devices: 107 us -> 28.7 us
  local copies, waits for them, and re-layouts: 62.6 us -> 12 us
  Pallas kernels: 0 us -> 35.6 us
  matrix products: 27.8 us -> 0 us
  other arithmetic: 17 us -> 2.7 us
  starting transfers between devices: 6.61 us -> 18 us
  between operations: 18.4 us -> 7.62 us
    all_gather x2 -> x0, waiting for transfers between devices: 99.3 us -> none  [the longest x1 98.2 us: local(): gathered = lax.all_gather(coeff, 'ao', axis=1, tiled=True)]
    gather x6 -> x0, local copies, waits for them, and re-layouts: 41.4 us -> none  [the longest x2 27.7 us: padded_rows(): jnp.take(matrix, jnp.minimum(real_rows, NAO - 1).reshape(-1), axis=0)]
    pallas_call x0 -> x9, Pallas kernels: none -> 35.6 us  [the longest x1 10.3 us: first_product(): pl.pallas_call(functools.partial(first_kernel, len(own), n_tiles), out_sh...]
    ppermute x0 -> x20, waiting for transfers between devices: none -> 28.7 us  [the longest x6 22.3 us: to_z(): return lax.ppermute(value, 'ao', ring_pairs(distance))]
    dot_general x3 -> x0, matrix products: 27.8 us -> none  [the longest x1 10.4 us: local(): jnp.einsum('ka,pkb->apb', gathered, packed_tile, preferred_element_type=j...]
    ppermute x0 -> x20, starting transfers between devices: none -> 18 us  [the longest x6 6.04 us: other_core(): return lax.ppermute(value, 'rep', SWAP)]
    another operation x2 -> x1, local copies, waits for them, and re-layouts: 12.8 us -> 2.58 us  [local(): ints = lambda values: jnp.stack([jnp.asarray(v, jnp.int32) for v in values])]
    reduce_scatter x1 -> x0, waiting for transfers between devices: 6.95 us -> none  [local(): lax.psum_scatter(jnp.einsum('ka,pkb->apb', gathered, packed_tile, preferr...]
  transfers between devices with their start and end apart: 4 -> 20, of which waited for: 3 -> 5; matrix products, arithmetic and copies ran while one was open for 22% -> 7% of each run, Pallas kernels for 0% -> 16%
where the time goes in v2:
time: 105 us
  Pallas kernels  35.6 us (34%)
  waiting for transfers between devices  28.7 us (27%)
  starting transfers between devices  18 us (17%)
  local copies, waits for them, and re-layouts  12 us (11%)
  between operations  7.62 us (7%)
  other arithmetic  2.7 us (3%)
    ppermute x6, waiting for transfers between devices, to_z(): return lax.ppermute(value, 'ao', ring_pairs(distance))  22.3 us
    pallas_call x1, Pallas kernels, first_product(): pl.pallas_call(functools.partial(first_kernel, len(own), n_tiles), out_sh...  10.3 us
    pallas_call x2, Pallas kernels, keep_product(): pl.pallas_call(functools.partial(keep_kernel, chunk), grid=(1,), out_shap...  9.43 us
    pallas_call x2, Pallas kernels, send_product(): pl.pallas_call(functools.partial(send_kernel, chunk), out_shape=jax.Shape...  8.73 us
    unnamed x27, local copies, waits for them, and re-layouts  6.45 us
    ppermute x6, starting transfers between devices, other_core(): return lax.ppermute(value, 'rep', SWAP)  6.04 us
    ppermute x6, starting transfers between devices, to_z(): return lax.ppermute(value, 'ao', ring_pairs(distance))  5.49 us
    ppermute x4, waiting for transfers between devices, to_x(): return lax.ppermute(value, 'vir', SWAP)  5.46 us
  transfers between devices with their start and end apart: 20, of which 5 were waited for; matrix products, arithmetic and copies ran while one was open for 7% of the time, Pallas kernels for 16%

profile of v2, /device:TPU:9, one launch (start us, length us, event | category | flops | bytes accessed | tf_op | source)
XLA Modules:
  0.0 104.7 jit_solution(17094939385554693528)
XLA Ops:
  0.0 1.1 %constant_dynamic-slice_fusion = bf16[1280,128]{1,0:T(8,128)(2,1)S(1)} fusion(bf16[1280,512]{1,0:T(8,128)(2,1)} %refs_0_.9, s32[]{:T(128)S(6)} %select_n.94), kind=kLoop, calls=%fused_computation.8 | loop fusion | bytes 655364 | tf_op jit(solution)/shard_map/dynamic_slice | solution.py:277
  1.1 2.4 %collective-permute-start = (bf16[1280,128]{1,0:T(8,128)(2,1)S(1)}, bf16[1280,128]{1,0:T(8,128)(2,1)S(1)}, u32[]{:S(2)}, u32[]{:S(2)}) collective-permute-start(bf16[1280,128]{1,0:T(8,128)(2,1)S(1)} %constant_dynamic-slice_fusion), channel_id=1, source_target_pairs={{0,4},{4,12},{12,8},{8,0},{1,5},{5,13},{13,9},{9,1},{2,6},{6,14},{... | collective-permute-start | bytes 983048 | tf_op jit(solution)/shard_map/ppermute | solution.py:263
  3.4 1.6 %fusion.1 = (s32[1]{0:T(128)}, s32[1]{0:T(128)}, s32[1]{0:T(128)}, s32[1]{0:T(128)}, s32[1]{0:T(128)}, /*index=5*/s32[1]{0:T(128)}, s32[1]{0:T(128)}) fusion(s32[4]{0:T(128)} %constant.90.clone, s32[]{:T(128)S(6)} %select_n.103, s32[]{:T(128)S(6)} %select_n.97, s32[]{:T(128)S(6)} %select_n.93, s32[]{:T(128)S(6)} %select_n.91, s32[]{:T(128)S(6)} %select_n.89, ...), kind=kLoop, calls=%fused_computation.12 | loop fusion | bytes 84 | tf_op jit(solution)/shard_map/dynamic_slice | solution.py:279
  12.5 1.3 %collective-permute-start.1 = (bf16[1280,128]{1,0:T(8,128)(2,1)S(1)}, bf16[1280,128]{1,0:T(8,128)(2,1)S(1)}, u32[]{:S(2)}, u32[]{:S(2)}) collective-permute-start(bf16[1280,128]{1,0:T(8,128)(2,1)S(1)} %collective-permute-done.own), channel_id=1, source_target_pairs={{0,2},{2,0},{1,3},{3,1},{4,6},{6,4},{5,7},{7,5},{8,10},{10,8},{9,1... | collective-permute-start | bytes 983048 | tf_op jit(solution)/shard_map/ppermute | solution.py:255
  13.8 1.2 %collective-permute-start.2 = (bf16[1280,128]{1,0:T(8,128)(2,1)S(1)}, bf16[1280,128]{1,0:T(8,128)(2,1)S(1)}, u32[]{:S(2)}, u32[]{:S(2)}) collective-permute-start(bf16[1280,128]{1,0:T(8,128)(2,1)S(1)} %collective-permute-done.own), channel_id=1, source_target_pairs={{0,16},{16,0},{1,17},{17,1},{2,18},{18,2},{3,19},{19,3},{4,20},{20... | collective-permute-start | bytes 983048 | tf_op jit(solution)/shard_map/ppermute | solution.py:259
  15.4 5.4 %collective-permute-done.1.by_x = bf16[1280,128]{1,0:T(8,128)(2,1)S(1)} collective-permute-done((bf16[1280,128]{1,0:T(8,128)(2,1)S(1)}, bf16[1280,128]{1,0:T(8,128)(2,1)S(1)}, u32[]{:S(2)}, u32[]{:S(2)}) %collective-permute-start.1) | collective-permute-done | bytes 327712 | tf_op jit(solution)/shard_map/ppermute | solution.py:255
  20.8 0.9 collective-permute-done.2.by_y
  21.7 1.0 collective-permute-done.3.own
  23.4 0.6 collective-permute-start.6
  24.1 9.9 %collective-permute-done.7.refs_4_ = bf16[6,128,128]{2,1,0:T(8,128)(2,1)S(1)} collective-permute-done((bf16[6,128,128]{2,1,0:T(8,128)(2,1)S(1)}, bf16[6,128,128]{2,1,0:T(8,128)(2,1)S(1)}, u32[]{:S(2)}, u32[]{:S(2)}) %collective-permute-start.7) | collective-permute-done | bytes 196640 | tf_op jit(solution)/shard_map/ppermute | solution.py:263
  34.1 1.2 %collective-permute-start.8 = (bf16[1920,128]{1,0:T(8,128)(2,1)S(1)}, bf16[1920,128]{1,0:T(8,128)(2,1)S(1)}, u32[]{:S(2)}, u32[]{:S(2)}) collective-permute-start(bf16[1920,128]{1,0:T(8,128)(2,1)S(1)} %get-tuple-element.62), channel_id=1, source_target_pairs={{0,2},{2,0},{1,3},{3,1},{4,6},{6,4},{5,7},{7,5},{8,10},{10,8},{9,1... | collective-permute-start | bytes 1474568 | tf_op jit(solution)/shard_map/ppermute | solution.py:255
  35.3 1.1 %collective-permute-start.9 = (bf16[1920,128]{1,0:T(8,128)(2,1)S(1)}, bf16[1920,128]{1,0:T(8,128)(2,1)S(1)}, u32[]{:S(2)}, u32[]{:S(2)}) collective-permute-start(bf16[1920,128]{1,0:T(8,128)(2,1)S(1)} %get-tuple-element.61), channel_id=1, source_target_pairs={{0,16},{16,0},{1,17},{17,1},{2,18},{18,2},{3,19},{19,3},{4,20},{20... | collective-permute-start | bytes 1474568 | tf_op jit(solution)/shard_map/ppermute | solution.py:259
  36.4 2.2 %collective-permute-start.11 = (bf16[6,128,128]{2,1,0:T(8,128)(2,1)S(1)}, bf16[6,128,128]{2,1,0:T(8,128)(2,1)S(1)}, u32[]{:S(2)}, u32[]{:S(2)}) collective-permute-start(bf16[6,128,128]{2,1,0:T(8,128)(2,1)S(1)} %get-tuple-element.48), channel_id=1, source_target_pairs={{0,8},{4,0},{12,4},{8,12},{1,9},{5,1},{13,5},{9,13},{2,10},{6,2},{... | collective-permute-start | bytes 589832 | tf_op jit(solution)/shard_map/ppermute | solution.py:263
  38.6 11.4 %collective-permute-done.10.refs_5_ = bf16[6,128,128]{2,1,0:T(8,128)(2,1)S(1)} collective-permute-done((bf16[6,128,128]{2,1,0:T(8,128)(2,1)S(1)}, bf16[6,128,128]{2,1,0:T(8,128)(2,1)S(1)}, u32[]{:S(2)}, u32[]{:S(2)}) %collective-permute-start.10) | collective-permute-done | bytes 196640 | tf_op jit(solution)/shard_map/ppermute | solution.py:263
  50.4 0.7 collective-permute-start.13
  51.1 2.5 %collective-permute-start.14 = (bf16[1280,512]{1,0:T(8,128)(2,1)}, bf16[1280,512]{1,0:T(8,128)(2,1)}, u32[]{:S(2)}, u32[]{:S(2)}) collective-permute-start(bf16[1280,512]{1,0:T(8,128)(2,1)} %refs_0_.9), channel_id=1, source_target_pairs={{0,1},{1,0},{2,3},{3,2},{4,5},{5,4},{6,7},{7,6},{8,9},{9,8},{10,11... | collective-permute-start | bytes 3932168 | tf_op jit(solution)/shard_map/ppermute | solution.py:251
  53.9 1.4 %assemble.4.refs_2_ = bf16[1280,512]{1,0:T(8,128)(2,1)} custom-call(s32[1]{0:T(128)} %bitcast.9.quarter, bf16[1280,128]{1,0:T(8,128)(2,1)S(1)} %collective-permute-done.3.own, bf16[1920,128]{1,0:T(8,128)(2,1)S(1)} %collective-permute-done.4.far_x.by_x, bf16[1920,128]{1,0:T(8,128)(2,1)S(1)} %collective-permute-done.5.far_y.by_y, ...), custom_call_target="tpu_custom_call" | custom-call | bytes 3145728 | tf_op jit(solution)/shard_map/assemble/pallas_call | solution.py:105
  55.9 2.5 %collective-permute-start.17 = (bf16[1280,512]{1,0:T(8,128)(2,1)S(1)}, bf16[1280,512]{1,0:T(8,128)(2,1)}, u32[]{:S(2)}, u32[]{:S(2)}) collective-permute-start(bf16[1280,512]{1,0:T(8,128)(2,1)S(1)} %assemble.5.refs_3_), channel_id=1, source_target_pairs={{0,1},{1,0},{2,3},{3,2},{4,5},{5,4},{6,7},{7,6},{8,9},{9,8},{10,11... | collective-permute-start | bytes 3932168 | tf_op jit(solution)/shard_map/ppermute | solution.py:251
  58.5 1.1 %copy-done.3 = bf16[1280,512]{1,0:T(8,128)(2,1)} copy-done((bf16[1280,512]{1,0:T(8,128)(2,1)}, bf16[1280,512]{1,0:T(8,128)(2,1)S(1)}, u32[]{:S(2)}) %copy-start.3) | copy-done | bytes 1310744
  59.6 2.6 %stack.12.refs_0_ = s32[5]{0:T(128)S(1)} concatenate(s32[1]{0:T(128)} %bitcast.place, s32[1]{0:T(128)} %get-tuple-element.72, s32[1]{0:T(128)} %get-tuple-element.71, s32[1]{0:T(128)} %get-tuple-element.70, s32[1]{0:T(128)} %get-tuple-element.69), dimensions={0} | concatenate | bytes 40 | tf_op jit(solution)/shard_map/stack | solution.py:320
  62.2 2.6 %broadcast_subtract_fusion = (s32[4]{0:T(128)S(1)}, s32[4]{0:T(128)S(1)}) fusion(s32[]{:T(128)S(6)} %mul.15, s32[1]{0:T(128)} %get-tuple-element.69, s32[1]{0:T(128)} %get-tuple-element.70, s32[1]{0:T(128)} %get-tuple-element.71, s32[1]{0:T(128)} %get-tuple-element.72), kind=kLoop, calls=%fused_computation.10 | loop fusion | flops 16 | bytes 52 | tf_op jit(solution)/shard_map/sub | solution.py:325
  64.8 5.3 %shift_tiles.1 = (bf16[24,144,256]{2,1,0:T(8,128)(2,1)S(1)}, s32[3,24]{1,0:T(4,128)S(1)}) custom-call(s32[5]{0:T(128)S(1)} %stack.12.refs_0_, s32[1,24,2]{2,1,0:T(8,128)S(1)} %copy.11.refs_1_, s32[2,12]{1,0:T(2,128)S(1)} %copy-done.9, bf16[6,128,128]{2,1,0:T(8,128)(2,1)S(1)} %get-tuple-element.42.refs_3_, ...), custom_call_target="tpu_custom_call" | custom-call | bytes 8388608 | tf_op jit(solution)/shard_map/shift_tiles/pallas_call | solution.py:72
  70.2 1.3 %copy-done.1 = bf16[1280,512]{1,0:T(8,128)(2,1)S(1)} copy-done((bf16[1280,512]{1,0:T(8,128)(2,1)S(1)}, bf16[1280,512]{1,0:T(8,128)(2,1)}, u32[]{:S(2)}) %copy-start.1) | copy-done | bytes 1310744
  71.5 1.3 %copy-done.4 = bf16[1280,512]{1,0:T(8,128)(2,1)S(1)} copy-done((bf16[1280,512]{1,0:T(8,128)(2,1)S(1)}, bf16[1280,512]{1,0:T(8,128)(2,1)}, u32[]{:S(2)}) %copy-start.4) | copy-done | bytes 1310744
  72.8 10.3 %first_product.1.middle = bf16[2,1280,512]{2,1,0:T(8,128)(2,1)S(1)} custom-call(s32[4]{0:T(128)S(1)} %get-tuple-element.55.ids, s32[3,24]{1,0:T(4,128)S(1)} %get-tuple-element.51.where, bf16[24,144,256]{2,1,0:T(8,128)(2,1)S(1)} %get-tuple-element.52.shifted, bf16[1280,512]{1,0:T(8,128)(2,1)} %refs_0_.9, bf16[1280,512]{1,0:T(8,128)(2,1)S(1)} %copy-done.1, ...), custom_call_target="tpu_custom_call" | custom-call | flops 1811939328 | bytes 20971520 | tf_op jit(solution)/shard_map/first_product/pallas_call | solution.py:149
  83.1 4.4 %send_product.3 = bf16[512,1024]{1,0:T(8,128)(2,1)} custom-call(s32[4]{0:T(128)S(1)} %get-tuple-element.56.ids, s32[1]{0:T(128)} %bitcast.place, bf16[2,1280,512]{2,1,0:T(8,128)(2,1)S(1)} %first_product.1.middle, bf16[1280,512]{1,0:T(8,128)(2,1)} %refs_0_.9, bf16[1280,512]{1,0:T(8,128)(2,1)S(1)} %copy-done.1, bf16[1280,512]{1,0:T(8,128)(2,1)} %assemble.4.refs_2_, ...), custom_call_target="tpu_custom_call" | custom-call | flops 1342177280 | bytes 8388608 | tf_op jit(solution)/shard_map/send_product/pallas_call | solution.py:211
  87.5 4.3 %send_product.2 = bf16[512,1024]{1,0:T(8,128)(2,1)} custom-call(s32[4]{0:T(128)S(1)} %get-tuple-element.56.ids, s32[1]{0:T(128)} %bitcast.place, bf16[2,1280,512]{2,1,0:T(8,128)(2,1)S(1)} %first_product.1.middle, bf16[1280,512]{1,0:T(8,128)(2,1)} %refs_0_.9, bf16[1280,512]{1,0:T(8,128)(2,1)S(1)} %copy-done.1, bf16[1280,512]{1,0:T(8,128)(2,1)} %assemble.4.refs_2_, ...), custom_call_target="tpu_custom_call" | custom-call | flops 1342177280 | bytes 8388608 | tf_op jit(solution)/shard_map/send_product/pallas_call | solution.py:211
  91.9 0.5 collective-permute-start.18
  92.7 1.3 %copy-done.2 = bf16[1280,512]{1,0:T(8,128)(2,1)S(1)} copy-done((bf16[1280,512]{1,0:T(8,128)(2,1)S(1)}, bf16[1280,512]{1,0:T(8,128)(2,1)}, u32[]{:S(2)}) %copy-start.2) | copy-done | bytes 1310744
  94.0 1.3 %copy-done.6 = bf16[1280,512]{1,0:T(8,128)(2,1)S(1)} copy-done((bf16[1280,512]{1,0:T(8,128)(2,1)S(1)}, bf16[1280,512]{1,0:T(8,128)(2,1)}, u32[]{:S(2)}) %copy-start.6) | copy-done | bytes 1310744
  95.3 4.7 %keep_product.2.refs_4_ = bf16[1,1024,1024]{2,1,0:T(8,128)(2,1)} custom-call(s32[4]{0:T(128)S(1)} %get-tuple-element.56.ids, s32[1]{0:T(128)} %bitcast.place, s32[1,2]{1,0:T(1,128)S(1)} %copy-done.8, f32[400]{0:T(512)S(1)} %copy-done.7, bf16[2,1280,512]{2,1,0:T(8,128)(2,1)S(1)} %first_product.1.middle, f32[1024,1]{1,0:T(8,128)S(1)} %copy.13.eps_rows, ...), custom_call_target="tpu_custom_call" | custom-call | flops 1342177280 | bytes 8388608 | tf_op jit(solution)/shard_map/keep_product/pallas_call | solution.py:229
  100.0 4.7 %keep_product.3 = bf16[1,1024,1024]{2,1,0:T(8,128)(2,1)} custom-call(s32[4]{0:T(128)S(1)} %get-tuple-element.56.ids, s32[1]{0:T(128)} %bitcast.place, s32[1,2]{1,0:T(1,128)S(1)} %copy-done.8, f32[400]{0:T(512)S(1)} %copy-done.7, bf16[2,1280,512]{2,1,0:T(8,128)(2,1)S(1)} %first_product.1.middle, ...), custom_call_target="tpu_custom_call", output_to_operand_aliasing={{}: (12, {})} | custom-call | flops 1342177280 | bytes 8388608 | tf_op jit(solution)/shard_map/keep_product/pallas_call | solution.py:229
  (59 shorter events, 3.0 us)
Async XLA Ops:
  0.0 12.4 %copy-start.10 = (bf16[4,1,6,128,128]{4,3,2,1,0:T(8,128)(2,1)S(1)}, bf16[4,1,6,128,128]{4,3,2,1,0:T(8,128)(2,1)}, u32[]{:S(2)}) copy-start(bf16[4,1,6,128,128]{4,3,2,1,0:T(8,128)(2,1)} %param.8) | copy-start | bytes 2359300
  1.1 11.4 %collective-permute-start = (bf16[1280,128]{1,0:T(8,128)(2,1)S(1)}, bf16[1280,128]{1,0:T(8,128)(2,1)S(1)}, u32[]{:S(2)}, u32[]{:S(2)}) collective-permute-start(bf16[1280,128]{1,0:T(8,128)(2,1)S(1)} %constant_dynamic-slice_fusion), channel_id=1, source_target_pairs={{0,4},{4,12},{12,8},{8,0},{1,5},{5,13},{13,9},{9,1},{2,6},{6,14},{... | collective-permute-start | bytes 983048 | tf_op jit(solution)/shard_map/ppermute | solution.py:263
  12.5 8.3 %collective-permute-start.1 = (bf16[1280,128]{1,0:T(8,128)(2,1)S(1)}, bf16[1280,128]{1,0:T(8,128)(2,1)S(1)}, u32[]{:S(2)}, u32[]{:S(2)}) collective-permute-start(bf16[1280,128]{1,0:T(8,128)(2,1)S(1)} %collective-permute-done.own), channel_id=1, source_target_pairs={{0,2},{2,0},{1,3},{3,1},{4,6},{6,4},{5,7},{7,5},{8,10},{10,8},{9,1... | collective-permute-start | bytes 983048 | tf_op jit(solution)/shard_map/ppermute | solution.py:255
  13.8 8.0 %collective-permute-start.2 = (bf16[1280,128]{1,0:T(8,128)(2,1)S(1)}, bf16[1280,128]{1,0:T(8,128)(2,1)S(1)}, u32[]{:S(2)}, u32[]{:S(2)}) collective-permute-start(bf16[1280,128]{1,0:T(8,128)(2,1)S(1)} %collective-permute-done.own), channel_id=1, source_target_pairs={{0,16},{16,0},{1,17},{17,1},{2,18},{18,2},{3,19},{19,3},{4,20},{20... | collective-permute-start | bytes 983048 | tf_op jit(solution)/shard_map/ppermute | solution.py:259
  15.0 7.7 %collective-permute-start.3 = (bf16[1280,128]{1,0:T(8,128)(2,1)S(1)}, bf16[1280,128]{1,0:T(8,128)(2,1)S(1)}, u32[]{:S(2)}, u32[]{:S(2)}) collective-permute-start(bf16[1280,128]{1,0:T(8,128)(2,1)S(1)} %collective-permute-done.own), channel_id=1, source_target_pairs={{0,4},{4,12},{12,8},{8,0},{1,5},{5,13},{13,9},{9,1},{2,6},{6,14},{... | collective-permute-start | bytes 983048 | tf_op jit(solution)/shard_map/ppermute | solution.py:263
  22.8 11.2 %collective-permute-start.4 = (bf16[1920,128]{1,0:T(8,128)(2,1)S(1)}, bf16[1920,128]{1,0:T(8,128)(2,1)S(1)}, u32[]{:S(2)}, u32[]{:S(2)}) collective-permute-start(bf16[1920,128]{1,0:T(8,128)(2,1)S(1)} %get-tuple-element.64), channel_id=1, source_target_pairs={{0,2},{2,0},{1,3},{3,1},{4,6},{6,4},{5,7},{7,5},{8,10},{10,8},{9,1... | collective-permute-start | bytes 1474568 | tf_op jit(solution)/shard_map/ppermute | solution.py:255
  23.1 10.9 %collective-permute-start.5 = (bf16[1920,128]{1,0:T(8,128)(2,1)S(1)}, bf16[1920,128]{1,0:T(8,128)(2,1)S(1)}, u32[]{:S(2)}, u32[]{:S(2)}) collective-permute-start(bf16[1920,128]{1,0:T(8,128)(2,1)S(1)} %get-tuple-element.63), channel_id=1, source_target_pairs={{0,16},{16,0},{1,17},{17,1},{2,18},{18,2},{3,19},{19,3},{4,20},{20... | collective-permute-start | bytes 1474568 | tf_op jit(solution)/shard_map/ppermute | solution.py:259
  23.4 10.5 %collective-permute-start.6 = (bf16[1280,128]{1,0:T(8,128)(2,1)S(1)}, bf16[1280,128]{1,0:T(8,128)(2,1)S(1)}, u32[]{:S(2)}, u32[]{:S(2)}) collective-permute-start(bf16[1280,128]{1,0:T(8,128)(2,1)S(1)} %collective-permute-done.3.own), channel_id=1, source_target_pairs={{0,4},{4,12},{12,8},{8,0},{1,5},{5,13},{13,9},{9,1},{2,6},{6,14},{... | collective-permute-start | bytes 983048 | tf_op jit(solution)/shard_map/ppermute | solution.py:263
  24.0 9.9 %collective-permute-start.7 = (bf16[6,128,128]{2,1,0:T(8,128)(2,1)S(1)}, bf16[6,128,128]{2,1,0:T(8,128)(2,1)S(1)}, u32[]{:S(2)}, u32[]{:S(2)}) collective-permute-start(bf16[6,128,128]{2,1,0:T(8,128)(2,1)S(1)} %get-tuple-element.38), channel_id=1, source_target_pairs={{0,4},{4,12},{12,8},{8,0},{1,5},{5,13},{13,9},{9,1},{2,6},{6,14},{... | collective-permute-start | bytes 589832 | tf_op jit(solution)/shard_map/ppermute | solution.py:263
  34.1 15.9 %collective-permute-start.8 = (bf16[1920,128]{1,0:T(8,128)(2,1)S(1)}, bf16[1920,128]{1,0:T(8,128)(2,1)S(1)}, u32[]{:S(2)}, u32[]{:S(2)}) collective-permute-start(bf16[1920,128]{1,0:T(8,128)(2,1)S(1)} %get-tuple-element.62), channel_id=1, source_target_pairs={{0,2},{2,0},{1,3},{3,1},{4,6},{6,4},{5,7},{7,5},{8,10},{10,8},{9,1... | collective-permute-start | bytes 1474568 | tf_op jit(solution)/shard_map/ppermute | solution.py:255
  35.3 14.7 %collective-permute-start.9 = (bf16[1920,128]{1,0:T(8,128)(2,1)S(1)}, bf16[1920,128]{1,0:T(8,128)(2,1)S(1)}, u32[]{:S(2)}, u32[]{:S(2)}) collective-permute-start(bf16[1920,128]{1,0:T(8,128)(2,1)S(1)} %get-tuple-element.61), channel_id=1, source_target_pairs={{0,16},{16,0},{1,17},{17,1},{2,18},{18,2},{3,19},{19,3},{4,20},{20... | collective-permute-start | bytes 1474568 | tf_op jit(solution)/shard_map/ppermute | solution.py:259
  36.4 13.6 %collective-permute-start.10 = (bf16[6,128,128]{2,1,0:T(8,128)(2,1)S(1)}, bf16[6,128,128]{2,1,0:T(8,128)(2,1)S(1)}, u32[]{:S(2)}, u32[]{:S(2)}) collective-permute-start(bf16[6,128,128]{2,1,0:T(8,128)(2,1)S(1)} %get-tuple-element.47), channel_id=1, source_target_pairs={{0,12},{4,8},{12,0},{8,4},{1,13},{5,9},{13,1},{9,5},{2,14},{6,10},... | collective-permute-start | bytes 589832 | tf_op jit(solution)/shard_map/ppermute | solution.py:263
  36.4 13.6 %collective-permute-start.11 = (bf16[6,128,128]{2,1,0:T(8,128)(2,1)S(1)}, bf16[6,128,128]{2,1,0:T(8,128)(2,1)S(1)}, u32[]{:S(2)}, u32[]{:S(2)}) collective-permute-start(bf16[6,128,128]{2,1,0:T(8,128)(2,1)S(1)} %get-tuple-element.48), channel_id=1, source_target_pairs={{0,8},{4,0},{12,4},{8,12},{1,9},{5,1},{13,5},{9,13},{2,10},{6,2},{... | collective-permute-start | bytes 589832 | tf_op jit(solution)/shard_map/ppermute | solution.py:263
  50.1 5.7 %collective-permute-start.12 = (bf16[640,128]{1,0:T(8,128)(2,1)S(1)}, bf16[640,128]{1,0:T(8,128)(2,1)S(1)}, u32[]{:S(2)}, u32[]{:S(2)}) collective-permute-start(bf16[640,128]{1,0:T(8,128)(2,1)S(1)} %slice.22), channel_id=1, source_target_pairs={{0,2},{2,0},{1,3},{3,1},{4,6},{6,4},{5,7},{7,5},{8,10},{10,8},{9,1... | collective-permute-start | bytes 491528 | tf_op jit(solution)/shard_map/ppermute | solution.py:255
  50.4 5.3 %collective-permute-start.13 = (bf16[640,128]{1,0:T(8,128)(2,1)S(1)}, bf16[640,128]{1,0:T(8,128)(2,1)S(1)}, u32[]{:S(2)}, u32[]{:S(2)}) collective-permute-start(bf16[640,128]{1,0:T(8,128)(2,1)S(1)} %slice.23), channel_id=1, source_target_pairs={{0,16},{16,0},{1,17},{17,1},{2,18},{18,2},{3,19},{19,3},{4,20},{20... | collective-permute-start | bytes 491528 | tf_op jit(solution)/shard_map/ppermute | solution.py:259
  51.1 19.0 %collective-permute-start.14 = (bf16[1280,512]{1,0:T(8,128)(2,1)}, bf16[1280,512]{1,0:T(8,128)(2,1)}, u32[]{:S(2)}, u32[]{:S(2)}) collective-permute-start(bf16[1280,512]{1,0:T(8,128)(2,1)} %refs_0_.9), channel_id=1, source_target_pairs={{0,1},{1,0},{2,3},{3,2},{4,5},{5,4},{6,7},{7,6},{8,9},{9,8},{10,11... | collective-permute-start | bytes 3932168 | tf_op jit(solution)/shard_map/ppermute | solution.py:251
  53.8 1.5 %copy-start = (bf16[1280,512]{1,0:T(8,128)(2,1)}, bf16[1280,512]{1,0:T(8,128)(2,1)S(1)}, u32[]{:S(2)}) copy-start(bf16[1280,512]{1,0:T(8,128)(2,1)S(1)} %assemble.3.refs_1_) | copy-start | bytes 3932164
  53.8 16.3 %collective-permute-start.15 = (bf16[1280,512]{1,0:T(8,128)(2,1)S(1)}, bf16[1280,512]{1,0:T(8,128)(2,1)}, u32[]{:S(2)}, u32[]{:S(2)}) collective-permute-start(bf16[1280,512]{1,0:T(8,128)(2,1)S(1)} %assemble.3.refs_1_), channel_id=1, source_target_pairs={{0,1},{1,0},{2,3},{3,2},{4,5},{5,4},{6,7},{7,6},{8,9},{9,8},{10,11... | collective-permute-start | bytes 3932168 | tf_op jit(solution)/shard_map/ppermute | solution.py:251
  55.3 4.2 %copy-start.12 = (s32[1,24,2]{1,2,0:T(2,128)S(1)}, s32[1,24,2]{1,2,0:T(2,128)}, u32[]{:S(2)}) copy-start(s32[1,24,2]{1,2,0:T(2,128)} %param.13) | copy-start | bytes 580
  55.3 9.5 %copy-start.9 = (s32[2,12]{1,0:T(2,128)S(1)}, s32[2,12]{1,0:T(2,128)}, u32[]{:S(2)}) copy-start(s32[2,12]{1,0:T(2,128)} %refs_2_.1) | copy-start | bytes 292
  55.3 14.8 %collective-permute-start.16 = (bf16[1280,512]{1,0:T(8,128)(2,1)}, bf16[1280,512]{1,0:T(8,128)(2,1)}, u32[]{:S(2)}, u32[]{:S(2)}) collective-permute-start(bf16[1280,512]{1,0:T(8,128)(2,1)} %assemble.4.refs_2_), channel_id=1, source_target_pairs={{0,1},{1,0},{2,3},{3,2},{4,5},{5,4},{6,7},{7,6},{8,9},{9,8},{10,11... | collective-permute-start | bytes 3932168 | tf_op jit(solution)/shard_map/ppermute | solution.py:251
  55.9 14.2 %collective-permute-start.17 = (bf16[1280,512]{1,0:T(8,128)(2,1)S(1)}, bf16[1280,512]{1,0:T(8,128)(2,1)}, u32[]{:S(2)}, u32[]{:S(2)}) collective-permute-start(bf16[1280,512]{1,0:T(8,128)(2,1)S(1)} %assemble.5.refs_3_), channel_id=1, source_target_pairs={{0,1},{1,0},{2,3},{3,2},{4,5},{5,4},{6,7},{7,6},{8,9},{9,8},{10,11... | collective-permute-start | bytes 3932168 | tf_op jit(solution)/shard_map/ppermute | solution.py:251
  70.1 1.3 %copy-start.1 = (bf16[1280,512]{1,0:T(8,128)(2,1)S(1)}, bf16[1280,512]{1,0:T(8,128)(2,1)}, u32[]{:S(2)}) copy-start(bf16[1280,512]{1,0:T(8,128)(2,1)} %copy-done) | copy-start | bytes 3932164
  71.5 1.3 %copy-start.4 = (bf16[1280,512]{1,0:T(8,128)(2,1)S(1)}, bf16[1280,512]{1,0:T(8,128)(2,1)}, u32[]{:S(2)}) copy-start(bf16[1280,512]{1,0:T(8,128)(2,1)} %copy-done.3) | copy-start | bytes 3932164
  72.8 10.3 %copy-start.5 = (bf16[1280,512]{1,0:T(8,128)(2,1)S(1)}, bf16[1280,512]{1,0:T(8,128)(2,1)}, u32[]{:S(2)}) copy-start(bf16[1280,512]{1,0:T(8,128)(2,1)} %copy-done.3) | copy-start | bytes 3932164
  87.5 4.9 %copy-start.11 = (f32[2048]{0:T(1024)S(1)}, f32[2048]{0:T(1024)}, u32[]{:S(2)}) copy-start(f32[2048]{0:T(1024)} %param.11) | copy-start | bytes 24580
  87.5 5.2 %copy-start.7 = (f32[400]{0:T(512)S(1)}, f32[400]{0:T(512)}, u32[]{:S(2)}) copy-start(f32[400]{0:T(512)} %eps_occ.3) | copy-start | bytes 4804
  87.5 5.2 %copy-start.8 = (s32[1,2]{1,0:T(1,128)S(1)}, s32[1,2]{1,0:T(1,128)}, u32[]{:S(2)}) copy-start(s32[1,2]{1,0:T(1,128)} %pair_occ.3) | copy-start | bytes 28
  87.5 5.2 %collective-permute-start.19 = (bf16[512,1024]{1,0:T(8,128)(2,1)}, bf16[512,1024]{1,0:T(8,128)(2,1)}, u32[]{:S(2)}, u32[]{:S(2)}) collective-permute-start(bf16[512,1024]{1,0:T(8,128)(2,1)} %send_product.3), channel_id=1, source_target_pairs={{0,1},{1,0},{2,3},{3,2},{4,5},{5,4},{6,7},{7,6},{8,9},{9,8},{10,11... | collective-permute-start | bytes 3145736 | tf_op jit(solution)/shard_map/ppermute | solution.py:251
  91.9 8.1 %collective-permute-start.18 = (bf16[512,1024]{1,0:T(8,128)(2,1)}, bf16[512,1024]{1,0:T(8,128)(2,1)}, u32[]{:S(2)}, u32[]{:S(2)}) collective-permute-start(bf16[512,1024]{1,0:T(8,128)(2,1)} %send_product.2), channel_id=1, source_target_pairs={{0,1},{1,0},{2,3},{3,2},{4,5},{5,4},{6,7},{7,6},{8,9},{9,8},{10,11... | collective-permute-start | bytes 3145736 | tf_op jit(solution)/shard_map/ppermute | solution.py:251
  92.6 1.3 %copy-start.2 = (bf16[1280,512]{1,0:T(8,128)(2,1)S(1)}, bf16[1280,512]{1,0:T(8,128)(2,1)}, u32[]{:S(2)}) copy-start(bf16[1280,512]{1,0:T(8,128)(2,1)} %copy-done) | copy-start | bytes 3932164
  94.0 1.3 %copy-start.6 = (bf16[1280,512]{1,0:T(8,128)(2,1)S(1)}, bf16[1280,512]{1,0:T(8,128)(2,1)}, u32[]{:S(2)}) copy-start(bf16[1280,512]{1,0:T(8,128)(2,1)} %copy-done.3) | copy-start | bytes 3932164
  (1 other events, 1.1 us)

commit v3 on v2

v3 whole, which is shorter than its diff:
```python
import functools

import jax
import jax.numpy as jnp
from jax import lax
from jax.experimental import pallas as pl
from jax.experimental.pallas import tpu as pltpu
from jax.sharding import PartitionSpec as P

TILE = 128
HALF_BLK = 12
LANES = 128
ROWS_WIN = 144
COLS_WIN = 256
GROUPS = 4
UNROLL = 4
RING = (0, 1, 3, 2)
SWAP = ((0, 1), (1, 0))
F32 = jnp.float32
BF16 = jnp.bfloat16
SMEM = pl.BlockSpec(memory_space=pltpu.SMEM)
VMEM = pl.BlockSpec(memory_space=pltpu.VMEM)
ANY = pl.BlockSpec(memory_space=pl.ANY)
MIB = 1 << 20


def ring_group(step):
    z = lax.axis_index("ao")
    spot = ((z ^ (z >> 1)) - step) & 3
    return spot ^ (spot >> 1)


def shift_kernel(rows_half, slots, *refs):
    listed, extra = refs[:2]
    tiles = refs[2 : 2 + len(slots)]
    shifted, where, offsets = refs[2 + len(slots) :]
    core = lax.axis_index("rep")

    def lay(k, start):
        start = jnp.where(k == HALF_BLK, 0, start)
        offsets[k] = start
        return start + TILE // 2 + extra[k // HALF_BLK, lax.rem(k, HALF_BLK)]

    lax.fori_loop(0, 2 * HALF_BLK, lay, jnp.int32(0))
    rows = lax.broadcasted_iota(jnp.int32, (TILE, TILE), 0)
    cols = lax.broadcasted_iota(jnp.int32, (TILE, TILE), 1)
    for r, slot in enumerate(slots):
        ref = tiles[r]
        count = ref.shape[0]
        first = 0 if slot is None else ring_group(slot) * count

        def one(i, carry, ref=ref, r=r, count=count, first=first):
            n = first + i
            m = listed[0, n, 0]
            k = listed[0, n, 1]
            half_k = k // HALF_BLK
            size_m = TILE // 2 + extra[core, m]
            size_k = TILE // 2 + extra[half_k, lax.rem(k, HALF_BLK)]
            off_m = offsets[core * HALF_BLK + m]
            off_k = offsets[k]
            base_m = (off_m // 16) * 16
            base_k = jnp.minimum((off_k // LANES) * LANES, rows_half - COLS_WIN)
            value = jnp.where((rows < size_m) & (cols < size_k), ref[i].astype(F32), 0.0)
            value = jnp.concatenate([value, jnp.zeros((TILE, COLS_WIN - TILE), F32)], axis=1)
            value = jnp.concatenate(
                [value, jnp.zeros((ROWS_WIN - TILE, COLS_WIN), F32)], axis=0
            )
            value = pltpu.roll(value, off_k - base_k, 1)
            value = pltpu.roll(value, off_m - base_m, 0)
            at = r * count + i
            shifted[at] = value.astype(BF16)
            where[0, at] = base_m
            where[1, at] = base_k
            where[2, at] = jnp.where(half_k == core, 0, 1)
            return carry

        lax.fori_loop(0, count, one, 0)


def shift_tiles(slots, listed, shell_extra, tiles, rows_half):
    total = sum(t.shape[0] for t in tiles)
    return pl.pallas_call(
        functools.partial(shift_kernel, rows_half, slots),
        out_shape=(
            jax.ShapeDtypeStruct((total, ROWS_WIN, COLS_WIN), BF16),
            jax.ShapeDtypeStruct((3, total), jnp.int32),
        ),
        in_specs=[SMEM] * 2 + [VMEM] * len(tiles),
        out_specs=(VMEM, SMEM),
        scratch_shapes=[pltpu.SMEM((2 * HALF_BLK,), jnp.int32)],
        compiler_params=pltpu.CompilerParams(vmem_limit_bytes=12 * MIB),
        cost_estimate=pl.CostEstimate(flops=0, bytes_accessed=8 * MIB, transcendentals=0),
        name="shift_tiles",
    )(listed, shell_extra, *tiles)


def assemble_kernel(own, by_x, by_y, far_x, far_y, out):
    rows = own.shape[0]

    def put(at, value, first):
        start = pl.multiple_of(at * LANES, LANES)
        out[first : first + value.shape[0], pl.ds(start, LANES)] = value

    q = lax.axis_index("grp") * 2 + lax.axis_index("vir")
    put(q, own[...], 0)
    put(q ^ 1, by_x[:rows], 0)
    put(q ^ 2, by_y[:rows], 0)
    half = rows // 2
    put(q ^ 3, far_x[far_x.shape[0] - half :], 0)
    put(q ^ 3, far_y[far_y.shape[0] - half :], half)


def assemble(*pieces):
    rows = pieces[0].shape[0]
    return pl.pallas_call(
        assemble_kernel,
        out_shape=jax.ShapeDtypeStruct((rows, 4 * LANES), BF16),
        in_specs=[VMEM] * 5,
        out_specs=VMEM,
        compiler_params=pltpu.CompilerParams(vmem_limit_bytes=8 * MIB),
        cost_estimate=pl.CostEstimate(flops=0, bytes_accessed=3 * MIB, transcendentals=0),
        name="assemble",
    )(*pieces)


def ring_slot(block):
    z = lax.axis_index("ao")
    return ((z ^ (z >> 1)) - (block ^ (block >> 1))) & 3


def column_block(which, blocks):
    first = lax.axis_index("vir") * blocks
    early, late = ring_slot(first), ring_slot(first + 1)
    swapped = jnp.where(early < late, 0, 1)
    return first + (swapped ^ which)


def fetch(slot, refs, target, sem):
    for s, ref in enumerate(refs):

        def start(ref=ref):
            pltpu.make_async_copy(ref, target, sem).start()

        if len(refs) == 1:
            start()
        else:
            pl.when(slot == s)(start)


def fetched(refs, target, sem):
    pltpu.make_async_copy(refs[0], target, sem).wait()


def first_kernel(n_own, n_shifted, which, blocks, *refs):
    where = refs[:n_shifted]
    shifted = refs[n_shifted : 2 * n_shifted]
    own = refs[2 * n_shifted : 2 * n_shifted + n_own]
    other = refs[2 * n_shifted + n_own : 2 * n_shifted + 2 * n_own]
    out, held, total, sems = refs[2 * n_shifted + 2 * n_own :]
    slot = ring_slot(column_block(which, blocks)) if n_own > 1 else 0
    fetch(slot, own, held.at[0], sems.at[0])
    fetch(slot, other, held.at[1], sems.at[1])
    total[...] = jnp.zeros_like(total)
    fetched(own, held.at[0], sems.at[0])
    fetched(other, held.at[1], sems.at[1])
    for there, tiles in zip(where, shifted):

        def add(i, carry, there=there, tiles=tiles):
            sums = []
            for u in range(UNROLL):
                n = i * UNROLL + u
                base_k = pl.multiple_of(there[1, n], LANES)
                window = held[there[2, n], pl.ds(base_k, COLS_WIN), :]
                sums.append((n, jnp.dot(tiles[n], window, preferred_element_type=F32)))
            for n, value in sums:
                base_m = pl.multiple_of(there[0, n], 16)
                total[pl.ds(base_m, ROWS_WIN), :] += value
            return carry

        lax.fori_loop(0, tiles.shape[0] // UNROLL, add, 0)
    out[...] = total[: out.shape[0], :].astype(BF16)


def first_product(where, shifted, own, other, which, blocks):
    rows, width = own[0].shape
    n_tiles = sum(t.shape[0] for t in shifted)
    count = len(shifted)
    return pl.pallas_call(
        functools.partial(first_kernel, len(own), count, which, blocks),
        out_shape=jax.ShapeDtypeStruct((rows, width), BF16),
        in_specs=[SMEM] * count + [VMEM] * count + [ANY] * (2 * len(own)),
        out_specs=VMEM,
        scratch_shapes=[
            pltpu.VMEM((2, rows, width), BF16),
            pltpu.VMEM((rows + TILE, width), F32),
            pltpu.SemaphoreType.DMA((2,)),
        ],
        compiler_params=pltpu.CompilerParams(vmem_limit_bytes=16 * MIB),
        cost_estimate=pl.CostEstimate(
            flops=n_tiles * 4 * ROWS_WIN * COLS_WIN * width, bytes_accessed=6 * MIB,
            transcendentals=0,
        ),
        name="first_product",
    )(*where, *shifted, *own, *other)


def second_kernel(which, blocks, n_before, *refs):
    pair_occ, eps_occ, eps_vir, middle, middle_other = refs[:5]
    own, other = refs[5 : 5 + GROUPS], refs[5 + GROUPS : 5 + 2 * GROUPS]
    out, held, ready, sems, out_sems = refs[5 + 2 * GROUPS + n_before :]
    core = lax.axis_index("rep")
    rows, width = own[0].shape
    columns = middle.shape[1]
    if blocks > 1:
        block = column_block(which, blocks)
        column = pl.multiple_of((block - lax.axis_index("vir") * blocks) * columns, LANES)
        column_energy = pl.multiple_of(block * columns, LANES)
    else:
        column, column_energy = 0, pl.multiple_of(lax.axis_index("vir") * columns, LANES)
    mine = GROUPS // 2

    def load(i):
        wanted = core * mine + i
        slot = ring_slot(wanted) if blocks > 1 else wanted
        fetch(slot, own, held.at[i, 0], sems.at[i, 0])
        fetch(slot, other, held.at[i, 1], sems.at[i, 1])

    load(0)
    energy = eps_occ[pair_occ[0, 0]] + eps_occ[pair_occ[0, 1]]
    by_column = energy - eps_vir[:, pl.ds(column_energy, columns)]
    dims = (((0,), (0,)), ((), ()))
    stores = []
    for i in range(mine):
        first = core * mine * width + i * width
        tall = [
            jnp.transpose(
                jnp.broadcast_to(
                    eps_vir[:, pl.ds(pl.multiple_of(first + k * LANES, LANES), LANES)],
                    (LANES, LANES),
                )
            )
            for k in range(width // LANES)
        ]
        tall = jnp.concatenate(tall, axis=0)
        tall = jnp.concatenate([tall] * (columns // LANES), axis=1)
        fetched(own, held.at[i, 0], sems.at[i, 0])
        if i + 1 < mine:
            load(i + 1)
        total = lax.dot_general(held[i, 0], middle[...], dims, preferred_element_type=F32)
        fetched(other, held.at[i, 1], sems.at[i, 1])
        total += lax.dot_general(held[i, 1], middle_other[...], dims, preferred_element_type=F32)
        ready[i] = (total / (by_column - tall)).astype(BF16)
        store = pltpu.make_async_copy(
            ready.at[i], out.at[0, pl.ds(i * width, width), pl.ds(column, columns)], out_sems.at[i]
        )
        store.start()
        stores.append(store)
    for store in stores:
        store.wait()


def second_product(which, blocks, pair_occ, eps_occ, eps_vir, middle, groups, others, before):
    rows, width = groups[0].shape
    columns = middle[0].shape[1]
    extra = [] if before is None else [before]
    fixed = [pair_occ, eps_occ, eps_vir, *middle, *groups, *others]
    mine = GROUPS // 2
    return pl.pallas_call(
        functools.partial(second_kernel, which, blocks, len(extra)),
        out_shape=jax.ShapeDtypeStruct((1, mine * width, blocks * columns), BF16),
        in_specs=[SMEM] * 2 + [VMEM] * 3 + [ANY] * (2 * GROUPS + len(extra)),
        out_specs=ANY,
        scratch_shapes=[
            pltpu.VMEM((mine, 2, rows, width), BF16),
            pltpu.VMEM((mine, width, columns), BF16),
            pltpu.SemaphoreType.DMA((mine, 2)),
            pltpu.SemaphoreType.DMA((mine,)),
        ],
        input_output_aliases={len(fixed): 0} if extra else {},
        compiler_params=pltpu.CompilerParams(vmem_limit_bytes=20 * MIB),
        cost_estimate=pl.CostEstimate(
            flops=4 * mine * rows * width * columns, bytes_accessed=10 * MIB, transcendentals=0
        ),
        name="second_product",
    )(*fixed, *extra)


def ring_pairs(distance):
    return [(RING[i], RING[(i + distance) % 4]) for i in range(4)]


def other_core(value):
    return lax.ppermute(value, "rep", SWAP)


def to_x(value):
    return lax.ppermute(value, "vir", SWAP)


def to_y(value):
    return lax.ppermute(value, "grp", SWAP)


def to_z(value, distance=1):
    return lax.ppermute(value, "ao", ring_pairs(distance))


def exchange_small(half_ints, coeff, shift):
    z, x, y = lax.axis_index("ao"), lax.axis_index("vir"), lax.axis_index("grp")
    quarter = y * 2 + x
    gray = lambda n: n ^ (n >> 1)
    owner = [gray((gray(z) + k) & 3) for k in range(4)]
    rows = coeff.shape[0]
    half = rows // 2
    together = lax.optimization_barrier
    join = lambda a, b: jnp.concatenate([a, b], axis=0)

    own = lax.dynamic_slice_in_dim(coeff, quarter * LANES, LANES, 1)
    t = [
        lax.dynamic_index_in_dim(half_ints[:, 0], owner[k], 0, False) for k in range(4)
    ]
    z1, t = together((to_z(own), t))
    x1, y1, z2, t = together((to_x(z1), to_y(z1), to_z(z1), t))
    x2, y2, z3, t1, t = together(
        (to_x(join(z2, y1[:half])), to_y(join(z2, x1[half:])), to_z(z2), to_z(t[1], 1), t)
    )
    group1 = assemble(z1, x1, y1, x2, y2)
    x3, y3, t2, t3, group1, early = together(
        (
            to_x(join(z3, y2[:half])), to_y(join(z3, x2[half:rows])),
            to_z(t[2], 2), to_z(t[3], 3), group1, shift((0, 1), [t[0], t1]),
        )
    )
    group2 = assemble(z2, x2, y2, x3, y3)
    x4, y4, late = together((to_x(y3[:half]), to_y(x3[half:rows]), shift((2, 3), [t2, t3])))
    group3 = assemble(z3, x3, y3, x4, y4)
    return [coeff, group1, group2, group3], [early, late]


def exchange_any(half_ints, coeff):
    count = lax.axis_size("ao")
    gathered = lax.all_gather(coeff, "ao", axis=1, tiled=True)
    width = gathered.shape[1] // GROUPS
    tiles = lax.all_to_all(half_ints, "ao", split_axis=0, concat_axis=2, tiled=True)[0, 0]
    groups = [gathered[:, g * width : (g + 1) * width] for g in range(GROUPS)]
    return gathered, groups, tiles


def local(half_ints, coeff, eps_occ, eps_vir, pair_occ, tile_list, shell_extra):
    sizes = tuple(lax.axis_size(name) for name in ("grp", "ao", "vir"))
    rows, width = coeff.shape
    full_width = width * sizes[1]
    b_width = full_width // sizes[2]
    vir = lax.axis_index("vir")
    ringed = sizes == (2, 4, 2) and width == 4 * LANES
    shift = lambda slots, tiles: shift_tiles(slots, tile_list, shell_extra, tiles, rows)
    if ringed:
        groups, moved = exchange_small(half_ints, coeff, shift)
        own, blocks = groups, b_width // width
    else:
        gathered, groups, tiles = exchange_any(half_ints, coeff)
        own, blocks = [lax.dynamic_slice_in_dim(gathered, vir * b_width, b_width, 1)], 1
        moved = [shift((None,), [tiles])]
    others = [other_core(g) for g in groups]
    other = others if ringed else [other_core(own[0])]
    shifted, where = [m[0] for m in moved], [m[1] for m in moved]
    energies = eps_vir.reshape(1, -1)
    out = None
    for which in range(blocks):
        middle = first_product(where, shifted, own, other, which, blocks)
        middle, where, shifted = lax.optimization_barrier((middle, where, shifted))
        both = (middle, other_core(middle))
        out = second_product(
            which, blocks, pair_occ, eps_occ, energies, both, groups, others, out
        )
    return out


def solution(mesh):
    in_specs = (
        P("grp", "rep", "ao", None, None),
        P("rep", "ao"),
        P(),
        P(),
        P(("grp", "ao"), None),
        P("rep", None, None),
        P(),
    )
    out_specs = P(("grp", "ao"), "rep", "vir")
    return jax.shard_map(local, mesh=mesh, in_specs=in_specs, out_specs=out_specs, check_vma=False)
```

time: 105 us -> 80.7 us (0.77); the launches traced: 105 us -> 79.3 us
  Pallas kernels: 35.6 us -> 25.4 us
  starting transfers between devices: 18 us -> 27.5 us
  waiting for transfers between devices: 28.7 us -> 20 us
  between operations: 7.62 us -> 0.41 us
  local copies, waits for them, and re-layouts: 12 us -> 4.83 us
  other arithmetic: 2.7 us -> 1.08 us
    pallas_call x6, Pallas kernels: 33.7 us -> 24.5 us  [the longest x2 11 us: second_product(): pl.pallas_call(functools.partial(second_kernel, which, blocks, len(extra)...]
    ppermute x6, waiting for transfers between devices: 22.3 us -> 13.8 us  [to_z(): return lax.ppermute(value, 'ao', ring_pairs(distance))]
    ppermute x6, starting transfers between devices: 5.49 us -> 12.9 us  [to_z(): return lax.ppermute(value, 'ao', ring_pairs(distance))]
    unnamed x27 -> x21, local copies, waits for them, and re-layouts: 6.45 us -> 1.71 us
    ppermute x4, waiting for transfers between devices: 5.46 us -> 2.11 us  [to_x(): return lax.ppermute(value, 'vir', SWAP)]
    ppermute x6, waiting for transfers between devices: 0.02 us -> 3.19 us  [other_core(): return lax.ppermute(value, 'rep', SWAP)]
    another operation x1 -> x0, local copies, waits for them, and re-layouts: 2.58 us -> none  [local(): ints = lambda values: jnp.stack([jnp.asarray(v, jnp.int32) for v in values])]
    sub x1 -> x0, other arithmetic: 2.57 us -> none  [local(): b_ids = ids - vir * blocks]
  transfers between devices with their start and end apart: 20 -> 20, of which waited for: 5 -> 7; matrix products, arithmetic and copies ran while one was open for 7% -> 3% of each run, Pallas kernels for 16% -> 21%
where the time goes in v3:
time: 80.7 us; the launch traced here: 79.3 us
  starting transfers between devices  27.5 us (34%)
  Pallas kernels  25.4 us (31%)
  waiting for transfers between devices  20 us (25%)
  local copies, waits for them, and re-layouts  4.83 us (6%)
  other arithmetic  1.08 us (1%)
    ppermute x6, waiting for transfers between devices, to_z(): return lax.ppermute(value, 'ao', ring_pairs(distance))  13.8 us
    ppermute x6, starting transfers between devices, to_z(): return lax.ppermute(value, 'ao', ring_pairs(distance))  12.9 us
    pallas_call x2, Pallas kernels, second_product(): pl.pallas_call(functools.partial(second_kernel, which, blocks, len(extra)...  11 us
    ppermute x6, starting transfers between devices, other_core(): return lax.ppermute(value, 'rep', SWAP)  8.6 us
    pallas_call x2, Pallas kernels, shift_tiles(): pl.pallas_call(functools.partial(shift_kernel, rows_half, slots), out_sha...  7.17 us
    pallas_call x2, Pallas kernels, first_product(): pl.pallas_call(functools.partial(first_kernel, len(own), count, which, bl...  6.29 us
    ppermute x6, waiting for transfers between devices, other_core(): return lax.ppermute(value, 'rep', SWAP)  3.19 us
    ppermute x4, starting transfers between devices, to_x(): return lax.ppermute(value, 'vir', SWAP)  3.06 us
  transfers between devices with their start and end apart: 20, of which 7 were waited for; matrix products, arithmetic and copies ran while one was open for 3% of the time, Pallas kernels for 21%

profile of v3, /device:TPU:9, one launch (start us, length us, event | category | flops | bytes accessed | tf_op | source)
XLA Modules:
  0.0 79.3 jit_solution(12547708475166793631)
XLA Ops:
  0.0 1.0 %constant_dynamic-slice_fusion = bf16[1280,128]{1,0:T(8,128)(2,1)S(1)} fusion(bf16[1280,512]{1,0:T(8,128)(2,1)} %refs_5_.3, s32[]{:T(128)S(6)} %select_n.16), kind=kLoop, calls=%fused_computation.8 | loop fusion | bytes 655364 | tf_op jit(solution)/shard_map/dynamic_slice | solution.py:318
  1.0 2.4 %collective-permute-start = (bf16[1280,128]{1,0:T(8,128)(2,1)S(1)}, bf16[1280,128]{1,0:T(8,128)(2,1)S(1)}, u32[]{:S(2)}, u32[]{:S(2)}) collective-permute-start(bf16[1280,128]{1,0:T(8,128)(2,1)S(1)} %constant_dynamic-slice_fusion), channel_id=1, source_target_pairs={{0,4},{4,12},{12,8},{8,0},{1,5},{5,13},{13,9},{9,1},{2,6},{6,14},{... | collective-permute-start | bytes 983048 | tf_op jit(solution)/shard_map/ppermute | solution.py:305
  3.4 2.1 %dynamic-slice_bitcast_fusion = (bf16[6,128,128]{2,1,0:T(8,128)(2,1)}, bf16[6,128,128]{2,1,0:T(8,128)(2,1)S(1)}, bf16[6,128,128]{2,1,0:T(8,128)(2,1)S(1)}, bf16[6,128,128]{2,1,0:T(8,128)(2,1)}) fusion(bf16[4,1,6,128,128]{4,3,2,1,0:T(8,128)(2,1)} %param.7, s32[]{:T(128)S(6)} %select_n.20, s32[]{:T(128)S(6)} %select_n.18, s32[]{:T(128)S(6)} %select_n.17, ...), kind=kLoop, calls=%fused_computation.4 | loop fusion | bytes 1572880 | tf_op jit(solution)/shard_map/jit(dynamic_index_in_dim)/squeeze | solution.py:320
  5.4 4.3 %collective-permute-done.own = bf16[1280,128]{1,0:T(8,128)(2,1)S(1)} collective-permute-done((bf16[1280,128]{1,0:T(8,128)(2,1)S(1)}, bf16[1280,128]{1,0:T(8,128)(2,1)S(1)}, u32[]{:S(2)}, u32[]{:S(2)}) %collective-permute-start) | collective-permute-done | bytes 327712 | tf_op jit(solution)/shard_map/ppermute | solution.py:305
  9.7 1.2 %collective-permute-start.1 = (bf16[1280,128]{1,0:T(8,128)(2,1)S(1)}, bf16[1280,128]{1,0:T(8,128)(2,1)S(1)}, u32[]{:S(2)}, u32[]{:S(2)}) collective-permute-start(bf16[1280,128]{1,0:T(8,128)(2,1)S(1)} %collective-permute-done.own), channel_id=1, source_target_pairs={{0,2},{2,0},{1,3},{3,1},{4,6},{6,4},{5,7},{7,5},{8,10},{10,8},{9,1... | collective-permute-start | bytes 983048 | tf_op jit(solution)/shard_map/ppermute | solution.py:297
  11.0 1.2 %collective-permute-start.2 = (bf16[1280,128]{1,0:T(8,128)(2,1)S(1)}, bf16[1280,128]{1,0:T(8,128)(2,1)S(1)}, u32[]{:S(2)}, u32[]{:S(2)}) collective-permute-start(bf16[1280,128]{1,0:T(8,128)(2,1)S(1)} %collective-permute-done.own), channel_id=1, source_target_pairs={{0,16},{16,0},{1,17},{17,1},{2,18},{18,2},{3,19},{19,3},{4,20},{20... | collective-permute-start | bytes 983048 | tf_op jit(solution)/shard_map/ppermute | solution.py:301
  12.2 3.1 %collective-permute-start.3 = (bf16[1280,128]{1,0:T(8,128)(2,1)S(1)}, bf16[1280,128]{1,0:T(8,128)(2,1)S(1)}, u32[]{:S(2)}, u32[]{:S(2)}) collective-permute-start(bf16[1280,128]{1,0:T(8,128)(2,1)S(1)} %collective-permute-done.own), channel_id=1, source_target_pairs={{0,4},{4,12},{12,8},{8,0},{1,5},{5,13},{13,9},{9,1},{2,6},{6,14},{... | collective-permute-start | bytes 983048 | tf_op jit(solution)/shard_map/ppermute | solution.py:305
  15.3 2.1 %collective-permute-done.1.by_x = bf16[1280,128]{1,0:T(8,128)(2,1)S(1)} collective-permute-done((bf16[1280,128]{1,0:T(8,128)(2,1)S(1)}, bf16[1280,128]{1,0:T(8,128)(2,1)S(1)}, u32[]{:S(2)}, u32[]{:S(2)}) %collective-permute-start.1) | collective-permute-done | bytes 327712 | tf_op jit(solution)/shard_map/ppermute | solution.py:297
  17.4 0.9 %collective-permute-done.2.by_y = bf16[1280,128]{1,0:T(8,128)(2,1)S(1)} collective-permute-done((bf16[1280,128]{1,0:T(8,128)(2,1)S(1)}, bf16[1280,128]{1,0:T(8,128)(2,1)S(1)}, u32[]{:S(2)}, u32[]{:S(2)}) %collective-permute-start.2) | collective-permute-done | bytes 327712 | tf_op jit(solution)/shard_map/ppermute | solution.py:301
  18.3 1.9 %collective-permute-done.3.own = bf16[1280,128]{1,0:T(8,128)(2,1)S(1)} collective-permute-done((bf16[1280,128]{1,0:T(8,128)(2,1)S(1)}, bf16[1280,128]{1,0:T(8,128)(2,1)S(1)}, u32[]{:S(2)}, u32[]{:S(2)}) %collective-permute-start.3) | collective-permute-done | bytes 327712 | tf_op jit(solution)/shard_map/ppermute | solution.py:305
  20.3 0.3 collective-permute-start.4
  20.9 3.1 %collective-permute-start.6 = (bf16[1280,128]{1,0:T(8,128)(2,1)S(1)}, bf16[1280,128]{1,0:T(8,128)(2,1)S(1)}, u32[]{:S(2)}, u32[]{:S(2)}) collective-permute-start(bf16[1280,128]{1,0:T(8,128)(2,1)S(1)} %collective-permute-done.3.own), channel_id=1, source_target_pairs={{0,4},{4,12},{12,8},{8,0},{1,5},{5,13},{13,9},{9,1},{2,6},{6,14},{... | collective-permute-start | bytes 983048 | tf_op jit(solution)/shard_map/ppermute | solution.py:305
  24.0 7.6 %collective-permute-done.7.refs_3_ = bf16[6,128,128]{2,1,0:T(8,128)(2,1)S(1)} collective-permute-done((bf16[6,128,128]{2,1,0:T(8,128)(2,1)S(1)}, bf16[6,128,128]{2,1,0:T(8,128)(2,1)S(1)}, u32[]{:S(2)}, u32[]{:S(2)}) %collective-permute-start.7) | collective-permute-done | bytes 196640 | tf_op jit(solution)/shard_map/ppermute | solution.py:305
  31.6 1.0 %pad_maximum_fusion.2 = (bf16[1920,128]{1,0:T(8,128)(2,1)}, bf16[1920,128]{1,0:T(8,128)(2,1)}) fusion(bf16[1280,128]{1,0:T(8,128)(2,1)S(1)} %collective-permute-done.6.own, bf16[640,128]{1,0:T(8,128)(2,1)S(1)} %slice.21, bf16[640,128]{1,0:T(8,128)(2,1)S(1)} %slice.20), kind=kLoop, calls=%fused_computation.2 | loop fusion | flops 1720320 | bytes 1638400 | tf_op jit(solution)/shard_map/concatenate | solution.py:316
  32.7 1.2 %collective-permute-start.8 = (bf16[1920,128]{1,0:T(8,128)(2,1)}, bf16[1920,128]{1,0:T(8,128)(2,1)S(1)}, u32[]{:S(2)}, u32[]{:S(2)}) collective-permute-start(bf16[1920,128]{1,0:T(8,128)(2,1)} %get-tuple-element.90), channel_id=1, source_target_pairs={{0,2},{2,0},{1,3},{3,1},{4,6},{6,4},{5,7},{7,5},{8,10},{10,8},{9,1... | collective-permute-start | bytes 1474568 | tf_op jit(solution)/shard_map/ppermute | solution.py:297
  33.9 1.2 %collective-permute-start.9 = (bf16[1920,128]{1,0:T(8,128)(2,1)}, bf16[1920,128]{1,0:T(8,128)(2,1)S(1)}, u32[]{:S(2)}, u32[]{:S(2)}) collective-permute-start(bf16[1920,128]{1,0:T(8,128)(2,1)} %get-tuple-element.89), channel_id=1, source_target_pairs={{0,16},{16,0},{1,17},{17,1},{2,18},{18,2},{3,19},{19,3},{4,20},{20... | collective-permute-start | bytes 1474568 | tf_op jit(solution)/shard_map/ppermute | solution.py:301
  35.1 1.3 %collective-permute-start.10 = (bf16[6,128,128]{2,1,0:T(8,128)(2,1)}, bf16[6,128,128]{2,1,0:T(8,128)(2,1)}, u32[]{:S(2)}, u32[]{:S(2)}) collective-permute-start(bf16[6,128,128]{2,1,0:T(8,128)(2,1)} %get-tuple-element.60), channel_id=1, source_target_pairs={{0,12},{4,8},{12,0},{8,4},{1,13},{5,9},{13,1},{9,5},{2,14},{6,10},... | collective-permute-start | bytes 589832 | tf_op jit(solution)/shard_map/ppermute | solution.py:305
  36.4 3.0 %collective-permute-start.11 = (bf16[6,128,128]{2,1,0:T(8,128)(2,1)}, bf16[6,128,128]{2,1,0:T(8,128)(2,1)}, u32[]{:S(2)}, u32[]{:S(2)}) collective-permute-start(bf16[6,128,128]{2,1,0:T(8,128)(2,1)} %get-tuple-element.61), channel_id=1, source_target_pairs={{0,8},{4,0},{12,4},{8,12},{1,9},{5,1},{13,5},{9,13},{2,10},{6,2},{... | collective-permute-start | bytes 589832 | tf_op jit(solution)/shard_map/ppermute | solution.py:305
  39.5 1.0 %copy-done.2 = bf16[1280,128]{1,0:T(8,128)(2,1)S(1)} copy-done((bf16[1280,128]{1,0:T(8,128)(2,1)S(1)}, bf16[1280,128]{1,0:T(8,128)(2,1)}, u32[]{:S(2)}) %copy-start.2) | copy-done | bytes 327704
  40.8 0.6 copy-done.4
  41.4 3.4 %shift_tiles.2 = (bf16[12,144,256]{2,1,0:T(8,128)(2,1)S(1)}, s32[3,12]{1,0:T(4,128)S(1)}) custom-call(s32[1,24,2]{2,1,0:T(8,128)S(1)} %copy.9.refs_0_, s32[2,12]{1,0:T(2,128)S(1)} %copy-done.7, bf16[6,128,128]{2,1,0:T(8,128)(2,1)S(1)} %get-tuple-element.62.refs_2_, bf16[6,128,128]{2,1,0:T(8,128)(2,1)S(1)} %copy-done.4), custom_call_target="tpu_custom_call" | custom-call | bytes 8388608 | tf_op jit(solution)/shard_map/shift_tiles/pallas_call | solution.py:82
  44.9 0.3 collective-permute-start.12
  45.5 7.2 %collective-permute-start.14 = (bf16[1280,512]{1,0:T(8,128)(2,1)S(1)}, bf16[1280,512]{1,0:T(8,128)(2,1)S(1)}, u32[]{:S(2)}, u32[]{:S(2)}) collective-permute-start(bf16[1280,512]{1,0:T(8,128)(2,1)S(1)} %copy-done), channel_id=1, source_target_pairs={{0,1},{1,0},{2,3},{3,2},{4,5},{5,4},{6,7},{7,6},{8,9},{9,8},{10,11... | collective-permute-start | bytes 3932168 | tf_op jit(solution)/shard_map/ppermute | solution.py:293
  53.2 0.5 collective-permute-start.15
  53.7 3.7 %shift_tiles.3 = (bf16[12,144,256]{2,1,0:T(8,128)(2,1)S(1)}, s32[3,12]{1,0:T(4,128)S(1)}) custom-call(s32[1,24,2]{2,1,0:T(8,128)S(1)} %copy.9.refs_0_, s32[2,12]{1,0:T(2,128)S(1)} %copy-done.7, bf16[6,128,128]{2,1,0:T(8,128)(2,1)} %collective-permute-done.10.refs_2_, bf16[6,128,128]{2,1,0:T(8,128)(2,1)} %collective-permute-done.11.refs_3_), custom_call_target="tpu_custom_call" | custom-call | bytes 8388608 | tf_op jit(solution)/shard_map/shift_tiles/pallas_call | solution.py:82
  57.9 1.3 %collective-permute-done.15.refs_9_.refs_10_ = bf16[1280,512]{1,0:T(8,128)(2,1)S(1)} collective-permute-done((bf16[1280,512]{1,0:T(8,128)(2,1)S(1)}, bf16[1280,512]{1,0:T(8,128)(2,1)S(1)}, u32[]{:S(2)}, u32[]{:S(2)}) %collective-permute-start.15) | collective-permute-done | bytes 1310752 | tf_op jit(solution)/shard_map/ppermute | solution.py:293
  59.2 1.9 %collective-permute-done.17.refs_11_.refs_12_ = bf16[1280,512]{1,0:T(8,128)(2,1)S(1)} collective-permute-done((bf16[1280,512]{1,0:T(8,128)(2,1)S(1)}, bf16[1280,512]{1,0:T(8,128)(2,1)S(1)}, u32[]{:S(2)}, u32[]{:S(2)}) %collective-permute-start.17) | collective-permute-done | bytes 1310752 | tf_op jit(solution)/shard_map/ppermute | solution.py:293
  61.1 3.1 %first_product.2.refs_3_ = bf16[1280,512]{1,0:T(8,128)(2,1)S(1)} custom-call(s32[3,12]{1,0:T(4,128)S(1)} %get-tuple-element.79.refs_0_, s32[3,12]{1,0:T(4,128)S(1)} %get-tuple-element.80.refs_1_, bf16[12,144,256]{2,1,0:T(8,128)(2,1)S(1)} %get-tuple-element.81.refs_2_, bf16[12,144,256]{2,1,0:T(8,128)(2,1)S(1)} %get-tuple-element.82.refs_3_, ...), custom_call_target="tpu_custom_call" | custom-call | flops 1811939328 | bytes 6291456 | tf_op jit(solution)/shard_map/first_product/pallas_call | solution.py:188
  64.3 0.4 collective-permute-start.19
  64.7 3.1 %first_product.3.refs_3_ = bf16[1280,512]{1,0:T(8,128)(2,1)S(1)} custom-call(s32[3,12]{1,0:T(4,128)S(1)} %get-tuple-element.79.refs_0_, s32[3,12]{1,0:T(4,128)S(1)} %get-tuple-element.80.refs_1_, bf16[12,144,256]{2,1,0:T(8,128)(2,1)S(1)} %get-tuple-element.81.refs_2_, bf16[12,144,256]{2,1,0:T(8,128)(2,1)S(1)} %get-tuple-element.82.refs_3_, ...), custom_call_target="tpu_custom_call" | custom-call | flops 1811939328 | bytes 6291456 | tf_op jit(solution)/shard_map/first_product/pallas_call | solution.py:188
  68.1 5.4 %second_product.2.refs_13_ = bf16[1,1024,1024]{2,1,0:T(8,128)(2,1)} custom-call(s32[1,2]{1,0:T(1,128)S(1)} %copy-done.8, f32[400]{0:T(512)S(1)} %copy-done.6, f32[1,2048]{1,0:T(1,128)S(1)} %bitcast.9, bf16[1280,512]{1,0:T(8,128)(2,1)S(1)} %first_product.2.refs_3_, bf16[1280,512]{1,0:T(8,128)(2,1)S(1)} %collective-permute-done.19.refs_4_, ...), custom_call_target="tpu_custom_call" | custom-call | flops 2684354560 | bytes 10485760 | tf_op jit(solution)/shard_map/second_product/pallas_call | solution.py:268
  73.5 5.6 %second_product.3 = bf16[1,1024,1024]{2,1,0:T(8,128)(2,1)} custom-call(s32[1,2]{1,0:T(1,128)S(1)} %copy-done.8, f32[400]{0:T(512)S(1)} %copy-done.6, f32[1,2048]{1,0:T(1,128)S(1)} %bitcast.10, bf16[1280,512]{1,0:T(8,128)(2,1)S(1)} %first_product.3.refs_3_, bf16[1280,512]{1,0:T(8,128)(2,1)S(1)} %collective-permute-done.18.refs_4_, ...), custom_call_target="tpu_custom_call", output_to_operand_aliasing={{}: (13, {})} | custom-call | flops 2684354560 | bytes 10485760 | tf_op jit(solution)/shard_map/second_product/pallas_call | solution.py:268
  (48 shorter events, 2.2 us)
Async XLA Ops:
  1.0 8.7 %collective-permute-start = (bf16[1280,128]{1,0:T(8,128)(2,1)S(1)}, bf16[1280,128]{1,0:T(8,128)(2,1)S(1)}, u32[]{:S(2)}, u32[]{:S(2)}) collective-permute-start(bf16[1280,128]{1,0:T(8,128)(2,1)S(1)} %constant_dynamic-slice_fusion), channel_id=1, source_target_pairs={{0,4},{4,12},{12,8},{8,0},{1,5},{5,13},{13,9},{9,1},{2,6},{6,14},{... | collective-permute-start | bytes 983048 | tf_op jit(solution)/shard_map/ppermute | solution.py:305
  9.7 10.9 %copy-start.1 = (bf16[1280,128]{1,0:T(8,128)(2,1)}, bf16[1280,128]{1,0:T(8,128)(2,1)S(1)}, u32[]{:S(2)}) copy-start(bf16[1280,128]{1,0:T(8,128)(2,1)S(1)} %collective-permute-done.own) | copy-start | bytes 983044
  9.7 7.7 %collective-permute-start.1 = (bf16[1280,128]{1,0:T(8,128)(2,1)S(1)}, bf16[1280,128]{1,0:T(8,128)(2,1)S(1)}, u32[]{:S(2)}, u32[]{:S(2)}) collective-permute-start(bf16[1280,128]{1,0:T(8,128)(2,1)S(1)} %collective-permute-done.own), channel_id=1, source_target_pairs={{0,2},{2,0},{1,3},{3,1},{4,6},{6,4},{5,7},{7,5},{8,10},{10,8},{9,1... | collective-permute-start | bytes 983048 | tf_op jit(solution)/shard_map/ppermute | solution.py:297
  11.0 7.4 %collective-permute-start.2 = (bf16[1280,128]{1,0:T(8,128)(2,1)S(1)}, bf16[1280,128]{1,0:T(8,128)(2,1)S(1)}, u32[]{:S(2)}, u32[]{:S(2)}) collective-permute-start(bf16[1280,128]{1,0:T(8,128)(2,1)S(1)} %collective-permute-done.own), channel_id=1, source_target_pairs={{0,16},{16,0},{1,17},{17,1},{2,18},{18,2},{3,19},{19,3},{4,20},{20... | collective-permute-start | bytes 983048 | tf_op jit(solution)/shard_map/ppermute | solution.py:301
  12.2 8.0 %collective-permute-start.3 = (bf16[1280,128]{1,0:T(8,128)(2,1)S(1)}, bf16[1280,128]{1,0:T(8,128)(2,1)S(1)}, u32[]{:S(2)}, u32[]{:S(2)}) collective-permute-start(bf16[1280,128]{1,0:T(8,128)(2,1)S(1)} %collective-permute-done.own), channel_id=1, source_target_pairs={{0,4},{4,12},{12,8},{8,0},{1,5},{5,13},{13,9},{9,1},{2,6},{6,14},{... | collective-permute-start | bytes 983048 | tf_op jit(solution)/shard_map/ppermute | solution.py:305
  20.3 19.1 %copy-start.9 = (s32[1,24,2]{1,2,0:T(2,128)S(1)}, s32[1,24,2]{1,2,0:T(2,128)}, u32[]{:S(2)}) copy-start(s32[1,24,2]{1,2,0:T(2,128)} %param.12) | copy-start | bytes 580
  20.3 11.3 %collective-permute-start.4 = (bf16[1920,128]{1,0:T(8,128)(2,1)S(1)}, bf16[1920,128]{1,0:T(8,128)(2,1)S(1)}, u32[]{:S(2)}, u32[]{:S(2)}) collective-permute-start(bf16[1920,128]{1,0:T(8,128)(2,1)S(1)} %get-tuple-element.92), channel_id=1, source_target_pairs={{0,2},{2,0},{1,3},{3,1},{4,6},{6,4},{5,7},{7,5},{8,10},{10,8},{9,1... | collective-permute-start | bytes 1474568 | tf_op jit(solution)/shard_map/ppermute | solution.py:297
  20.6 11.0 %collective-permute-start.5 = (bf16[1920,128]{1,0:T(8,128)(2,1)S(1)}, bf16[1920,128]{1,0:T(8,128)(2,1)S(1)}, u32[]{:S(2)}, u32[]{:S(2)}) collective-permute-start(bf16[1920,128]{1,0:T(8,128)(2,1)S(1)} %get-tuple-element.91), channel_id=1, source_target_pairs={{0,16},{16,0},{1,17},{17,1},{2,18},{18,2},{3,19},{19,3},{4,20},{20... | collective-permute-start | bytes 1474568 | tf_op jit(solution)/shard_map/ppermute | solution.py:301
  20.9 10.7 %collective-permute-start.6 = (bf16[1280,128]{1,0:T(8,128)(2,1)S(1)}, bf16[1280,128]{1,0:T(8,128)(2,1)S(1)}, u32[]{:S(2)}, u32[]{:S(2)}) collective-permute-start(bf16[1280,128]{1,0:T(8,128)(2,1)S(1)} %collective-permute-done.3.own), channel_id=1, source_target_pairs={{0,4},{4,12},{12,8},{8,0},{1,5},{5,13},{13,9},{9,1},{2,6},{6,14},{... | collective-permute-start | bytes 983048 | tf_op jit(solution)/shard_map/ppermute | solution.py:305
  24.0 7.6 %collective-permute-start.7 = (bf16[6,128,128]{2,1,0:T(8,128)(2,1)S(1)}, bf16[6,128,128]{2,1,0:T(8,128)(2,1)S(1)}, u32[]{:S(2)}, u32[]{:S(2)}) collective-permute-start(bf16[6,128,128]{2,1,0:T(8,128)(2,1)S(1)} %get-tuple-element.53), channel_id=1, source_target_pairs={{0,4},{4,12},{12,8},{8,0},{1,5},{5,13},{13,9},{9,1},{2,6},{6,14},{... | collective-permute-start | bytes 589832 | tf_op jit(solution)/shard_map/ppermute | solution.py:305
  31.6 1.1 %copy-start.3 = (bf16[6,128,128]{2,1,0:T(8,128)(2,1)}, bf16[6,128,128]{2,1,0:T(8,128)(2,1)S(1)}, u32[]{:S(2)}) copy-start(bf16[6,128,128]{2,1,0:T(8,128)(2,1)S(1)} %collective-permute-done.7.refs_3_) | copy-start | bytes 589828
  32.7 12.2 %collective-permute-start.8 = (bf16[1920,128]{1,0:T(8,128)(2,1)}, bf16[1920,128]{1,0:T(8,128)(2,1)S(1)}, u32[]{:S(2)}, u32[]{:S(2)}) collective-permute-start(bf16[1920,128]{1,0:T(8,128)(2,1)} %get-tuple-element.90), channel_id=1, source_target_pairs={{0,2},{2,0},{1,3},{3,1},{4,6},{6,4},{5,7},{7,5},{8,10},{10,8},{9,1... | collective-permute-start | bytes 1474568 | tf_op jit(solution)/shard_map/ppermute | solution.py:297
  33.9 11.0 %collective-permute-start.9 = (bf16[1920,128]{1,0:T(8,128)(2,1)}, bf16[1920,128]{1,0:T(8,128)(2,1)S(1)}, u32[]{:S(2)}, u32[]{:S(2)}) collective-permute-start(bf16[1920,128]{1,0:T(8,128)(2,1)} %get-tuple-element.89), channel_id=1, source_target_pairs={{0,16},{16,0},{1,17},{17,1},{2,18},{18,2},{3,19},{19,3},{4,20},{20... | collective-permute-start | bytes 1474568 | tf_op jit(solution)/shard_map/ppermute | solution.py:301
  35.1 9.7 %collective-permute-start.10 = (bf16[6,128,128]{2,1,0:T(8,128)(2,1)}, bf16[6,128,128]{2,1,0:T(8,128)(2,1)}, u32[]{:S(2)}, u32[]{:S(2)}) collective-permute-start(bf16[6,128,128]{2,1,0:T(8,128)(2,1)} %get-tuple-element.60), channel_id=1, source_target_pairs={{0,12},{4,8},{12,0},{8,4},{1,13},{5,9},{13,1},{9,5},{2,14},{6,10},... | collective-permute-start | bytes 589832 | tf_op jit(solution)/shard_map/ppermute | solution.py:305
  36.4 8.4 %collective-permute-start.11 = (bf16[6,128,128]{2,1,0:T(8,128)(2,1)}, bf16[6,128,128]{2,1,0:T(8,128)(2,1)}, u32[]{:S(2)}, u32[]{:S(2)}) collective-permute-start(bf16[6,128,128]{2,1,0:T(8,128)(2,1)} %get-tuple-element.61), channel_id=1, source_target_pairs={{0,8},{4,0},{12,4},{8,12},{1,9},{5,1},{13,5},{9,13},{2,10},{6,2},{... | collective-permute-start | bytes 589832 | tf_op jit(solution)/shard_map/ppermute | solution.py:305
  39.5 1.0 %copy-start.2 = (bf16[1280,128]{1,0:T(8,128)(2,1)S(1)}, bf16[1280,128]{1,0:T(8,128)(2,1)}, u32[]{:S(2)}) copy-start(bf16[1280,128]{1,0:T(8,128)(2,1)} %copy-done.1) | copy-start | bytes 983044
  40.5 0.9 %copy-start.4 = (bf16[6,128,128]{2,1,0:T(8,128)(2,1)S(1)}, bf16[6,128,128]{2,1,0:T(8,128)(2,1)}, u32[]{:S(2)}) copy-start(bf16[6,128,128]{2,1,0:T(8,128)(2,1)} %copy-done.3) | copy-start | bytes 589828
  40.5 0.9 %copy-start.7 = (s32[2,12]{1,0:T(2,128)S(1)}, s32[2,12]{1,0:T(2,128)}, u32[]{:S(2)}) copy-start(s32[2,12]{1,0:T(2,128)} %refs_1_.5) | copy-start | bytes 292
  40.5 5.1 %copy-start = (bf16[1280,512]{1,0:T(8,128)(2,1)S(1)}, bf16[1280,512]{1,0:T(8,128)(2,1)}, u32[]{:S(2)}) copy-start(bf16[1280,512]{1,0:T(8,128)(2,1)} %refs_5_.3) | copy-start | bytes 3932164
  44.9 12.5 %collective-permute-start.12 = (bf16[640,128]{1,0:T(8,128)(2,1)S(1)}, bf16[640,128]{1,0:T(8,128)(2,1)S(1)}, u32[]{:S(2)}, u32[]{:S(2)}) collective-permute-start(bf16[640,128]{1,0:T(8,128)(2,1)S(1)} %slice.22), channel_id=1, source_target_pairs={{0,2},{2,0},{1,3},{3,1},{4,6},{6,4},{5,7},{7,5},{8,10},{10,8},{9,1... | collective-permute-start | bytes 491528 | tf_op jit(solution)/shard_map/ppermute | solution.py:297
  45.2 12.2 %collective-permute-start.13 = (bf16[640,128]{1,0:T(8,128)(2,1)S(1)}, bf16[640,128]{1,0:T(8,128)(2,1)S(1)}, u32[]{:S(2)}, u32[]{:S(2)}) collective-permute-start(bf16[640,128]{1,0:T(8,128)(2,1)S(1)} %slice.23), channel_id=1, source_target_pairs={{0,16},{16,0},{1,17},{17,1},{2,18},{18,2},{3,19},{19,3},{4,20},{20... | collective-permute-start | bytes 491528 | tf_op jit(solution)/shard_map/ppermute | solution.py:301
  45.5 12.3 %collective-permute-start.14 = (bf16[1280,512]{1,0:T(8,128)(2,1)S(1)}, bf16[1280,512]{1,0:T(8,128)(2,1)S(1)}, u32[]{:S(2)}, u32[]{:S(2)}) collective-permute-start(bf16[1280,512]{1,0:T(8,128)(2,1)S(1)} %copy-done), channel_id=1, source_target_pairs={{0,1},{1,0},{2,3},{3,2},{4,5},{5,4},{6,7},{7,6},{8,9},{9,8},{10,11... | collective-permute-start | bytes 3932168 | tf_op jit(solution)/shard_map/ppermute | solution.py:293
  53.1 4.8 %collective-permute-start.16 = (bf16[1280,512]{1,0:T(8,128)(2,1)S(1)}, bf16[1280,512]{1,0:T(8,128)(2,1)S(1)}, u32[]{:S(2)}, u32[]{:S(2)}) collective-permute-start(bf16[1280,512]{1,0:T(8,128)(2,1)S(1)} %assemble.4.refs_6_.refs_7_), channel_id=1, source_target_pairs={{0,1},{1,0},{2,3},{3,2},{4,5},{5,4},{6,7},{7,6},{8,9},{9,8},{10,11... | collective-permute-start | bytes 3932168 | tf_op jit(solution)/shard_map/ppermute | solution.py:293
  53.2 6.0 %collective-permute-start.15 = (bf16[1280,512]{1,0:T(8,128)(2,1)S(1)}, bf16[1280,512]{1,0:T(8,128)(2,1)S(1)}, u32[]{:S(2)}, u32[]{:S(2)}) collective-permute-start(bf16[1280,512]{1,0:T(8,128)(2,1)S(1)} %assemble.3.refs_5_.refs_6_), channel_id=1, source_target_pairs={{0,1},{1,0},{2,3},{3,2},{4,5},{5,4},{6,7},{7,6},{8,9},{9,8},{10,11... | collective-permute-start | bytes 3932168 | tf_op jit(solution)/shard_map/ppermute | solution.py:293
  57.7 3.3 %collective-permute-start.17 = (bf16[1280,512]{1,0:T(8,128)(2,1)S(1)}, bf16[1280,512]{1,0:T(8,128)(2,1)S(1)}, u32[]{:S(2)}, u32[]{:S(2)}) collective-permute-start(bf16[1280,512]{1,0:T(8,128)(2,1)S(1)} %assemble.5.refs_7_.refs_8_), channel_id=1, source_target_pairs={{0,1},{1,0},{2,3},{3,2},{4,5},{5,4},{6,7},{7,6},{8,9},{9,8},{10,11... | collective-permute-start | bytes 3932168 | tf_op jit(solution)/shard_map/ppermute | solution.py:293
  64.2 3.8 %copy-start.5 = (f32[2048]{0:T(1024)S(1)}, f32[2048]{0:T(1024)}, u32[]{:S(2)}) copy-start(f32[2048]{0:T(1024)} %param.10) | copy-start | bytes 24580
  64.2 3.8 %copy-start.6 = (f32[400]{0:T(512)S(1)}, f32[400]{0:T(512)}, u32[]{:S(2)}) copy-start(f32[400]{0:T(512)} %refs_1_.7) | copy-start | bytes 4804
  64.2 3.8 %copy-start.8 = (s32[1,2]{1,0:T(1,128)S(1)}, s32[1,2]{1,0:T(1,128)}, u32[]{:S(2)}) copy-start(s32[1,2]{1,0:T(1,128)} %refs_0_.5) | copy-start | bytes 28
  64.3 3.8 %collective-permute-start.19 = (bf16[1280,512]{1,0:T(8,128)(2,1)S(1)}, bf16[1280,512]{1,0:T(8,128)(2,1)S(1)}, u32[]{:S(2)}, u32[]{:S(2)}) collective-permute-start(bf16[1280,512]{1,0:T(8,128)(2,1)S(1)} %first_product.2.refs_3_), channel_id=1, source_target_pairs={{0,1},{1,0},{2,3},{3,2},{4,5},{5,4},{6,7},{7,6},{8,9},{9,8},{10,11... | collective-permute-start | bytes 3932168 | tf_op jit(solution)/shard_map/ppermute | solution.py:293
  67.8 5.6 %collective-permute-start.18 = (bf16[1280,512]{1,0:T(8,128)(2,1)S(1)}, bf16[1280,512]{1,0:T(8,128)(2,1)S(1)}, u32[]{:S(2)}, u32[]{:S(2)}) collective-permute-start(bf16[1280,512]{1,0:T(8,128)(2,1)S(1)} %first_product.3.refs_3_), channel_id=1, source_target_pairs={{0,1},{1,0},{2,3},{3,2},{4,5},{5,4},{6,7},{7,6},{8,9},{9,8},{10,11... | collective-permute-start | bytes 3932168 | tf_op jit(solution)/shard_map/ppermute | solution.py:293

commit v4 on v3

v4 whole, which is shorter than its diff:
```python
import functools

import jax
import jax.numpy as jnp
from jax import lax
from jax.experimental import pallas as pl
from jax.experimental.pallas import tpu as pltpu
from jax.sharding import PartitionSpec as P

TILE = 128
HALF_BLK = 12
LANES = 128
ROWS_WIN = 144
COLS_WIN = 256
GROUPS = 4
UNROLL = 6
SHIFT_UNROLL = 3
RING = (0, 1, 3, 2)
SWAP = ((0, 1), (1, 0))
F32 = jnp.float32
BF16 = jnp.bfloat16
SMEM = pl.BlockSpec(memory_space=pltpu.SMEM)
VMEM = pl.BlockSpec(memory_space=pltpu.VMEM)
ANY = pl.BlockSpec(memory_space=pl.ANY)
MIB = 1 << 20


def ring_group(step):
    z = lax.axis_index("ao")
    spot = ((z ^ (z >> 1)) - step) & 3
    return spot ^ (spot >> 1)


def plan_kernel(slots, count, rows_half, a_width, listed, extra, pair_occ, eps_occ, eps_vir, plan, by_col, by_row, offsets):
    core = lax.axis_index("rep")

    def lay(k, start):
        start = jnp.where(k == HALF_BLK, 0, start)
        offsets[k] = start
        return start + TILE // 2 + extra[k // HALF_BLK, lax.rem(k, HALF_BLK)]

    lax.fori_loop(0, 2 * HALF_BLK, lay, jnp.int32(0))
    for r, slot in enumerate(slots):
        first = 0 if slot is None else ring_group(slot) * count

        def one(i, carry, r=r, first=first):
            m = listed[0, first + i, 0]
            k = listed[0, first + i, 1]
            half_k = k // HALF_BLK
            off_m = offsets[core * HALF_BLK + m]
            off_k = offsets[k]
            base_m = (off_m // 16) * 16
            base_k = jnp.minimum((off_k // LANES) * LANES, rows_half - COLS_WIN)
            at = r * count + i
            plan[0, at] = base_m
            plan[1, at] = base_k
            plan[2, at] = jnp.where(half_k == core, 0, 1)
            plan[3, at] = off_m - base_m
            plan[4, at] = off_k - base_k
            plan[5, at] = TILE // 2 + extra[core, m]
            plan[6, at] = TILE // 2 + extra[half_k, lax.rem(k, HALF_BLK)]
            return carry

        lax.fori_loop(0, count, one, 0)
    energy = eps_occ[pair_occ[0, 0]] + eps_occ[pair_occ[0, 1]]
    columns = by_col.shape[1]
    start = pl.multiple_of(lax.axis_index("vir") * columns, LANES)
    by_col[...] = energy - eps_vir[:, pl.ds(start, columns)]
    for k in range(a_width // LANES):
        start = pl.multiple_of(core * a_width + k * LANES, LANES)
        row = jnp.broadcast_to(eps_vir[:, pl.ds(start, LANES)], (LANES, LANES))
        by_row[k * LANES : (k + 1) * LANES, :] = jnp.transpose(row)


def make_plan(slots, listed, shell_extra, pair_occ, eps_occ, eps_vir, rows_half, a_width, b_width):
    total = listed.shape[1]
    return pl.pallas_call(
        functools.partial(plan_kernel, slots, total // len(slots), rows_half, a_width),
        out_shape=(
            jax.ShapeDtypeStruct((7, total), jnp.int32),
            jax.ShapeDtypeStruct((1, b_width), F32),
            jax.ShapeDtypeStruct((a_width, LANES), F32),
        ),
        in_specs=[SMEM] * 4 + [VMEM],
        out_specs=(SMEM, VMEM, VMEM),
        scratch_shapes=[pltpu.SMEM((2 * HALF_BLK,), jnp.int32)],
        compiler_params=pltpu.CompilerParams(vmem_limit_bytes=6 * MIB),
        cost_estimate=pl.CostEstimate(flops=0, bytes_accessed=2 * MIB, transcendentals=0),
        name="make_plan",
    )(listed, shell_extra, pair_occ, eps_occ, eps_vir)


def shift_loop(plan, first, held, shifted):
    down_from = lax.broadcasted_iota(jnp.int32, (ROWS_WIN, TILE), 1)
    down = lax.broadcasted_iota(jnp.int32, (ROWS_WIN, TILE), 0) - down_from
    right_from = lax.broadcasted_iota(jnp.int32, (TILE, COLS_WIN), 0)
    right = lax.broadcasted_iota(jnp.int32, (TILE, COLS_WIN), 1) - right_from

    def some(group, carry):
        moved = []
        for u in range(SHIFT_UNROLL):
            i = group * SHIFT_UNROLL + u
            at = first + i
            take_m = jnp.where((down == plan[3, at]) & (down_from < plan[5, at]), 1.0, 0.0)
            take_k = jnp.where((right == plan[4, at]) & (right_from < plan[6, at]), 1.0, 0.0)
            value = jnp.dot(take_m.astype(BF16), held[i], preferred_element_type=F32)
            moved.append((i, value.astype(BF16), take_k.astype(BF16)))
        for i, value, take_k in moved:
            value = jnp.dot(value, take_k, preferred_element_type=F32)
            shifted[i] = value.astype(BF16)
        return carry

    lax.fori_loop(0, held.shape[0] // SHIFT_UNROLL, some, 0)


def tile_copies(tiles, held, sems):
    count = tiles[0].shape[0]
    return [
        pltpu.make_async_copy(ref, held.at[pl.ds(r * count, count)], sems.at[r])
        for r, ref in enumerate(tiles)
    ]


def shift_kernel(first, n_refs, *refs):
    plan = refs[0]
    tiles = refs[1 : 1 + n_refs]
    shifted, held, sems = refs[1 + n_refs :]
    copies = tile_copies(tiles, held, sems)
    for copy in copies:
        copy.start()
    for copy in copies:
        copy.wait()
    shift_loop(plan, first, held, shifted)


def shift_tiles(plan, first, tiles):
    total = sum(t.shape[0] for t in tiles)
    return pl.pallas_call(
        functools.partial(shift_kernel, first, len(tiles)),
        out_shape=jax.ShapeDtypeStruct((total, ROWS_WIN, COLS_WIN), BF16),
        in_specs=[SMEM] + [ANY] * len(tiles),
        out_specs=VMEM,
        scratch_shapes=[
            pltpu.VMEM((total, TILE, TILE), BF16),
            pltpu.SemaphoreType.DMA((len(tiles),)),
        ],
        compiler_params=pltpu.CompilerParams(vmem_limit_bytes=14 * MIB),
        cost_estimate=pl.CostEstimate(flops=0, bytes_accessed=8 * MIB, transcendentals=0),
        name="shift_tiles",
    )(plan, *tiles)


def stay_kernel(value, out):
    out[...] = value[...]


def stay(value):
    return pl.pallas_call(
        stay_kernel,
        out_shape=jax.ShapeDtypeStruct(value.shape, value.dtype),
        in_specs=[VMEM],
        out_specs=VMEM,
        compiler_params=pltpu.CompilerParams(vmem_limit_bytes=8 * MIB),
        cost_estimate=pl.CostEstimate(flops=0, bytes_accessed=3 * MIB, transcendentals=0),
        name="stay",
    )(value)


def assemble_kernel(own, by_x, by_y, far_x, far_y, out, sems):
    rows = own.shape[0]
    half = rows // 2
    q = lax.axis_index("grp") * 2 + lax.axis_index("vir")
    parts = (
        (own, 0, rows, q, 0),
        (by_x, 0, rows, q ^ 1, 0),
        (by_y, 0, rows, q ^ 2, 0),
        (far_x, far_x.shape[0] - half, half, q ^ 3, 0),
        (far_y, far_y.shape[0] - half, half, q ^ 3, half),
    )
    copies = []
    for piece, start, count, at, first in parts:
        lanes = pl.ds(pl.multiple_of(at * LANES, LANES), LANES)
        copies.append(
            pltpu.make_async_copy(
                piece.at[pl.ds(start, count)], out.at[pl.ds(first, count), lanes],
                sems.at[len(copies)],
            )
        )
    for copy in copies:
        copy.start()
    for copy in copies:
        copy.wait()


def assemble(*pieces):
    rows = pieces[0].shape[0]
    return pl.pallas_call(
        assemble_kernel,
        out_shape=jax.ShapeDtypeStruct((rows, 4 * LANES), BF16),
        in_specs=[ANY] * 5,
        out_specs=VMEM,
        scratch_shapes=[pltpu.SemaphoreType.DMA((5,))],
        compiler_params=pltpu.CompilerParams(vmem_limit_bytes=8 * MIB),
        cost_estimate=pl.CostEstimate(flops=0, bytes_accessed=3 * MIB, transcendentals=0),
        name="assemble",
    )(*pieces)


def ring_slot(block):
    z = lax.axis_index("ao")
    return ((z ^ (z >> 1)) - (block ^ (block >> 1))) & 3


def column_block(which, blocks):
    first = lax.axis_index("vir") * blocks
    early, late = ring_slot(first), ring_slot(first + 1)
    swapped = jnp.where(early < late, 0, 1)
    return first + (swapped ^ which)


def pick(slot, first, refs, target):
    for s, ref in enumerate(refs):

        def copy(ref=ref):
            target[...] = ref[...]

        if len(refs) == 1:
            copy()
        else:
            pl.when(slot == first + s)(copy)


def first_kernel(n_own, n_shifted, n_late, which, blocks, *refs):
    plan = refs[0]
    shifted = list(refs[1 : 1 + n_shifted])
    late = refs[1 + n_shifted : 1 + n_shifted + n_late]
    refs = refs[1 + n_shifted + n_late :]
    own, other = refs[:n_own], refs[n_own : 2 * n_own]
    out = refs[2 * n_own]
    refs = refs[2 * n_own + 1 :]
    if n_late:
        late_shifted, held, total, late_held, sems = refs
        copies = tile_copies(late, late_held, sems)
        for copy in copies:
            copy.start()
    else:
        held, total = refs
    slot = ring_slot(column_block(which, blocks)) if n_own > 1 else 0
    pick(slot, which, own, held.at[0])
    pick(slot, which, other, held.at[1])
    total[...] = jnp.zeros_like(total)
    if n_late:
        for copy in copies:
            copy.wait()
        shift_loop(plan, sum(t.shape[0] for t in shifted), late_held, late_shifted)
        shifted.append(late_shifted)
    before = 0
    for tiles in shifted:

        def add(i, carry, before=before, tiles=tiles):
            sums = []
            for u in range(UNROLL):
                n = i * UNROLL + u
                base_k = pl.multiple_of(plan[1, before + n], LANES)
                window = held[plan[2, before + n], pl.ds(base_k, COLS_WIN), :]
                sums.append((n, jnp.dot(tiles[n], window, preferred_element_type=F32)))
            for n, value in sums:
                base_m = pl.multiple_of(plan[0, before + n], 16)
                total[pl.ds(base_m, ROWS_WIN), :] += value
            return carry

        lax.fori_loop(0, tiles.shape[0] // UNROLL, add, 0)
        before += tiles.shape[0]
    out[...] = total[: out.shape[0], :].astype(BF16)


def first_product(plan, shifted, late, own, other, which, blocks):
    rows, width = own[0].shape
    n_tiles = plan.shape[1]
    n_late = sum(t.shape[0] for t in late)
    out_shape = [jax.ShapeDtypeStruct((rows, width), BF16)]
    scratch = [
        pltpu.VMEM((2, rows, width), BF16),
        pltpu.VMEM((rows + TILE, width), F32),
    ]
    if late:
        out_shape.append(jax.ShapeDtypeStruct((n_late, ROWS_WIN, COLS_WIN), BF16))
        scratch += [
            pltpu.VMEM((n_late, TILE, TILE), BF16),
            pltpu.SemaphoreType.DMA((len(late),)),
        ]
    result = pl.pallas_call(
        functools.partial(first_kernel, len(own), len(shifted), len(late), which, blocks),
        out_shape=out_shape,
        in_specs=[SMEM] + [VMEM] * len(shifted) + [ANY] * len(late) + [VMEM] * (2 * len(own)),
        out_specs=[VMEM] * len(out_shape),
        scratch_shapes=scratch,
        compiler_params=pltpu.CompilerParams(vmem_limit_bytes=14 * MIB),
        cost_estimate=pl.CostEstimate(
            flops=n_tiles * 4 * ROWS_WIN * COLS_WIN * width, bytes_accessed=6 * MIB,
            transcendentals=0,
        ),
        name="first_product",
    )(plan, *shifted, *late, *own, *other)
    return result[0], [*shifted, *result[1:]]


def second_kernel(which, blocks, n_groups, n_before, *refs):
    by_col, by_row, middle, middle_other = refs[:4]
    core = lax.axis_index("rep")
    mine = GROUPS // 2
    if n_groups:
        own, other = refs[4 : 4 + GROUPS], refs[4 + GROUPS : 4 + 2 * GROUPS]
        out, held, ready, out_sems = refs[4 + 2 * GROUPS + n_before :]
        for i in range(mine):
            wanted = core * mine + i
            slot = ring_slot(wanted) if blocks > 1 else wanted
            pick(slot, 0, own, held.at[i, 0])
            pick(slot, 0, other, held.at[i, 1])
    else:
        held = refs[4]
        out, ready, out_sems = refs[5 + n_before :]
    width = held.shape[3]
    columns = middle.shape[1]
    if blocks > 1:
        block = column_block(which, blocks) - lax.axis_index("vir") * blocks
        column = pl.multiple_of(block * columns, LANES)
    else:
        column = 0
    dims = (((0,), (0,)), ((), ()))
    stores = []
    for i in range(mine):
        total = lax.dot_general(held[i, 0], middle[...], dims, preferred_element_type=F32)
        total += lax.dot_general(held[i, 1], middle_other[...], dims, preferred_element_type=F32)
        tall = by_row[i * width : (i + 1) * width, :]
        tall = jnp.concatenate([tall] * (columns // LANES), axis=1)
        ready[i] = (total / (by_col[:, pl.ds(column, columns)] - tall)).astype(BF16)
        store = pltpu.make_async_copy(
            ready.at[i], out.at[0, pl.ds(i * width, width), pl.ds(column, columns)], out_sems.at[i]
        )
        store.start()
        stores.append(store)
    for store in stores:
        store.wait()


def second_product(which, blocks, energies, middle, groups, held, before):
    rows, columns = middle[0].shape
    mine = GROUPS // 2
    width = energies[1].shape[0] // mine
    extra = [] if before is None else [before]
    fixed = [*energies, *middle, *(groups if held is None else [held])]
    out_shape = [jax.ShapeDtypeStruct((1, mine * width, blocks * columns), BF16)]
    out_specs = [ANY]
    if held is None:
        out_shape.append(jax.ShapeDtypeStruct((mine, 2, rows, width), BF16))
        out_specs.append(VMEM)
    result = pl.pallas_call(
        functools.partial(
            second_kernel, which, blocks, len(groups) if held is None else 0, len(extra)
        ),
        out_shape=out_shape,
        in_specs=[VMEM] * len(fixed) + [ANY] * len(extra),
        out_specs=out_specs,
        scratch_shapes=[
            pltpu.VMEM((mine, width, columns), BF16),
            pltpu.SemaphoreType.DMA((mine,)),
        ],
        input_output_aliases={len(fixed): 0} if extra else {},
        compiler_params=pltpu.CompilerParams(vmem_limit_bytes=16 * MIB),
        cost_estimate=pl.CostEstimate(
            flops=4 * mine * rows * width * columns, bytes_accessed=10 * MIB, transcendentals=0
        ),
        name="second_product",
    )(*fixed, *extra)
    return (result[0], result[1] if held is None else held)


def ring_pairs(distance):
    return [(RING[i], RING[(i + distance) % 4]) for i in range(4)]


def other_core(value):
    return lax.ppermute(value, "rep", SWAP)


def to_x(value):
    return lax.ppermute(value, "vir", SWAP)


def to_y(value):
    return lax.ppermute(value, "grp", SWAP)


def to_z(value, distance=1):
    return lax.ppermute(value, "ao", ring_pairs(distance))


def exchange_small(half_ints, coeff, plan, shift):
    z, x, y = lax.axis_index("ao"), lax.axis_index("vir"), lax.axis_index("grp")
    quarter = y * 2 + x
    gray = lambda n: n ^ (n >> 1)
    owner = [gray((gray(z) + k) & 3) for k in range(4)]
    rows = coeff.shape[0]
    half = rows // 2
    together = lax.optimization_barrier
    join = lambda a, b: jnp.concatenate([a, b], axis=0)

    own = lax.dynamic_slice_in_dim(coeff, quarter * LANES, LANES, 1)
    t = [
        lax.dynamic_index_in_dim(half_ints[:, 0], owner[k], 0, False) for k in range(4)
    ]
    z1, t, group0 = together((to_z(own), t, stay(coeff)))
    x1, y1, z2, t, plan = together((to_x(z1), to_y(z1), to_z(z1), t, plan))
    x2, y2, z3, t1, t = together(
        (to_x(join(z2, y1[:half])), to_y(join(z2, x1[half:])), to_z(z2), to_z(t[1], 1), t)
    )
    group1 = assemble(z1, x1, y1, x2, y2)
    early = shift(plan, 0, [t[0], t1])
    early, last = together((early, t[2]))
    t2, t3 = to_z(last, 2), to_z(t[3], 3)
    x3, y3, group1, early = together(
        (to_x(join(z3, y2[:half])), to_y(join(z3, x2[half:rows])), group1, early)
    )
    group2 = assemble(z2, x2, y2, x3, y3)
    late = shift(plan, 2 * t2.shape[0], [t2, t3])
    x4, y4, late = together((to_x(y3[:half]), to_y(x3[half:rows]), late))
    group3 = assemble(z3, x3, y3, x4, y4)
    return [group0, group1, group2, group3], [early, late], [], plan


def exchange_any(half_ints, coeff):
    count = lax.axis_size("ao")
    gathered = lax.all_gather(coeff, "ao", axis=1, tiled=True)
    width = gathered.shape[1] // GROUPS
    tiles = lax.all_to_all(half_ints, "ao", split_axis=0, concat_axis=2, tiled=True)[0, 0]
    groups = [gathered[:, g * width : (g + 1) * width] for g in range(GROUPS)]
    return gathered, groups, tiles


def local(half_ints, coeff, eps_occ, eps_vir, pair_occ, tile_list, shell_extra):
    sizes = tuple(lax.axis_size(name) for name in ("grp", "ao", "vir"))
    rows, width = coeff.shape
    full_width = width * sizes[1]
    b_width = full_width // sizes[2]
    vir = lax.axis_index("vir")
    ringed = sizes == (2, 4, 2) and width == 4 * LANES
    plan, *energies = make_plan(
        tuple(range(4)) if ringed else (None,), tile_list, shell_extra, pair_occ, eps_occ,
        eps_vir.reshape(1, -1), rows, full_width // lax.axis_size("rep"), b_width,
    )
    if ringed:
        groups, shifted, late, plan = exchange_small(half_ints, coeff, plan, shift_tiles)
        own, blocks = groups, b_width // width
    else:
        gathered, groups, tiles = exchange_any(half_ints, coeff)
        own, blocks = [lax.dynamic_slice_in_dim(gathered, vir * b_width, b_width, 1)], 1
        shifted, late = [shift_tiles(plan, 0, [tiles])], []
    others = [other_core(g) for g in groups]
    other = others if ringed else [other_core(own[0])]
    out = held = None
    for which in range(blocks):
        some = slice(which, GROUPS - 1 + which) if ringed else slice(None)
        middle, shifted = first_product(
            plan, shifted, late, own[some], other[some], which, blocks
        )
        middle, shifted = lax.optimization_barrier((middle, shifted))
        late = []
        both = (middle, other_core(middle))
        out, held = second_product(
            which, blocks, energies, both, [*groups, *others], held, out
        )
    return out


def solution(mesh):
    in_specs = (
        P("grp", "rep", "ao", None, None),
        P("rep", "ao"),
        P(),
        P(),
        P(("grp", "ao"), None),
        P("rep", None, None),
        P(),
    )
    out_specs = P(("grp", "ao"), "rep", "vir")
    return jax.shard_map(local, mesh=mesh, in_specs=in_specs, out_specs=out_specs, check_vma=False)
```

time: 80.7 us -> 74 us (0.917)
  waiting for transfers between devices: 20 us -> 14.1 us
  starting transfers between devices: 27.5 us -> 32 us
  Pallas kernels: 25.4 us -> 22.2 us
  other arithmetic: 1.08 us -> 0.13 us
    ppermute x6, starting transfers between devices: 8.6 us -> 12.9 us  [other_core(): return lax.ppermute(value, 'rep', SWAP)]
    ppermute x6, waiting for transfers between devices: 3.19 us -> 0.02 us  [other_core(): return lax.ppermute(value, 'rep', SWAP)]
    pallas_call x6 -> x8, Pallas kernels: 24.5 us -> 21.4 us  [the longest x2 7.99 us: second_product(): pl.pallas_call(functools.partial(second_kernel, which, blocks, len(groups...]
    squeeze x1, local copies, waits for them, and re-layouts: 2.05 us -> 0.8 us  [exchange_small(): lax.dynamic_index_in_dim(half_ints[:, 0], owner[k], 0, False)]
    ppermute x6, waiting for transfers between devices: 13.8 us -> 12.6 us  [to_z(): return lax.ppermute(value, 'ao', ring_pairs(distance))]
    ppermute x4, waiting for transfers between devices: 2.11 us -> 1.01 us  [to_x(): return lax.ppermute(value, 'vir', SWAP)]
    concatenate x2, other arithmetic: 1.08 us -> 0.13 us  [exchange_small(): join = lambda a, b: jnp.concatenate([a, b], axis=0)]
    unnamed x21 -> x19, local copies, waits for them, and re-layouts: 1.71 us -> 2.4 us
  transfers between devices with their start and end apart: 20 -> 20, of which waited for: 7 -> 6; matrix products, arithmetic and copies ran while one was open for 3% -> 1% of each run, Pallas kernels for 21% -> 25%
where the time goes in v4:
time: 74 us; the launch traced here: 73.2 us
  starting transfers between devices  32 us (43%)
  Pallas kernels  22.2 us (30%)
  waiting for transfers between devices  14.1 us (19%)
  local copies, waits for them, and re-layouts  4.27 us (6%)
    ppermute x6, starting transfers between devices, to_z(): return lax.ppermute(value, 'ao', ring_pairs(distance))  12.9 us
    ppermute x6, starting transfers between devices, other_core(): return lax.ppermute(value, 'rep', SWAP)  12.9 us
    ppermute x6, waiting for transfers between devices, to_z(): return lax.ppermute(value, 'ao', ring_pairs(distance))  12.6 us
    pallas_call x2, Pallas kernels, second_product(): pl.pallas_call(functools.partial(second_kernel, which, blocks, len(groups...  7.99 us
    pallas_call x2, Pallas kernels, first_product(): pl.pallas_call(functools.partial(first_kernel, len(own), len(shifted), le...  5.53 us
    pallas_call x2, Pallas kernels, shift_tiles(): pl.pallas_call(functools.partial(shift_kernel, first, len(tiles)), out_sh...  5.03 us
    ppermute x4, starting transfers between devices, to_x(): return lax.ppermute(value, 'vir', SWAP)  3.13 us
    ppermute x4, starting transfers between devices, to_y(): return lax.ppermute(value, 'grp', SWAP)  3.09 us
  transfers between devices with their start and end apart: 20, of which 6 were waited for; matrix products, arithmetic and copies ran while one was open for 1% of the time, Pallas kernels for 25%

profile of v4, /device:TPU:9, one launch (start us, length us, event | category | flops | bytes accessed | tf_op | source)
XLA Modules:
  0.0 73.2 jit_solution(14870044278283744984)
XLA Ops:
  0.0 1.0 %constant_dynamic-slice_fusion = bf16[1280,128]{1,0:T(8,128)(2,1)S(1)} fusion(bf16[1280,512]{1,0:T(8,128)(2,1)} %value.1, s32[]{:T(128)S(6)} %select_n.16), kind=kLoop, calls=%fused_computation.8 | loop fusion | bytes 655364 | tf_op jit(solution)/shard_map/dynamic_slice | solution.py:409
  1.0 2.4 %collective-permute-start = (bf16[1280,128]{1,0:T(8,128)(2,1)S(1)}, bf16[1280,128]{1,0:T(8,128)(2,1)S(1)}, u32[]{:S(2)}, u32[]{:S(2)}) collective-permute-start(bf16[1280,128]{1,0:T(8,128)(2,1)S(1)} %constant_dynamic-slice_fusion), channel_id=1, source_target_pairs={{0,4},{4,12},{12,8},{8,0},{1,5},{5,13},{13,9},{9,1},{2,6},{6,14},{... | collective-permute-start | bytes 983048 | tf_op jit(solution)/shard_map/ppermute | solution.py:396
  3.4 1.3 %copy-done = bf16[1280,512]{1,0:T(8,128)(2,1)S(1)} copy-done((bf16[1280,512]{1,0:T(8,128)(2,1)S(1)}, bf16[1280,512]{1,0:T(8,128)(2,1)}, u32[]{:S(2)}) %copy-start) | copy-done | bytes 1310744
  4.8 1.0 %copy-done.5 = bf16[4,1,6,128,128]{4,3,2,1,0:T(8,128)(2,1)S(1)} copy-done((bf16[4,1,6,128,128]{4,3,2,1,0:T(8,128)(2,1)S(1)}, bf16[4,1,6,128,128]{4,3,2,1,0:T(8,128)(2,1)}, u32[]{:S(2)}) %copy-start.5) | copy-done | bytes 786456
  5.8 0.8 %dynamic-slice_bitcast_fusion = (bf16[6,128,128]{2,1,0:T(8,128)(2,1)S(1)}, bf16[6,128,128]{2,1,0:T(8,128)(2,1)}, bf16[6,128,128]{2,1,0:T(8,128)(2,1)S(1)}, bf16[6,128,128]{2,1,0:T(8,128)(2,1)}) fusion(bf16[4,1,6,128,128]{4,3,2,1,0:T(8,128)(2,1)S(1)} %copy-done.5, s32[]{:T(128)S(6)} %select_n.20, s32[]{:T(128)S(6)} %select_n.18, s32[]{:T(128)S(6)} %select_n.17, ...), kind=kLoop, calls=%fused_computation.4 | loop fusion | bytes 1572880 | tf_op jit(solution)/shard_map/jit(dynamic_index_in_dim)/squeeze | solution.py:411
  6.6 3.1 %collective-permute-done.own = bf16[1280,128]{1,0:T(8,128)(2,1)S(1)} collective-permute-done((bf16[1280,128]{1,0:T(8,128)(2,1)S(1)}, bf16[1280,128]{1,0:T(8,128)(2,1)S(1)}, u32[]{:S(2)}, u32[]{:S(2)}) %collective-permute-start) | collective-permute-done | bytes 327712 | tf_op jit(solution)/shard_map/ppermute | solution.py:396
  9.7 1.2 %collective-permute-start.1 = (bf16[1280,128]{1,0:T(8,128)(2,1)S(1)}, bf16[1280,128]{1,0:T(8,128)(2,1)S(1)}, u32[]{:S(2)}, u32[]{:S(2)}) collective-permute-start(bf16[1280,128]{1,0:T(8,128)(2,1)S(1)} %collective-permute-done.own), channel_id=1, source_target_pairs={{0,2},{2,0},{1,3},{3,1},{4,6},{6,4},{5,7},{7,5},{8,10},{10,8},{9,1... | collective-permute-start | bytes 983048 | tf_op jit(solution)/shard_map/ppermute | solution.py:388
  11.0 1.2 %collective-permute-start.2 = (bf16[1280,128]{1,0:T(8,128)(2,1)S(1)}, bf16[1280,128]{1,0:T(8,128)(2,1)S(1)}, u32[]{:S(2)}, u32[]{:S(2)}) collective-permute-start(bf16[1280,128]{1,0:T(8,128)(2,1)S(1)} %collective-permute-done.own), channel_id=1, source_target_pairs={{0,16},{16,0},{1,17},{17,1},{2,18},{18,2},{3,19},{19,3},{4,20},{20... | collective-permute-start | bytes 983048 | tf_op jit(solution)/shard_map/ppermute | solution.py:392
  12.2 3.1 %collective-permute-start.3 = (bf16[1280,128]{1,0:T(8,128)(2,1)S(1)}, bf16[1280,128]{1,0:T(8,128)(2,1)S(1)}, u32[]{:S(2)}, u32[]{:S(2)}) collective-permute-start(bf16[1280,128]{1,0:T(8,128)(2,1)S(1)} %collective-permute-done.own), channel_id=1, source_target_pairs={{0,4},{4,12},{12,8},{8,0},{1,5},{5,13},{13,9},{9,1},{2,6},{6,14},{... | collective-permute-start | bytes 983048 | tf_op jit(solution)/shard_map/ppermute | solution.py:396
  15.4 2.7 %make_plan.1 = (s32[7,24]{1,0:T(8,128)S(1)}, f32[1,1024]{1,0:T(1,128)S(1)}, f32[1024,128]{1,0:T(8,128)S(1)}) custom-call(s32[1,24,2]{2,1,0:T(8,128)S(1)} %copy.9.listed, s32[2,12]{1,0:T(2,128)S(1)} %copy-done.3, s32[1,2]{1,0:T(1,128)S(1)} %copy-done.4, f32[400]{0:T(512)S(1)} %copy-done.2, f32[1,2048]{1,0:T(1,128)S(1)} %bitcast.9), custom_call_target="tpu_custom_call" | custom-call | bytes 2097152 | tf_op jit(solution)/shard_map/make_plan/pallas_call | solution.py:77
  18.3 1.9 %collective-permute-done.3.own = bf16[1280,128]{1,0:T(8,128)(2,1)S(1)} collective-permute-done((bf16[1280,128]{1,0:T(8,128)(2,1)S(1)}, bf16[1280,128]{1,0:T(8,128)(2,1)S(1)}, u32[]{:S(2)}, u32[]{:S(2)}) %collective-permute-start.3) | collective-permute-done | bytes 327712 | tf_op jit(solution)/shard_map/ppermute | solution.py:396
  20.3 0.3 collective-permute-start.4
  20.8 3.1 %collective-permute-start.6 = (bf16[1280,128]{1,0:T(8,128)(2,1)S(1)}, bf16[1280,128]{1,0:T(8,128)(2,1)S(1)}, u32[]{:S(2)}, u32[]{:S(2)}) collective-permute-start(bf16[1280,128]{1,0:T(8,128)(2,1)S(1)} %collective-permute-done.3.own), channel_id=1, source_target_pairs={{0,4},{4,12},{12,8},{8,0},{1,5},{5,13},{13,9},{9,1},{2,6},{6,14},{... | collective-permute-start | bytes 983048 | tf_op jit(solution)/shard_map/ppermute | solution.py:396
  24.0 7.6 %collective-permute-done.7.refs_2_ = bf16[6,128,128]{2,1,0:T(8,128)(2,1)S(1)} collective-permute-done((bf16[6,128,128]{2,1,0:T(8,128)(2,1)S(1)}, bf16[6,128,128]{2,1,0:T(8,128)(2,1)S(1)}, u32[]{:S(2)}, u32[]{:S(2)}) %collective-permute-start.7) | collective-permute-done | bytes 196640 | tf_op jit(solution)/shard_map/ppermute | solution.py:396
  31.7 1.3 %collective-permute-start.8 = (bf16[1920,128]{1,0:T(8,128)(2,1)S(1)}, bf16[1920,128]{1,0:T(8,128)(2,1)S(1)}, u32[]{:S(2)}, u32[]{:S(2)}) collective-permute-start(bf16[1920,128]{1,0:T(8,128)(2,1)S(1)} %get-tuple-element.88), channel_id=1, source_target_pairs={{0,2},{2,0},{1,3},{3,1},{4,6},{6,4},{5,7},{7,5},{8,10},{10,8},{9,1... | collective-permute-start | bytes 1474568 | tf_op jit(solution)/shard_map/ppermute | solution.py:388
  33.0 1.2 %collective-permute-start.9 = (bf16[1920,128]{1,0:T(8,128)(2,1)S(1)}, bf16[1920,128]{1,0:T(8,128)(2,1)S(1)}, u32[]{:S(2)}, u32[]{:S(2)}) collective-permute-start(bf16[1920,128]{1,0:T(8,128)(2,1)S(1)} %get-tuple-element.87), channel_id=1, source_target_pairs={{0,16},{16,0},{1,17},{17,1},{2,18},{18,2},{3,19},{19,3},{4,20},{20... | collective-permute-start | bytes 1474568 | tf_op jit(solution)/shard_map/ppermute | solution.py:392
  34.2 2.5 %shift_tiles.2.refs_1_ = bf16[12,144,256]{2,1,0:T(8,128)(2,1)S(1)} custom-call(s32[7,24]{1,0:T(8,128)S(1)} %get-tuple-element.52.refs_0_, bf16[6,128,128]{2,1,0:T(8,128)(2,1)S(1)} %get-tuple-element.63.refs_1_, bf16[6,128,128]{2,1,0:T(8,128)(2,1)S(1)} %collective-permute-done.7.refs_2_), custom_call_target="tpu_custom_call" | custom-call | bytes 8388608 | tf_op jit(solution)/shard_map/shift_tiles/pallas_call | solution.py:138
  36.8 1.4 %collective-permute-start.12 = (bf16[6,128,128]{2,1,0:T(8,128)(2,1)S(1)}, bf16[6,128,128]{2,1,0:T(8,128)(2,1)S(1)}, u32[]{:S(2)}, u32[]{:S(2)}) collective-permute-start(bf16[6,128,128]{2,1,0:T(8,128)(2,1)S(1)} %copy-done.6), channel_id=1, source_target_pairs={{0,12},{4,8},{12,0},{8,4},{1,13},{5,9},{13,1},{9,5},{2,14},{6,10},... | collective-permute-start | bytes 589832 | tf_op jit(solution)/shard_map/ppermute | solution.py:396
  38.1 3.0 %collective-permute-start.13 = (bf16[6,128,128]{2,1,0:T(8,128)(2,1)S(1)}, bf16[6,128,128]{2,1,0:T(8,128)(2,1)S(1)}, u32[]{:S(2)}, u32[]{:S(2)}) collective-permute-start(bf16[6,128,128]{2,1,0:T(8,128)(2,1)S(1)} %get-tuple-element.71), channel_id=1, source_target_pairs={{0,8},{4,0},{12,4},{8,12},{1,9},{5,1},{13,5},{9,13},{2,10},{6,2},{... | collective-permute-start | bytes 589832 | tf_op jit(solution)/shard_map/ppermute | solution.py:396
  41.1 5.6 %collective-permute-start.14 = (bf16[1280,512]{1,0:T(8,128)(2,1)S(1)}, bf16[1280,512]{1,0:T(8,128)(2,1)S(1)}, u32[]{:S(2)}, u32[]{:S(2)}) collective-permute-start(bf16[1280,512]{1,0:T(8,128)(2,1)S(1)} %stay.1.refs_3_.refs_4_), channel_id=1, source_target_pairs={{0,1},{1,0},{2,3},{3,2},{4,5},{5,4},{6,7},{7,6},{8,9},{9,8},{10,11... | collective-permute-start | bytes 3932168 | tf_op jit(solution)/shard_map/ppermute | solution.py:384
  47.1 0.3 assemble.4.refs_5_.refs_4_.refs_6_
  47.4 0.5 collective-permute-start.15
  48.0 0.3 collective-permute-start.10
  48.3 0.4 collective-permute-start.11
  48.7 2.5 %shift_tiles.3.refs_2_ = bf16[12,144,256]{2,1,0:T(8,128)(2,1)S(1)} custom-call(s32[7,24]{1,0:T(8,128)S(1)} %get-tuple-element.52.refs_0_, bf16[6,128,128]{2,1,0:T(8,128)(2,1)S(1)} %collective-permute-done.12.refs_1_, bf16[6,128,128]{2,1,0:T(8,128)(2,1)S(1)} %collective-permute-done.13.refs_2_), custom_call_target="tpu_custom_call" | custom-call | bytes 8388608 | tf_op jit(solution)/shard_map/shift_tiles/pallas_call | solution.py:138
  51.2 1.0 %collective-permute-done.10.far_x = bf16[640,128]{1,0:T(8,128)(2,1)S(1)} collective-permute-done((bf16[640,128]{1,0:T(8,128)(2,1)S(1)}, bf16[640,128]{1,0:T(8,128)(2,1)S(1)}, u32[]{:S(2)}, u32[]{:S(2)}) %collective-permute-start.10) | collective-permute-done | bytes 163872 | tf_op jit(solution)/shard_map/ppermute | solution.py:388
  52.8 6.0 %collective-permute-start.17 = (bf16[1280,512]{1,0:T(8,128)(2,1)S(1)}, bf16[1280,512]{1,0:T(8,128)(2,1)S(1)}, u32[]{:S(2)}, u32[]{:S(2)}) collective-permute-start(bf16[1280,512]{1,0:T(8,128)(2,1)S(1)} %assemble.5.refs_5_.refs_7_), channel_id=1, source_target_pairs={{0,1},{1,0},{2,3},{3,2},{4,5},{5,4},{6,7},{7,6},{8,9},{9,8},{10,11... | collective-permute-start | bytes 3932168 | tf_op jit(solution)/shard_map/ppermute | solution.py:384
  58.8 2.8 %first_product.2.refs_2_ = bf16[1280,512]{1,0:T(8,128)(2,1)S(1)} custom-call(s32[7,24]{1,0:T(8,128)S(1)} %get-tuple-element.52.refs_0_, bf16[12,144,256]{2,1,0:T(8,128)(2,1)S(1)} %shift_tiles.2.refs_1_, bf16[12,144,256]{2,1,0:T(8,128)(2,1)S(1)} %shift_tiles.3.refs_2_, bf16[1280,512]{1,0:T(8,128)(2,1)S(1)} %stay.1.refs_3_.refs_4_, ...), custom_call_target="tpu_custom_call" | custom-call | flops 1811939328 | bytes 6291456 | tf_op jit(solution)/shard_map/first_product/pallas_call | solution.py:292
  61.7 2.8 %first_product.3.refs_2_ = bf16[1280,512]{1,0:T(8,128)(2,1)S(1)} custom-call(s32[7,24]{1,0:T(8,128)S(1)} %get-tuple-element.52.refs_0_, bf16[12,144,256]{2,1,0:T(8,128)(2,1)S(1)} %shift_tiles.2.refs_1_, bf16[12,144,256]{2,1,0:T(8,128)(2,1)S(1)} %shift_tiles.3.refs_2_, bf16[1280,512]{1,0:T(8,128)(2,1)S(1)} %assemble.3.refs_4_.refs_3_.refs_5_, ...), custom_call_target="tpu_custom_call" | custom-call | flops 1811939328 | bytes 6291456 | tf_op jit(solution)/shard_map/first_product/pallas_call | solution.py:292
  64.5 0.5 collective-permute-start.18
  65.0 4.3 %second_product.2 = (bf16[1,1024,1024]{2,1,0:T(8,128)(2,1)}, bf16[2,2,1280,512]{3,2,1,0:T(8,128)(2,1)S(1)}) custom-call(f32[1,1024]{1,0:T(1,128)S(1)} %get-tuple-element.44.refs_0_, f32[1024,128]{1,0:T(8,128)S(1)} %get-tuple-element.45.refs_1_, bf16[1280,512]{1,0:T(8,128)(2,1)S(1)} %first_product.2.refs_2_, ...), custom_call_target="tpu_custom_call" | custom-call | flops 2684354560 | bytes 10485760 | tf_op jit(solution)/shard_map/second_product/pallas_call | solution.py:358
  69.3 3.7 %second_product.3 = bf16[1,1024,1024]{2,1,0:T(8,128)(2,1)} custom-call(f32[1,1024]{1,0:T(1,128)S(1)} %get-tuple-element.44.refs_0_, f32[1024,128]{1,0:T(8,128)S(1)} %get-tuple-element.45.refs_1_, bf16[1280,512]{1,0:T(8,128)(2,1)S(1)} %first_product.3.refs_2_, bf16[1280,512]{1,0:T(8,128)(2,1)S(1)} %collective-permute-done.18.refs_3_, ...), custom_call_target="tpu_custom_call", output_to_operand_aliasing={{}: (5, {})} | custom-call | flops 2684354560 | bytes 10485760 | tf_op jit(solution)/shard_map/second_product/pallas_call | solution.py:358
  (48 shorter events, 1.9 us)
Async XLA Ops:
  1.0 8.7 %collective-permute-start = (bf16[1280,128]{1,0:T(8,128)(2,1)S(1)}, bf16[1280,128]{1,0:T(8,128)(2,1)S(1)}, u32[]{:S(2)}, u32[]{:S(2)}) collective-permute-start(bf16[1280,128]{1,0:T(8,128)(2,1)S(1)} %constant_dynamic-slice_fusion), channel_id=1, source_target_pairs={{0,4},{4,12},{12,8},{8,0},{1,5},{5,13},{13,9},{9,1},{2,6},{6,14},{... | collective-permute-start | bytes 983048 | tf_op jit(solution)/shard_map/ppermute | solution.py:396
  3.4 1.3 %copy-start = (bf16[1280,512]{1,0:T(8,128)(2,1)S(1)}, bf16[1280,512]{1,0:T(8,128)(2,1)}, u32[]{:S(2)}) copy-start(bf16[1280,512]{1,0:T(8,128)(2,1)} %value.1) | copy-start | bytes 3932164
  4.7 1.1 %copy-start.5 = (bf16[4,1,6,128,128]{4,3,2,1,0:T(8,128)(2,1)S(1)}, bf16[4,1,6,128,128]{4,3,2,1,0:T(8,128)(2,1)}, u32[]{:S(2)}) copy-start(bf16[4,1,6,128,128]{4,3,2,1,0:T(8,128)(2,1)} %param.7) | copy-start | bytes 2359300
  4.8 10.5 %copy-start.8 = (s32[1,24,2]{1,2,0:T(2,128)S(1)}, s32[1,24,2]{1,2,0:T(2,128)}, u32[]{:S(2)}) copy-start(s32[1,24,2]{1,2,0:T(2,128)} %param.12) | copy-start | bytes 580
  4.8 10.6 %copy-start.1 = (f32[2048]{0:T(1024)S(1)}, f32[2048]{0:T(1024)}, u32[]{:S(2)}) copy-start(f32[2048]{0:T(1024)} %param.10) | copy-start | bytes 24580
  4.8 10.6 %copy-start.2 = (f32[400]{0:T(512)S(1)}, f32[400]{0:T(512)}, u32[]{:S(2)}) copy-start(f32[400]{0:T(512)} %eps_occ.1) | copy-start | bytes 4804
  4.8 10.6 %copy-start.3 = (s32[2,12]{1,0:T(2,128)S(1)}, s32[2,12]{1,0:T(2,128)}, u32[]{:S(2)}) copy-start(s32[2,12]{1,0:T(2,128)} %extra.1) | copy-start | bytes 292
  4.8 10.6 %copy-start.4 = (s32[1,2]{1,0:T(1,128)S(1)}, s32[1,2]{1,0:T(1,128)}, u32[]{:S(2)}) copy-start(s32[1,2]{1,0:T(1,128)} %pair_occ.1) | copy-start | bytes 28
  9.7 14.2 %copy-start.7 = (bf16[6,128,128]{2,1,0:T(8,128)(2,1)S(1)}, bf16[6,128,128]{2,1,0:T(8,128)(2,1)}, u32[]{:S(2)}) copy-start(bf16[6,128,128]{2,1,0:T(8,128)(2,1)} %get-tuple-element.56) | copy-start | bytes 589828
  9.7 8.4 %collective-permute-start.1 = (bf16[1280,128]{1,0:T(8,128)(2,1)S(1)}, bf16[1280,128]{1,0:T(8,128)(2,1)S(1)}, u32[]{:S(2)}, u32[]{:S(2)}) collective-permute-start(bf16[1280,128]{1,0:T(8,128)(2,1)S(1)} %collective-permute-done.own), channel_id=1, source_target_pairs={{0,2},{2,0},{1,3},{3,1},{4,6},{6,4},{5,7},{7,5},{8,10},{10,8},{9,1... | collective-permute-start | bytes 983048 | tf_op jit(solution)/shard_map/ppermute | solution.py:388
  11.0 7.4 %collective-permute-start.2 = (bf16[1280,128]{1,0:T(8,128)(2,1)S(1)}, bf16[1280,128]{1,0:T(8,128)(2,1)S(1)}, u32[]{:S(2)}, u32[]{:S(2)}) collective-permute-start(bf16[1280,128]{1,0:T(8,128)(2,1)S(1)} %collective-permute-done.own), channel_id=1, source_target_pairs={{0,16},{16,0},{1,17},{17,1},{2,18},{18,2},{3,19},{19,3},{4,20},{20... | collective-permute-start | bytes 983048 | tf_op jit(solution)/shard_map/ppermute | solution.py:392
  12.2 8.0 %collective-permute-start.3 = (bf16[1280,128]{1,0:T(8,128)(2,1)S(1)}, bf16[1280,128]{1,0:T(8,128)(2,1)S(1)}, u32[]{:S(2)}, u32[]{:S(2)}) collective-permute-start(bf16[1280,128]{1,0:T(8,128)(2,1)S(1)} %collective-permute-done.own), channel_id=1, source_target_pairs={{0,4},{4,12},{12,8},{8,0},{1,5},{5,13},{13,9},{9,1},{2,6},{6,14},{... | collective-permute-start | bytes 983048 | tf_op jit(solution)/shard_map/ppermute | solution.py:396
  20.3 11.3 %collective-permute-start.4 = (bf16[1920,128]{1,0:T(8,128)(2,1)S(1)}, bf16[1920,128]{1,0:T(8,128)(2,1)S(1)}, u32[]{:S(2)}, u32[]{:S(2)}) collective-permute-start(bf16[1920,128]{1,0:T(8,128)(2,1)S(1)} %get-tuple-element.90), channel_id=1, source_target_pairs={{0,2},{2,0},{1,3},{3,1},{4,6},{6,4},{5,7},{7,5},{8,10},{10,8},{9,1... | collective-permute-start | bytes 1474568 | tf_op jit(solution)/shard_map/ppermute | solution.py:388
  20.6 11.0 %collective-permute-start.5 = (bf16[1920,128]{1,0:T(8,128)(2,1)S(1)}, bf16[1920,128]{1,0:T(8,128)(2,1)S(1)}, u32[]{:S(2)}, u32[]{:S(2)}) collective-permute-start(bf16[1920,128]{1,0:T(8,128)(2,1)S(1)} %get-tuple-element.89), channel_id=1, source_target_pairs={{0,16},{16,0},{1,17},{17,1},{2,18},{18,2},{3,19},{19,3},{4,20},{20... | collective-permute-start | bytes 1474568 | tf_op jit(solution)/shard_map/ppermute | solution.py:392
  20.8 10.7 %collective-permute-start.6 = (bf16[1280,128]{1,0:T(8,128)(2,1)S(1)}, bf16[1280,128]{1,0:T(8,128)(2,1)S(1)}, u32[]{:S(2)}, u32[]{:S(2)}) collective-permute-start(bf16[1280,128]{1,0:T(8,128)(2,1)S(1)} %collective-permute-done.3.own), channel_id=1, source_target_pairs={{0,4},{4,12},{12,8},{8,0},{1,5},{5,13},{13,9},{9,1},{2,6},{6,14},{... | collective-permute-start | bytes 983048 | tf_op jit(solution)/shard_map/ppermute | solution.py:396
  23.9 7.6 %collective-permute-start.7 = (bf16[6,128,128]{2,1,0:T(8,128)(2,1)S(1)}, bf16[6,128,128]{2,1,0:T(8,128)(2,1)S(1)}, u32[]{:S(2)}, u32[]{:S(2)}) collective-permute-start(bf16[6,128,128]{2,1,0:T(8,128)(2,1)S(1)} %copy-done.7), channel_id=1, source_target_pairs={{0,4},{4,12},{12,8},{8,0},{1,5},{5,13},{13,9},{9,1},{2,6},{6,14},{... | collective-permute-start | bytes 589832 | tf_op jit(solution)/shard_map/ppermute | solution.py:396
  31.6 5.1 %copy-start.6 = (bf16[6,128,128]{2,1,0:T(8,128)(2,1)S(1)}, bf16[6,128,128]{2,1,0:T(8,128)(2,1)}, u32[]{:S(2)}) copy-start(bf16[6,128,128]{2,1,0:T(8,128)(2,1)} %get-tuple-element.70) | copy-start | bytes 589828
  31.7 15.3 %collective-permute-start.8 = (bf16[1920,128]{1,0:T(8,128)(2,1)S(1)}, bf16[1920,128]{1,0:T(8,128)(2,1)S(1)}, u32[]{:S(2)}, u32[]{:S(2)}) collective-permute-start(bf16[1920,128]{1,0:T(8,128)(2,1)S(1)} %get-tuple-element.88), channel_id=1, source_target_pairs={{0,2},{2,0},{1,3},{3,1},{4,6},{6,4},{5,7},{7,5},{8,10},{10,8},{9,1... | collective-permute-start | bytes 1474568 | tf_op jit(solution)/shard_map/ppermute | solution.py:388
  33.0 14.1 %collective-permute-start.9 = (bf16[1920,128]{1,0:T(8,128)(2,1)S(1)}, bf16[1920,128]{1,0:T(8,128)(2,1)S(1)}, u32[]{:S(2)}, u32[]{:S(2)}) collective-permute-start(bf16[1920,128]{1,0:T(8,128)(2,1)S(1)} %get-tuple-element.87), channel_id=1, source_target_pairs={{0,16},{16,0},{1,17},{17,1},{2,18},{18,2},{3,19},{19,3},{4,20},{20... | collective-permute-start | bytes 1474568 | tf_op jit(solution)/shard_map/ppermute | solution.py:392
  36.8 11.2 %collective-permute-start.12 = (bf16[6,128,128]{2,1,0:T(8,128)(2,1)S(1)}, bf16[6,128,128]{2,1,0:T(8,128)(2,1)S(1)}, u32[]{:S(2)}, u32[]{:S(2)}) collective-permute-start(bf16[6,128,128]{2,1,0:T(8,128)(2,1)S(1)} %copy-done.6), channel_id=1, source_target_pairs={{0,12},{4,8},{12,0},{8,4},{1,13},{5,9},{13,1},{9,5},{2,14},{6,10},... | collective-permute-start | bytes 589832 | tf_op jit(solution)/shard_map/ppermute | solution.py:396
  38.1 10.2 %collective-permute-start.13 = (bf16[6,128,128]{2,1,0:T(8,128)(2,1)S(1)}, bf16[6,128,128]{2,1,0:T(8,128)(2,1)S(1)}, u32[]{:S(2)}, u32[]{:S(2)}) collective-permute-start(bf16[6,128,128]{2,1,0:T(8,128)(2,1)S(1)} %get-tuple-element.71), channel_id=1, source_target_pairs={{0,8},{4,0},{12,4},{8,12},{1,9},{5,1},{13,5},{9,13},{2,10},{6,2},{... | collective-permute-start | bytes 589832 | tf_op jit(solution)/shard_map/ppermute | solution.py:396
  41.1 17.7 %collective-permute-start.14 = (bf16[1280,512]{1,0:T(8,128)(2,1)S(1)}, bf16[1280,512]{1,0:T(8,128)(2,1)S(1)}, u32[]{:S(2)}, u32[]{:S(2)}) collective-permute-start(bf16[1280,512]{1,0:T(8,128)(2,1)S(1)} %stay.1.refs_3_.refs_4_), channel_id=1, source_target_pairs={{0,1},{1,0},{2,3},{3,2},{4,5},{5,4},{6,7},{7,6},{8,9},{9,8},{10,11... | collective-permute-start | bytes 3932168 | tf_op jit(solution)/shard_map/ppermute | solution.py:384
  47.3 11.4 %collective-permute-start.16 = (bf16[1280,512]{1,0:T(8,128)(2,1)S(1)}, bf16[1280,512]{1,0:T(8,128)(2,1)S(1)}, u32[]{:S(2)}, u32[]{:S(2)}) collective-permute-start(bf16[1280,512]{1,0:T(8,128)(2,1)S(1)} %assemble.4.refs_5_.refs_4_.refs_6_), channel_id=1, source_target_pairs={{0,1},{1,0},{2,3},{3,2},{4,5},{5,4},{6,7},{7,6},{8,9},{9,8},{10,11... | collective-permute-start | bytes 3932168 | tf_op jit(solution)/shard_map/ppermute | solution.py:384
  47.4 11.4 %collective-permute-start.15 = (bf16[1280,512]{1,0:T(8,128)(2,1)S(1)}, bf16[1280,512]{1,0:T(8,128)(2,1)S(1)}, u32[]{:S(2)}, u32[]{:S(2)}) collective-permute-start(bf16[1280,512]{1,0:T(8,128)(2,1)S(1)} %assemble.3.refs_4_.refs_3_.refs_5_), channel_id=1, source_target_pairs={{0,1},{1,0},{2,3},{3,2},{4,5},{5,4},{6,7},{7,6},{8,9},{9,8},{10,11... | collective-permute-start | bytes 3932168 | tf_op jit(solution)/shard_map/ppermute | solution.py:384
  48.0 4.2 %collective-permute-start.10 = (bf16[640,128]{1,0:T(8,128)(2,1)S(1)}, bf16[640,128]{1,0:T(8,128)(2,1)S(1)}, u32[]{:S(2)}, u32[]{:S(2)}) collective-permute-start(bf16[640,128]{1,0:T(8,128)(2,1)S(1)} %slice.22), channel_id=1, source_target_pairs={{0,2},{2,0},{1,3},{3,1},{4,6},{6,4},{5,7},{7,5},{8,10},{10,8},{9,1... | collective-permute-start | bytes 491528 | tf_op jit(solution)/shard_map/ppermute | solution.py:388
  48.3 4.2 %collective-permute-start.11 = (bf16[640,128]{1,0:T(8,128)(2,1)S(1)}, bf16[640,128]{1,0:T(8,128)(2,1)S(1)}, u32[]{:S(2)}, u32[]{:S(2)}) collective-permute-start(bf16[640,128]{1,0:T(8,128)(2,1)S(1)} %slice.23), channel_id=1, source_target_pairs={{0,16},{16,0},{1,17},{17,1},{2,18},{18,2},{3,19},{19,3},{4,20},{20... | collective-permute-start | bytes 491528 | tf_op jit(solution)/shard_map/ppermute | solution.py:392
  52.8 8.9 %collective-permute-start.17 = (bf16[1280,512]{1,0:T(8,128)(2,1)S(1)}, bf16[1280,512]{1,0:T(8,128)(2,1)S(1)}, u32[]{:S(2)}, u32[]{:S(2)}) collective-permute-start(bf16[1280,512]{1,0:T(8,128)(2,1)S(1)} %assemble.5.refs_5_.refs_7_), channel_id=1, source_target_pairs={{0,1},{1,0},{2,3},{3,2},{4,5},{5,4},{6,7},{7,6},{8,9},{9,8},{10,11... | collective-permute-start | bytes 3932168 | tf_op jit(solution)/shard_map/ppermute | solution.py:384
  61.6 3.4 %collective-permute-start.19 = (bf16[1280,512]{1,0:T(8,128)(2,1)S(1)}, bf16[1280,512]{1,0:T(8,128)(2,1)S(1)}, u32[]{:S(2)}, u32[]{:S(2)}) collective-permute-start(bf16[1280,512]{1,0:T(8,128)(2,1)S(1)} %first_product.2.refs_2_), channel_id=1, source_target_pairs={{0,1},{1,0},{2,3},{3,2},{4,5},{5,4},{6,7},{7,6},{8,9},{9,8},{10,11... | collective-permute-start | bytes 3932168 | tf_op jit(solution)/shard_map/ppermute | solution.py:384
  64.5 4.8 %collective-permute-start.18 = (bf16[1280,512]{1,0:T(8,128)(2,1)S(1)}, bf16[1280,512]{1,0:T(8,128)(2,1)S(1)}, u32[]{:S(2)}, u32[]{:S(2)}) collective-permute-start(bf16[1280,512]{1,0:T(8,128)(2,1)S(1)} %first_product.3.refs_2_), channel_id=1, source_target_pairs={{0,1},{1,0},{2,3},{3,2},{4,5},{5,4},{6,7},{7,6},{8,9},{9,8},{10,11... | collective-permute-start | bytes 3932168 | tf_op jit(solution)/shard_map/ppermute | solution.py:384

commit v5 on v4

--- a/solution.py
+++ b/solution.py
@@ -13,8 +13,8 @@
 ROWS_WIN = 144
 COLS_WIN = 256
 GROUPS = 4
-UNROLL = 6
-SHIFT_UNROLL = 3
+UNROLL = 12
+SHIFT_UNROLL = 6
 RING = (0, 1, 3, 2)
 SWAP = ((0, 1), (1, 0))
 F32 = jnp.float32

time: 74 us -> 72.5 us (0.980)
  Pallas kernels: 22.2 us -> 19.9 us
    pallas_call x2, Pallas kernels: 5.03 us -> 3.82 us  [shift_tiles(): pl.pallas_call(functools.partial(shift_kernel, first, len(tiles)), out_sh...]
    pallas_call x2, Pallas kernels: 5.53 us -> 4.4 us  [first_product(): pl.pallas_call(functools.partial(first_kernel, len(own), len(shifted), le...]
  transfers between devices with their start and end apart: 20 -> 20, of which waited for: 6 -> 7; matrix products, arithmetic and copies ran while one was open for 1% -> 1% of each run, Pallas kernels for 25% -> 23%
where the time goes in v5:
time: 72.5 us; the launch traced here: 71.7 us
  starting transfers between devices  32.5 us (45%)
  Pallas kernels  19.9 us (27%)
  waiting for transfers between devices  14.4 us (20%)
  local copies, waits for them, and re-layouts  4.27 us (6%)
    ppermute x6, starting transfers between devices, to_z(): return lax.ppermute(value, 'ao', ring_pairs(distance))  12.9 us
    ppermute x6, starting transfers between devices, other_core(): return lax.ppermute(value, 'rep', SWAP)  12.8 us
    ppermute x6, waiting for transfers between devices, to_z(): return lax.ppermute(value, 'ao', ring_pairs(distance))  12.6 us
    pallas_call x2, Pallas kernels, second_product(): pl.pallas_call(functools.partial(second_kernel, which, blocks, len(groups...  8 us
    pallas_call x2, Pallas kernels, first_product(): pl.pallas_call(functools.partial(first_kernel, len(own), len(shifted), le...  4.4 us
    pallas_call x2, Pallas kernels, shift_tiles(): pl.pallas_call(functools.partial(shift_kernel, first, len(tiles)), out_sh...  3.82 us
    ppermute x4, starting transfers between devices, to_y(): return lax.ppermute(value, 'grp', SWAP)  3.69 us
    ppermute x4, starting transfers between devices, to_x(): return lax.ppermute(value, 'vir', SWAP)  3.13 us
  transfers between devices with their start and end apart: 20, of which 7 were waited for; matrix products, arithmetic and copies ran while one was open for 1% of the time, Pallas kernels for 23%

profile of v5, /device:TPU:9, one launch (start us, length us, event | category | flops | bytes accessed | tf_op | source)
XLA Modules:
  0.0 71.7 jit_solution(17888486992812380438)
XLA Ops:
  0.0 1.0 %constant_dynamic-slice_fusion = bf16[1280,128]{1,0:T(8,128)(2,1)S(1)} fusion(bf16[1280,512]{1,0:T(8,128)(2,1)} %value.1, s32[]{:T(128)S(6)} %select_n.16), kind=kLoop, calls=%fused_computation.8 | loop fusion | bytes 655364 | tf_op jit(solution)/shard_map/dynamic_slice | solution.py:409
  1.0 2.4 %collective-permute-start = (bf16[1280,128]{1,0:T(8,128)(2,1)S(1)}, bf16[1280,128]{1,0:T(8,128)(2,1)S(1)}, u32[]{:S(2)}, u32[]{:S(2)}) collective-permute-start(bf16[1280,128]{1,0:T(8,128)(2,1)S(1)} %constant_dynamic-slice_fusion), channel_id=1, source_target_pairs={{0,4},{4,12},{12,8},{8,0},{1,5},{5,13},{13,9},{9,1},{2,6},{6,14},{... | collective-permute-start | bytes 983048 | tf_op jit(solution)/shard_map/ppermute | solution.py:396
  3.4 1.3 %copy-done = bf16[1280,512]{1,0:T(8,128)(2,1)S(1)} copy-done((bf16[1280,512]{1,0:T(8,128)(2,1)S(1)}, bf16[1280,512]{1,0:T(8,128)(2,1)}, u32[]{:S(2)}) %copy-start) | copy-done | bytes 1310744
  4.8 1.0 %copy-done.5 = bf16[4,1,6,128,128]{4,3,2,1,0:T(8,128)(2,1)S(1)} copy-done((bf16[4,1,6,128,128]{4,3,2,1,0:T(8,128)(2,1)S(1)}, bf16[4,1,6,128,128]{4,3,2,1,0:T(8,128)(2,1)}, u32[]{:S(2)}) %copy-start.5) | copy-done | bytes 786456
  5.8 0.8 %dynamic-slice_bitcast_fusion = (bf16[6,128,128]{2,1,0:T(8,128)(2,1)S(1)}, bf16[6,128,128]{2,1,0:T(8,128)(2,1)}, bf16[6,128,128]{2,1,0:T(8,128)(2,1)S(1)}, bf16[6,128,128]{2,1,0:T(8,128)(2,1)}) fusion(bf16[4,1,6,128,128]{4,3,2,1,0:T(8,128)(2,1)S(1)} %copy-done.5, s32[]{:T(128)S(6)} %select_n.20, s32[]{:T(128)S(6)} %select_n.18, s32[]{:T(128)S(6)} %select_n.17, ...), kind=kLoop, calls=%fused_computation.4 | loop fusion | bytes 1572880 | tf_op jit(solution)/shard_map/jit(dynamic_index_in_dim)/squeeze | solution.py:411
  6.6 3.1 %collective-permute-done.own = bf16[1280,128]{1,0:T(8,128)(2,1)S(1)} collective-permute-done((bf16[1280,128]{1,0:T(8,128)(2,1)S(1)}, bf16[1280,128]{1,0:T(8,128)(2,1)S(1)}, u32[]{:S(2)}, u32[]{:S(2)}) %collective-permute-start) | collective-permute-done | bytes 327712 | tf_op jit(solution)/shard_map/ppermute | solution.py:396
  9.7 1.2 %collective-permute-start.1 = (bf16[1280,128]{1,0:T(8,128)(2,1)S(1)}, bf16[1280,128]{1,0:T(8,128)(2,1)S(1)}, u32[]{:S(2)}, u32[]{:S(2)}) collective-permute-start(bf16[1280,128]{1,0:T(8,128)(2,1)S(1)} %collective-permute-done.own), channel_id=1, source_target_pairs={{0,2},{2,0},{1,3},{3,1},{4,6},{6,4},{5,7},{7,5},{8,10},{10,8},{9,1... | collective-permute-start | bytes 983048 | tf_op jit(solution)/shard_map/ppermute | solution.py:388
  11.0 1.2 %collective-permute-start.2 = (bf16[1280,128]{1,0:T(8,128)(2,1)S(1)}, bf16[1280,128]{1,0:T(8,128)(2,1)S(1)}, u32[]{:S(2)}, u32[]{:S(2)}) collective-permute-start(bf16[1280,128]{1,0:T(8,128)(2,1)S(1)} %collective-permute-done.own), channel_id=1, source_target_pairs={{0,16},{16,0},{1,17},{17,1},{2,18},{18,2},{3,19},{19,3},{4,20},{20... | collective-permute-start | bytes 983048 | tf_op jit(solution)/shard_map/ppermute | solution.py:392
  12.2 3.1 %collective-permute-start.3 = (bf16[1280,128]{1,0:T(8,128)(2,1)S(1)}, bf16[1280,128]{1,0:T(8,128)(2,1)S(1)}, u32[]{:S(2)}, u32[]{:S(2)}) collective-permute-start(bf16[1280,128]{1,0:T(8,128)(2,1)S(1)} %collective-permute-done.own), channel_id=1, source_target_pairs={{0,4},{4,12},{12,8},{8,0},{1,5},{5,13},{13,9},{9,1},{2,6},{6,14},{... | collective-permute-start | bytes 983048 | tf_op jit(solution)/shard_map/ppermute | solution.py:396
  15.4 2.7 %make_plan.1 = (s32[7,24]{1,0:T(8,128)S(1)}, f32[1,1024]{1,0:T(1,128)S(1)}, f32[1024,128]{1,0:T(8,128)S(1)}) custom-call(s32[1,24,2]{2,1,0:T(8,128)S(1)} %copy.9.listed, s32[2,12]{1,0:T(2,128)S(1)} %copy-done.3, s32[1,2]{1,0:T(1,128)S(1)} %copy-done.4, f32[400]{0:T(512)S(1)} %copy-done.2, f32[1,2048]{1,0:T(1,128)S(1)} %bitcast.9), custom_call_target="tpu_custom_call" | custom-call | bytes 2097152 | tf_op jit(solution)/shard_map/make_plan/pallas_call | solution.py:77
  18.3 1.9 %collective-permute-done.3.own = bf16[1280,128]{1,0:T(8,128)(2,1)S(1)} collective-permute-done((bf16[1280,128]{1,0:T(8,128)(2,1)S(1)}, bf16[1280,128]{1,0:T(8,128)(2,1)S(1)}, u32[]{:S(2)}, u32[]{:S(2)}) %collective-permute-start.3) | collective-permute-done | bytes 327712 | tf_op jit(solution)/shard_map/ppermute | solution.py:396
  20.3 0.3 collective-permute-start.4
  20.8 3.1 %collective-permute-start.6 = (bf16[1280,128]{1,0:T(8,128)(2,1)S(1)}, bf16[1280,128]{1,0:T(8,128)(2,1)S(1)}, u32[]{:S(2)}, u32[]{:S(2)}) collective-permute-start(bf16[1280,128]{1,0:T(8,128)(2,1)S(1)} %collective-permute-done.3.own), channel_id=1, source_target_pairs={{0,4},{4,12},{12,8},{8,0},{1,5},{5,13},{13,9},{9,1},{2,6},{6,14},{... | collective-permute-start | bytes 983048 | tf_op jit(solution)/shard_map/ppermute | solution.py:396
  24.0 7.6 %collective-permute-done.7.refs_2_ = bf16[6,128,128]{2,1,0:T(8,128)(2,1)S(1)} collective-permute-done((bf16[6,128,128]{2,1,0:T(8,128)(2,1)S(1)}, bf16[6,128,128]{2,1,0:T(8,128)(2,1)S(1)}, u32[]{:S(2)}, u32[]{:S(2)}) %collective-permute-start.7) | collective-permute-done | bytes 196640 | tf_op jit(solution)/shard_map/ppermute | solution.py:396
  31.7 1.3 %collective-permute-start.8 = (bf16[1920,128]{1,0:T(8,128)(2,1)S(1)}, bf16[1920,128]{1,0:T(8,128)(2,1)S(1)}, u32[]{:S(2)}, u32[]{:S(2)}) collective-permute-start(bf16[1920,128]{1,0:T(8,128)(2,1)S(1)} %get-tuple-element.88), channel_id=1, source_target_pairs={{0,2},{2,0},{1,3},{3,1},{4,6},{6,4},{5,7},{7,5},{8,10},{10,8},{9,1... | collective-permute-start | bytes 1474568 | tf_op jit(solution)/shard_map/ppermute | solution.py:388
  33.0 1.2 %collective-permute-start.9 = (bf16[1920,128]{1,0:T(8,128)(2,1)S(1)}, bf16[1920,128]{1,0:T(8,128)(2,1)S(1)}, u32[]{:S(2)}, u32[]{:S(2)}) collective-permute-start(bf16[1920,128]{1,0:T(8,128)(2,1)S(1)} %get-tuple-element.87), channel_id=1, source_target_pairs={{0,16},{16,0},{1,17},{17,1},{2,18},{18,2},{3,19},{19,3},{4,20},{20... | collective-permute-start | bytes 1474568 | tf_op jit(solution)/shard_map/ppermute | solution.py:392
  34.2 1.9 %shift_tiles.2.refs_1_ = bf16[12,144,256]{2,1,0:T(8,128)(2,1)S(1)} custom-call(s32[7,24]{1,0:T(8,128)S(1)} %get-tuple-element.52.refs_0_, bf16[6,128,128]{2,1,0:T(8,128)(2,1)S(1)} %get-tuple-element.63.refs_1_, bf16[6,128,128]{2,1,0:T(8,128)(2,1)S(1)} %collective-permute-done.7.refs_2_), custom_call_target="tpu_custom_call" | custom-call | bytes 8388608 | tf_op jit(solution)/shard_map/shift_tiles/pallas_call | solution.py:138
  36.2 1.4 %collective-permute-start.12 = (bf16[6,128,128]{2,1,0:T(8,128)(2,1)S(1)}, bf16[6,128,128]{2,1,0:T(8,128)(2,1)S(1)}, u32[]{:S(2)}, u32[]{:S(2)}) collective-permute-start(bf16[6,128,128]{2,1,0:T(8,128)(2,1)S(1)} %copy-done.6), channel_id=1, source_target_pairs={{0,12},{4,8},{12,0},{8,4},{1,13},{5,9},{13,1},{9,5},{2,14},{6,10},... | collective-permute-start | bytes 589832 | tf_op jit(solution)/shard_map/ppermute | solution.py:396
  37.5 3.0 %collective-permute-start.13 = (bf16[6,128,128]{2,1,0:T(8,128)(2,1)S(1)}, bf16[6,128,128]{2,1,0:T(8,128)(2,1)S(1)}, u32[]{:S(2)}, u32[]{:S(2)}) collective-permute-start(bf16[6,128,128]{2,1,0:T(8,128)(2,1)S(1)} %get-tuple-element.71), channel_id=1, source_target_pairs={{0,8},{4,0},{12,4},{8,12},{1,9},{5,1},{13,5},{9,13},{2,10},{6,2},{... | collective-permute-start | bytes 589832 | tf_op jit(solution)/shard_map/ppermute | solution.py:396
  40.5 5.6 %collective-permute-start.14 = (bf16[1280,512]{1,0:T(8,128)(2,1)S(1)}, bf16[1280,512]{1,0:T(8,128)(2,1)S(1)}, u32[]{:S(2)}, u32[]{:S(2)}) collective-permute-start(bf16[1280,512]{1,0:T(8,128)(2,1)S(1)} %stay.1.refs_3_.refs_4_), channel_id=1, source_target_pairs={{0,1},{1,0},{2,3},{3,2},{4,5},{5,4},{6,7},{7,6},{8,9},{9,8},{10,11... | collective-permute-start | bytes 3932168 | tf_op jit(solution)/shard_map/ppermute | solution.py:384
  47.0 0.3 collective-permute-start.15
  47.4 0.3 collective-permute-start.10
  47.7 1.0 %collective-permute-start.11 = (bf16[640,128]{1,0:T(8,128)(2,1)S(1)}, bf16[640,128]{1,0:T(8,128)(2,1)S(1)}, u32[]{:S(2)}, u32[]{:S(2)}) collective-permute-start(bf16[640,128]{1,0:T(8,128)(2,1)S(1)} %slice.23), channel_id=1, source_target_pairs={{0,16},{16,0},{1,17},{17,1},{2,18},{18,2},{3,19},{19,3},{4,20},{20... | collective-permute-start | bytes 491528 | tf_op jit(solution)/shard_map/ppermute | solution.py:392
  48.7 1.9 %shift_tiles.3.refs_2_ = bf16[12,144,256]{2,1,0:T(8,128)(2,1)S(1)} custom-call(s32[7,24]{1,0:T(8,128)S(1)} %get-tuple-element.52.refs_0_, bf16[6,128,128]{2,1,0:T(8,128)(2,1)S(1)} %collective-permute-done.12.refs_1_, bf16[6,128,128]{2,1,0:T(8,128)(2,1)S(1)} %collective-permute-done.13.refs_2_), custom_call_target="tpu_custom_call" | custom-call | bytes 8388608 | tf_op jit(solution)/shard_map/shift_tiles/pallas_call | solution.py:138
  50.6 1.0 %collective-permute-done.10.far_x = bf16[640,128]{1,0:T(8,128)(2,1)S(1)} collective-permute-done((bf16[640,128]{1,0:T(8,128)(2,1)S(1)}, bf16[640,128]{1,0:T(8,128)(2,1)S(1)}, u32[]{:S(2)}, u32[]{:S(2)}) %collective-permute-start.10) | collective-permute-done | bytes 163872 | tf_op jit(solution)/shard_map/ppermute | solution.py:388
  52.2 6.0 %collective-permute-start.17 = (bf16[1280,512]{1,0:T(8,128)(2,1)S(1)}, bf16[1280,512]{1,0:T(8,128)(2,1)S(1)}, u32[]{:S(2)}, u32[]{:S(2)}) collective-permute-start(bf16[1280,512]{1,0:T(8,128)(2,1)S(1)} %assemble.5.refs_5_.refs_7_), channel_id=1, source_target_pairs={{0,1},{1,0},{2,3},{3,2},{4,5},{5,4},{6,7},{7,6},{8,9},{9,8},{10,11... | collective-permute-start | bytes 3932168 | tf_op jit(solution)/shard_map/ppermute | solution.py:384
  58.2 2.2 %first_product.2.refs_2_ = bf16[1280,512]{1,0:T(8,128)(2,1)S(1)} custom-call(s32[7,24]{1,0:T(8,128)S(1)} %get-tuple-element.52.refs_0_, bf16[12,144,256]{2,1,0:T(8,128)(2,1)S(1)} %shift_tiles.2.refs_1_, bf16[12,144,256]{2,1,0:T(8,128)(2,1)S(1)} %shift_tiles.3.refs_2_, bf16[1280,512]{1,0:T(8,128)(2,1)S(1)} %stay.1.refs_3_.refs_4_, ...), custom_call_target="tpu_custom_call" | custom-call | flops 1811939328 | bytes 6291456 | tf_op jit(solution)/shard_map/first_product/pallas_call | solution.py:292
  60.5 0.3 collective-permute-done.17.refs_8_.refs_11_
  60.8 2.2 %first_product.3.refs_2_ = bf16[1280,512]{1,0:T(8,128)(2,1)S(1)} custom-call(s32[7,24]{1,0:T(8,128)S(1)} %get-tuple-element.52.refs_0_, bf16[12,144,256]{2,1,0:T(8,128)(2,1)S(1)} %shift_tiles.2.refs_1_, bf16[12,144,256]{2,1,0:T(8,128)(2,1)S(1)} %shift_tiles.3.refs_2_, bf16[1280,512]{1,0:T(8,128)(2,1)S(1)} %assemble.3.refs_4_.refs_3_.refs_5_, ...), custom_call_target="tpu_custom_call" | custom-call | flops 1811939328 | bytes 6291456 | tf_op jit(solution)/shard_map/first_product/pallas_call | solution.py:292
  63.1 0.5 collective-permute-start.18
  63.5 4.3 %second_product.2 = (bf16[1,1024,1024]{2,1,0:T(8,128)(2,1)}, bf16[2,2,1280,512]{3,2,1,0:T(8,128)(2,1)S(1)}) custom-call(f32[1,1024]{1,0:T(1,128)S(1)} %get-tuple-element.44.refs_0_, f32[1024,128]{1,0:T(8,128)S(1)} %get-tuple-element.45.refs_1_, bf16[1280,512]{1,0:T(8,128)(2,1)S(1)} %first_product.2.refs_2_, ...), custom_call_target="tpu_custom_call" | custom-call | flops 2684354560 | bytes 10485760 | tf_op jit(solution)/shard_map/second_product/pallas_call | solution.py:358
  67.8 3.7 %second_product.3 = bf16[1,1024,1024]{2,1,0:T(8,128)(2,1)} custom-call(f32[1,1024]{1,0:T(1,128)S(1)} %get-tuple-element.44.refs_0_, f32[1024,128]{1,0:T(8,128)S(1)} %get-tuple-element.45.refs_1_, bf16[1280,512]{1,0:T(8,128)(2,1)S(1)} %first_product.3.refs_2_, bf16[1280,512]{1,0:T(8,128)(2,1)S(1)} %collective-permute-done.18.refs_3_, ...), custom_call_target="tpu_custom_call", output_to_operand_aliasing={{}: (5, {})} | custom-call | flops 2684354560 | bytes 10485760 | tf_op jit(solution)/shard_map/second_product/pallas_call | solution.py:358
  (48 shorter events, 2.4 us)
Async XLA Ops:
  1.0 8.7 %collective-permute-start = (bf16[1280,128]{1,0:T(8,128)(2,1)S(1)}, bf16[1280,128]{1,0:T(8,128)(2,1)S(1)}, u32[]{:S(2)}, u32[]{:S(2)}) collective-permute-start(bf16[1280,128]{1,0:T(8,128)(2,1)S(1)} %constant_dynamic-slice_fusion), channel_id=1, source_target_pairs={{0,4},{4,12},{12,8},{8,0},{1,5},{5,13},{13,9},{9,1},{2,6},{6,14},{... | collective-permute-start | bytes 983048 | tf_op jit(solution)/shard_map/ppermute | solution.py:396
  3.4 1.3 %copy-start = (bf16[1280,512]{1,0:T(8,128)(2,1)S(1)}, bf16[1280,512]{1,0:T(8,128)(2,1)}, u32[]{:S(2)}) copy-start(bf16[1280,512]{1,0:T(8,128)(2,1)} %value.1) | copy-start | bytes 3932164
  4.7 1.1 %copy-start.5 = (bf16[4,1,6,128,128]{4,3,2,1,0:T(8,128)(2,1)S(1)}, bf16[4,1,6,128,128]{4,3,2,1,0:T(8,128)(2,1)}, u32[]{:S(2)}) copy-start(bf16[4,1,6,128,128]{4,3,2,1,0:T(8,128)(2,1)} %param.7) | copy-start | bytes 2359300
  4.8 10.5 %copy-start.8 = (s32[1,24,2]{1,2,0:T(2,128)S(1)}, s32[1,24,2]{1,2,0:T(2,128)}, u32[]{:S(2)}) copy-start(s32[1,24,2]{1,2,0:T(2,128)} %param.12) | copy-start | bytes 580
  4.8 10.6 %copy-start.1 = (f32[2048]{0:T(1024)S(1)}, f32[2048]{0:T(1024)}, u32[]{:S(2)}) copy-start(f32[2048]{0:T(1024)} %param.10) | copy-start | bytes 24580
  4.8 10.6 %copy-start.2 = (f32[400]{0:T(512)S(1)}, f32[400]{0:T(512)}, u32[]{:S(2)}) copy-start(f32[400]{0:T(512)} %eps_occ.1) | copy-start | bytes 4804
  4.8 10.6 %copy-start.3 = (s32[2,12]{1,0:T(2,128)S(1)}, s32[2,12]{1,0:T(2,128)}, u32[]{:S(2)}) copy-start(s32[2,12]{1,0:T(2,128)} %extra.1) | copy-start | bytes 292
  4.8 10.6 %copy-start.4 = (s32[1,2]{1,0:T(1,128)S(1)}, s32[1,2]{1,0:T(1,128)}, u32[]{:S(2)}) copy-start(s32[1,2]{1,0:T(1,128)} %pair_occ.1) | copy-start | bytes 28
  9.7 14.2 %copy-start.7 = (bf16[6,128,128]{2,1,0:T(8,128)(2,1)S(1)}, bf16[6,128,128]{2,1,0:T(8,128)(2,1)}, u32[]{:S(2)}) copy-start(bf16[6,128,128]{2,1,0:T(8,128)(2,1)} %get-tuple-element.56) | copy-start | bytes 589828
  9.7 8.4 %collective-permute-start.1 = (bf16[1280,128]{1,0:T(8,128)(2,1)S(1)}, bf16[1280,128]{1,0:T(8,128)(2,1)S(1)}, u32[]{:S(2)}, u32[]{:S(2)}) collective-permute-start(bf16[1280,128]{1,0:T(8,128)(2,1)S(1)} %collective-permute-done.own), channel_id=1, source_target_pairs={{0,2},{2,0},{1,3},{3,1},{4,6},{6,4},{5,7},{7,5},{8,10},{10,8},{9,1... | collective-permute-start | bytes 983048 | tf_op jit(solution)/shard_map/ppermute | solution.py:388
  11.0 7.4 %collective-permute-start.2 = (bf16[1280,128]{1,0:T(8,128)(2,1)S(1)}, bf16[1280,128]{1,0:T(8,128)(2,1)S(1)}, u32[]{:S(2)}, u32[]{:S(2)}) collective-permute-start(bf16[1280,128]{1,0:T(8,128)(2,1)S(1)} %collective-permute-done.own), channel_id=1, source_target_pairs={{0,16},{16,0},{1,17},{17,1},{2,18},{18,2},{3,19},{19,3},{4,20},{20... | collective-permute-start | bytes 983048 | tf_op jit(solution)/shard_map/ppermute | solution.py:392
  12.2 8.0 %collective-permute-start.3 = (bf16[1280,128]{1,0:T(8,128)(2,1)S(1)}, bf16[1280,128]{1,0:T(8,128)(2,1)S(1)}, u32[]{:S(2)}, u32[]{:S(2)}) collective-permute-start(bf16[1280,128]{1,0:T(8,128)(2,1)S(1)} %collective-permute-done.own), channel_id=1, source_target_pairs={{0,4},{4,12},{12,8},{8,0},{1,5},{5,13},{13,9},{9,1},{2,6},{6,14},{... | collective-permute-start | bytes 983048 | tf_op jit(solution)/shard_map/ppermute | solution.py:396
  20.3 11.3 %collective-permute-start.4 = (bf16[1920,128]{1,0:T(8,128)(2,1)S(1)}, bf16[1920,128]{1,0:T(8,128)(2,1)S(1)}, u32[]{:S(2)}, u32[]{:S(2)}) collective-permute-start(bf16[1920,128]{1,0:T(8,128)(2,1)S(1)} %get-tuple-element.90), channel_id=1, source_target_pairs={{0,2},{2,0},{1,3},{3,1},{4,6},{6,4},{5,7},{7,5},{8,10},{10,8},{9,1... | collective-permute-start | bytes 1474568 | tf_op jit(solution)/shard_map/ppermute | solution.py:388
  20.6 11.0 %collective-permute-start.5 = (bf16[1920,128]{1,0:T(8,128)(2,1)S(1)}, bf16[1920,128]{1,0:T(8,128)(2,1)S(1)}, u32[]{:S(2)}, u32[]{:S(2)}) collective-permute-start(bf16[1920,128]{1,0:T(8,128)(2,1)S(1)} %get-tuple-element.89), channel_id=1, source_target_pairs={{0,16},{16,0},{1,17},{17,1},{2,18},{18,2},{3,19},{19,3},{4,20},{20... | collective-permute-start | bytes 1474568 | tf_op jit(solution)/shard_map/ppermute | solution.py:392
  20.8 10.7 %collective-permute-start.6 = (bf16[1280,128]{1,0:T(8,128)(2,1)S(1)}, bf16[1280,128]{1,0:T(8,128)(2,1)S(1)}, u32[]{:S(2)}, u32[]{:S(2)}) collective-permute-start(bf16[1280,128]{1,0:T(8,128)(2,1)S(1)} %collective-permute-done.3.own), channel_id=1, source_target_pairs={{0,4},{4,12},{12,8},{8,0},{1,5},{5,13},{13,9},{9,1},{2,6},{6,14},{... | collective-permute-start | bytes 983048 | tf_op jit(solution)/shard_map/ppermute | solution.py:396
  23.9 7.6 %collective-permute-start.7 = (bf16[6,128,128]{2,1,0:T(8,128)(2,1)S(1)}, bf16[6,128,128]{2,1,0:T(8,128)(2,1)S(1)}, u32[]{:S(2)}, u32[]{:S(2)}) collective-permute-start(bf16[6,128,128]{2,1,0:T(8,128)(2,1)S(1)} %copy-done.7), channel_id=1, source_target_pairs={{0,4},{4,12},{12,8},{8,0},{1,5},{5,13},{13,9},{9,1},{2,6},{6,14},{... | collective-permute-start | bytes 589832 | tf_op jit(solution)/shard_map/ppermute | solution.py:396
  31.6 4.5 %copy-start.6 = (bf16[6,128,128]{2,1,0:T(8,128)(2,1)S(1)}, bf16[6,128,128]{2,1,0:T(8,128)(2,1)}, u32[]{:S(2)}) copy-start(bf16[6,128,128]{2,1,0:T(8,128)(2,1)} %get-tuple-element.70) | copy-start | bytes 589828
  31.7 14.7 %collective-permute-start.8 = (bf16[1920,128]{1,0:T(8,128)(2,1)S(1)}, bf16[1920,128]{1,0:T(8,128)(2,1)S(1)}, u32[]{:S(2)}, u32[]{:S(2)}) collective-permute-start(bf16[1920,128]{1,0:T(8,128)(2,1)S(1)} %get-tuple-element.88), channel_id=1, source_target_pairs={{0,2},{2,0},{1,3},{3,1},{4,6},{6,4},{5,7},{7,5},{8,10},{10,8},{9,1... | collective-permute-start | bytes 1474568 | tf_op jit(solution)/shard_map/ppermute | solution.py:388
  33.0 13.4 %collective-permute-start.9 = (bf16[1920,128]{1,0:T(8,128)(2,1)S(1)}, bf16[1920,128]{1,0:T(8,128)(2,1)S(1)}, u32[]{:S(2)}, u32[]{:S(2)}) collective-permute-start(bf16[1920,128]{1,0:T(8,128)(2,1)S(1)} %get-tuple-element.87), channel_id=1, source_target_pairs={{0,16},{16,0},{1,17},{17,1},{2,18},{18,2},{3,19},{19,3},{4,20},{20... | collective-permute-start | bytes 1474568 | tf_op jit(solution)/shard_map/ppermute | solution.py:392
  36.2 11.2 %collective-permute-start.12 = (bf16[6,128,128]{2,1,0:T(8,128)(2,1)S(1)}, bf16[6,128,128]{2,1,0:T(8,128)(2,1)S(1)}, u32[]{:S(2)}, u32[]{:S(2)}) collective-permute-start(bf16[6,128,128]{2,1,0:T(8,128)(2,1)S(1)} %copy-done.6), channel_id=1, source_target_pairs={{0,12},{4,8},{12,0},{8,4},{1,13},{5,9},{13,1},{9,5},{2,14},{6,10},... | collective-permute-start | bytes 589832 | tf_op jit(solution)/shard_map/ppermute | solution.py:396
  37.5 10.2 %collective-permute-start.13 = (bf16[6,128,128]{2,1,0:T(8,128)(2,1)S(1)}, bf16[6,128,128]{2,1,0:T(8,128)(2,1)S(1)}, u32[]{:S(2)}, u32[]{:S(2)}) collective-permute-start(bf16[6,128,128]{2,1,0:T(8,128)(2,1)S(1)} %get-tuple-element.71), channel_id=1, source_target_pairs={{0,8},{4,0},{12,4},{8,12},{1,9},{5,1},{13,5},{9,13},{2,10},{6,2},{... | collective-permute-start | bytes 589832 | tf_op jit(solution)/shard_map/ppermute | solution.py:396
  40.5 17.7 %collective-permute-start.14 = (bf16[1280,512]{1,0:T(8,128)(2,1)S(1)}, bf16[1280,512]{1,0:T(8,128)(2,1)S(1)}, u32[]{:S(2)}, u32[]{:S(2)}) collective-permute-start(bf16[1280,512]{1,0:T(8,128)(2,1)S(1)} %stay.1.refs_3_.refs_4_), channel_id=1, source_target_pairs={{0,1},{1,0},{2,3},{3,2},{4,5},{5,4},{6,7},{7,6},{8,9},{9,8},{10,11... | collective-permute-start | bytes 3932168 | tf_op jit(solution)/shard_map/ppermute | solution.py:384
  46.7 11.4 %collective-permute-start.16 = (bf16[1280,512]{1,0:T(8,128)(2,1)S(1)}, bf16[1280,512]{1,0:T(8,128)(2,1)S(1)}, u32[]{:S(2)}, u32[]{:S(2)}) collective-permute-start(bf16[1280,512]{1,0:T(8,128)(2,1)S(1)} %assemble.4.refs_5_.refs_4_.refs_6_), channel_id=1, source_target_pairs={{0,1},{1,0},{2,3},{3,2},{4,5},{5,4},{6,7},{7,6},{8,9},{9,8},{10,11... | collective-permute-start | bytes 3932168 | tf_op jit(solution)/shard_map/ppermute | solution.py:384
  47.0 11.2 %collective-permute-start.15 = (bf16[1280,512]{1,0:T(8,128)(2,1)S(1)}, bf16[1280,512]{1,0:T(8,128)(2,1)S(1)}, u32[]{:S(2)}, u32[]{:S(2)}) collective-permute-start(bf16[1280,512]{1,0:T(8,128)(2,1)S(1)} %assemble.3.refs_4_.refs_3_.refs_5_), channel_id=1, source_target_pairs={{0,1},{1,0},{2,3},{3,2},{4,5},{5,4},{6,7},{7,6},{8,9},{9,8},{10,11... | collective-permute-start | bytes 3932168 | tf_op jit(solution)/shard_map/ppermute | solution.py:384
  47.4 4.2 %collective-permute-start.10 = (bf16[640,128]{1,0:T(8,128)(2,1)S(1)}, bf16[640,128]{1,0:T(8,128)(2,1)S(1)}, u32[]{:S(2)}, u32[]{:S(2)}) collective-permute-start(bf16[640,128]{1,0:T(8,128)(2,1)S(1)} %slice.22), channel_id=1, source_target_pairs={{0,2},{2,0},{1,3},{3,1},{4,6},{6,4},{5,7},{7,5},{8,10},{10,8},{9,1... | collective-permute-start | bytes 491528 | tf_op jit(solution)/shard_map/ppermute | solution.py:388
  47.7 4.2 %collective-permute-start.11 = (bf16[640,128]{1,0:T(8,128)(2,1)S(1)}, bf16[640,128]{1,0:T(8,128)(2,1)S(1)}, u32[]{:S(2)}, u32[]{:S(2)}) collective-permute-start(bf16[640,128]{1,0:T(8,128)(2,1)S(1)} %slice.23), channel_id=1, source_target_pairs={{0,16},{16,0},{1,17},{17,1},{2,18},{18,2},{3,19},{19,3},{4,20},{20... | collective-permute-start | bytes 491528 | tf_op jit(solution)/shard_map/ppermute | solution.py:392
  52.2 8.7 %collective-permute-start.17 = (bf16[1280,512]{1,0:T(8,128)(2,1)S(1)}, bf16[1280,512]{1,0:T(8,128)(2,1)S(1)}, u32[]{:S(2)}, u32[]{:S(2)}) collective-permute-start(bf16[1280,512]{1,0:T(8,128)(2,1)S(1)} %assemble.5.refs_5_.refs_7_), channel_id=1, source_target_pairs={{0,1},{1,0},{2,3},{3,2},{4,5},{5,4},{6,7},{7,6},{8,9},{9,8},{10,11... | collective-permute-start | bytes 3932168 | tf_op jit(solution)/shard_map/ppermute | solution.py:384
  60.4 3.1 %collective-permute-start.19 = (bf16[1280,512]{1,0:T(8,128)(2,1)S(1)}, bf16[1280,512]{1,0:T(8,128)(2,1)S(1)}, u32[]{:S(2)}, u32[]{:S(2)}) collective-permute-start(bf16[1280,512]{1,0:T(8,128)(2,1)S(1)} %first_product.2.refs_2_), channel_id=1, source_target_pairs={{0,1},{1,0},{2,3},{3,2},{4,5},{5,4},{6,7},{7,6},{8,9},{9,8},{10,11... | collective-permute-start | bytes 3932168 | tf_op jit(solution)/shard_map/ppermute | solution.py:384
  63.1 4.7 %collective-permute-start.18 = (bf16[1280,512]{1,0:T(8,128)(2,1)S(1)}, bf16[1280,512]{1,0:T(8,128)(2,1)S(1)}, u32[]{:S(2)}, u32[]{:S(2)}) collective-permute-start(bf16[1280,512]{1,0:T(8,128)(2,1)S(1)} %first_product.3.refs_2_), channel_id=1, source_target_pairs={{0,1},{1,0},{2,3},{3,2},{4,5},{5,4},{6,7},{7,6},{8,9},{9,8},{10,11... | collective-permute-start | bytes 3932168 | tf_op jit(solution)/shard_map/ppermute | solution.py:384

commit v6 on v5

--- a/solution.py
+++ b/solution.py
@@ -228,6 +228,22 @@
             copy()
         else:
             pl.when(slot == first + s)(copy)
+
+
+def choose_kernel(which, blocks, *refs):
+    pick(ring_slot(column_block(which, blocks)), which, refs[:-1], refs[-1])
+
+
+def choose(which, blocks, groups):
+    return pl.pallas_call(
+        functools.partial(choose_kernel, which, blocks),
+        out_shape=jax.ShapeDtypeStruct(groups[0].shape, BF16),
+        in_specs=[VMEM] * len(groups),
+        out_specs=VMEM,
+        compiler_params=pltpu.CompilerParams(vmem_limit_bytes=8 * MIB),
+        cost_estimate=pl.CostEstimate(flops=0, bytes_accessed=MIB, transcendentals=0),
+        name="choose",
+    )(*groups)
 
 
 def first_kernel(n_own, n_shifted, n_late, which, blocks, *refs):
@@ -305,23 +321,48 @@
     return result[0], [*shifted, *result[1:]]
 
 
-def second_kernel(which, blocks, n_groups, n_before, *refs):
-    by_col, by_row, middle, middle_other = refs[:4]
-    core = lax.axis_index("rep")
+def send_kernel(ringed, middle, *refs):
+    groups = refs[:GROUPS]
+    out, held = refs[GROUPS:]
     mine = GROUPS // 2
-    if n_groups:
-        own, other = refs[4 : 4 + GROUPS], refs[4 + GROUPS : 4 + 2 * GROUPS]
-        out, held, ready, out_sems = refs[4 + 2 * GROUPS + n_before :]
-        for i in range(mine):
-            wanted = core * mine + i
-            slot = ring_slot(wanted) if blocks > 1 else wanted
-            pick(slot, 0, own, held.at[i, 0])
-            pick(slot, 0, other, held.at[i, 1])
-    else:
-        held = refs[4]
-        out, ready, out_sems = refs[5 + n_before :]
-    width = held.shape[3]
+    for i in range(mine):
+        wanted = (1 - lax.axis_index("rep")) * mine + i
+        pick(ring_slot(wanted) if ringed else wanted, 0, groups, held.at[i])
+    dims = (((0,), (0,)), ((), ()))
+    for i in range(mine):
+        out[i] = lax.dot_general(
+            held[i], middle[...], dims, preferred_element_type=F32
+        ).astype(BF16)
+
+
+def send_product(middle, groups, ringed):
+    rows, width = groups[0].shape
     columns = middle.shape[1]
+    mine = GROUPS // 2
+    return pl.pallas_call(
+        functools.partial(send_kernel, ringed),
+        out_shape=jax.ShapeDtypeStruct((mine, width, columns), BF16),
+        in_specs=[VMEM] * (1 + GROUPS),
+        out_specs=VMEM,
+        scratch_shapes=[pltpu.VMEM((mine, rows, width), BF16)],
+        compiler_params=pltpu.CompilerParams(vmem_limit_bytes=12 * MIB),
+        cost_estimate=pl.CostEstimate(
+            flops=2 * mine * rows * width * columns, bytes_accessed=5 * MIB, transcendentals=0
+        ),
+        name="send_product",
+    )(middle, *groups)
+
+
+def keep_kernel(which, blocks, n_before, *refs):
+    by_col, by_row, middle, got = refs[:4]
+    groups = refs[4 : 4 + GROUPS]
+    out, held, ready, out_sems = refs[4 + GROUPS + n_before :]
+    mine = GROUPS // 2
+    width = held.shape[2]
+    columns = middle.shape[1]
+    for i in range(mine):
+        wanted = lax.axis_index("rep") * mine + i
+        pick(ring_slot(wanted) if blocks > 1 else wanted, 0, groups, held.at[i])
     if blocks > 1:
         block = column_block(which, blocks) - lax.axis_index("vir") * blocks
         column = pl.multiple_of(block * columns, LANES)
@@ -330,8 +371,8 @@
     dims = (((0,), (0,)), ((), ()))
     stores = []
     for i in range(mine):
-        total = lax.dot_general(held[i, 0], middle[...], dims, preferred_element_type=F32)
-        total += lax.dot_general(held[i, 1], middle_other[...], dims, preferred_element_type=F32)
+        total = lax.dot_general(held[i], middle[...], dims, preferred_element_type=F32)
+        total += got[i].astype(F32)
         tall = by_row[i * width : (i + 1) * width, :]
         tall = jnp.concatenate([tall] * (columns // LANES), axis=1)
         ready[i] = (total / (by_col[:, pl.ds(column, columns)] - tall)).astype(BF16)
@@ -344,36 +385,29 @@
         store.wait()
 
 
-def second_product(which, blocks, energies, middle, groups, held, before):
-    rows, columns = middle[0].shape
+def keep_product(which, blocks, energies, middle, got, groups, before):
+    rows, width = groups[0].shape
+    columns = middle.shape[1]
     mine = GROUPS // 2
-    width = energies[1].shape[0] // mine
     extra = [] if before is None else [before]
-    fixed = [*energies, *middle, *(groups if held is None else [held])]
-    out_shape = [jax.ShapeDtypeStruct((1, mine * width, blocks * columns), BF16)]
-    out_specs = [ANY]
-    if held is None:
-        out_shape.append(jax.ShapeDtypeStruct((mine, 2, rows, width), BF16))
-        out_specs.append(VMEM)
-    result = pl.pallas_call(
-        functools.partial(
-            second_kernel, which, blocks, len(groups) if held is None else 0, len(extra)
-        ),
-        out_shape=out_shape,
+    fixed = [*energies, middle, got, *groups]
+    return pl.pallas_call(
+        functools.partial(keep_kernel, which, blocks, len(extra)),
+        out_shape=jax.ShapeDtypeStruct((1, mine * width, blocks * columns), BF16),
         in_specs=[VMEM] * len(fixed) + [ANY] * len(extra),
-        out_specs=out_specs,
+        out_specs=ANY,
         scratch_shapes=[
+            pltpu.VMEM((mine, rows, width), BF16),
             pltpu.VMEM((mine, width, columns), BF16),
             pltpu.SemaphoreType.DMA((mine,)),
         ],
         input_output_aliases={len(fixed): 0} if extra else {},
-        compiler_params=pltpu.CompilerParams(vmem_limit_bytes=16 * MIB),
+        compiler_params=pltpu.CompilerParams(vmem_limit_bytes=14 * MIB),
         cost_estimate=pl.CostEstimate(
-            flops=4 * mine * rows * width * columns, bytes_accessed=10 * MIB, transcendentals=0
+            flops=2 * mine * rows * width * columns, bytes_accessed=6 * MIB, transcendentals=0
         ),
-        name="second_product",
+        name="keep_product",
     )(*fixed, *extra)
-    return (result[0], result[1] if held is None else held)
 
 
 def ring_pairs(distance):
@@ -411,22 +445,26 @@
         lax.dynamic_index_in_dim(half_ints[:, 0], owner[k], 0, False) for k in range(4)
     ]
     z1, t, group0 = together((to_z(own), t, stay(coeff)))
-    x1, y1, z2, t, plan = together((to_x(z1), to_y(z1), to_z(z1), t, plan))
+    z2, y1, x1, t, plan = together((to_z(z1), to_y(z1), to_x(z1), t, plan))
     x2, y2, z3, t1, t = together(
         (to_x(join(z2, y1[:half])), to_y(join(z2, x1[half:])), to_z(z2), to_z(t[1], 1), t)
     )
     group1 = assemble(z1, x1, y1, x2, y2)
     early = shift(plan, 0, [t[0], t1])
-    early, last = together((early, t[2]))
-    t2, t3 = to_z(last, 2), to_z(t[3], 3)
-    x3, y3, group1, early = together(
-        (to_x(join(z3, y2[:half])), to_y(join(z3, x2[half:rows])), group1, early)
+    t2, t3 = to_z(t[2], 2), to_z(t[3], 3)
+    x3, y3, early, group1, t2, t3 = together(
+        (to_x(join(z3, y2[:half])), to_y(join(z3, x2[half:rows])), early, group1, t2, t3)
     )
     group2 = assemble(z2, x2, y2, x3, y3)
+    blocks = 4 // lax.axis_size("vir")
+    first = choose(0, blocks, [group0, group1, group2])
     late = shift(plan, 2 * t2.shape[0], [t2, t3])
-    x4, y4, late = together((to_x(y3[:half]), to_y(x3[half:rows]), late))
+    middle, shifted = first_product(
+        plan, [early, late], [], [first], [other_core(first)], 0, blocks
+    )
+    x4, y4, middle = together((to_x(y3[:half]), to_y(x3[half:rows]), middle))
     group3 = assemble(z3, x3, y3, x4, y4)
-    return [group0, group1, group2, group3], [early, late], [], plan
+    return [group0, group1, group2, group3], middle, shifted, plan
 
 
 def exchange_any(half_ints, coeff):
@@ -450,26 +488,28 @@
         eps_vir.reshape(1, -1), rows, full_width // lax.axis_size("rep"), b_width,
     )
     if ringed:
-        groups, shifted, late, plan = exchange_small(half_ints, coeff, plan, shift_tiles)
-        own, blocks = groups, b_width // width
+        groups, early_middle, shifted, plan = exchange_small(half_ints, coeff, plan, shift_tiles)
+        blocks = b_width // width
     else:
         gathered, groups, tiles = exchange_any(half_ints, coeff)
         own, blocks = [lax.dynamic_slice_in_dim(gathered, vir * b_width, b_width, 1)], 1
-        shifted, late = [shift_tiles(plan, 0, [tiles])], []
-    others = [other_core(g) for g in groups]
-    other = others if ringed else [other_core(own[0])]
-    out = held = None
+        shifted = [shift_tiles(plan, 0, [tiles])]
+    if ringed:
+        own = [choose(1, blocks, groups[1:])]
+    other = [other_core(g) for g in own]
+    middles, got = [], []
     for which in range(blocks):
-        some = slice(which, GROUPS - 1 + which) if ringed else slice(None)
-        middle, shifted = first_product(
-            plan, shifted, late, own[some], other[some], which, blocks
-        )
-        middle, shifted = lax.optimization_barrier((middle, shifted))
-        late = []
-        both = (middle, other_core(middle))
-        out, held = second_product(
-            which, blocks, energies, both, [*groups, *others], held, out
-        )
+        if ringed and which == 0:
+            middle = early_middle
+        else:
+            middle, shifted = first_product(plan, shifted, [], own, other, which, blocks)
+        sent = send_product(middle, groups, ringed)
+        middle, sent = lax.optimization_barrier((middle, sent))
+        middles.append(middle)
+        got.append(other_core(sent))
+    out = None
+    for which in range(blocks):
+        out = keep_product(which, blocks, energies, middles[which], got[which], groups, out)
     return out
 
 

time: 72.5 us -> 71.8 us (level)
  starting transfers between devices: 32.5 us -> 19.9 us
  waiting for transfers between devices: 14.4 us -> 25.8 us
  Pallas kernels: 19.9 us -> 21 us
    ppermute x6 -> x4, starting transfers between devices: 12.8 us -> 3.56 us  [other_core(): return lax.ppermute(value, 'rep', SWAP)]
    ppermute x6, waiting for transfers between devices: 12.6 us -> 21.1 us  [to_z(): return lax.ppermute(value, 'ao', ring_pairs(distance))]
    ppermute x6, starting transfers between devices: 12.9 us -> 9.32 us  [to_z(): return lax.ppermute(value, 'ao', ring_pairs(distance))]
    ppermute x4, waiting for transfers between devices: 0.46 us -> 2.82 us  [to_y(): return lax.ppermute(value, 'grp', SWAP)]
    pallas_call x2 -> x6, Pallas kernels: 8 us -> 9.13 us  [the longest x2 5.41 us: keep_product(): pl.pallas_call(functools.partial(keep_kernel, which, blocks, len(extra)),...]
    ppermute x4, starting transfers between devices: 3.13 us -> 4.08 us  [to_x(): return lax.ppermute(value, 'vir', SWAP)]
  transfers between devices with their start and end apart: 20 -> 18, of which waited for: 7 -> 9; matrix products, arithmetic and copies ran while one was open for 1% -> 1% of each run, Pallas kernels for 23% -> 25%
where the time goes in v6:
time: 71.8 us; the launch traced here: 71.6 us
  waiting for transfers between devices  25.8 us (36%)
  Pallas kernels  21 us (29%)
  starting transfers between devices  19.9 us (28%)
  local copies, waits for them, and re-layouts  4.28 us (6%)
    ppermute x6, waiting for transfers between devices, to_z(): return lax.ppermute(value, 'ao', ring_pairs(distance))  21.1 us
    ppermute x6, starting transfers between devices, to_z(): return lax.ppermute(value, 'ao', ring_pairs(distance))  9.32 us
    pallas_call x2, Pallas kernels, keep_product(): pl.pallas_call(functools.partial(keep_kernel, which, blocks, len(extra)),...  5.41 us
    pallas_call x2, Pallas kernels, first_product(): pl.pallas_call(functools.partial(first_kernel, len(own), len(shifted), le...  4.36 us
    ppermute x4, starting transfers between devices, to_x(): return lax.ppermute(value, 'vir', SWAP)  4.08 us
    pallas_call x2, Pallas kernels, shift_tiles(): pl.pallas_call(functools.partial(shift_kernel, first, len(tiles)), out_sh...  3.83 us
    ppermute x4, starting transfers between devices, other_core(): return lax.ppermute(value, 'rep', SWAP)  3.56 us
    pallas_call x2, Pallas kernels, send_product(): pl.pallas_call(functools.partial(send_kernel, ringed), out_shape=jax.Shap...  3.49 us
  transfers between devices with their start and end apart: 18, of which 9 were waited for; matrix products, arithmetic and copies ran while one was open for 1% of the time, Pallas kernels for 25%

profile of v6, /device:TPU:9, one launch (start us, length us, event | category | flops | bytes accessed | tf_op | source)
XLA Modules:
  0.0 71.6 jit_solution(18391182130385553398)
XLA Ops:
  0.0 1.0 %constant_dynamic-slice_fusion = bf16[1280,128]{1,0:T(8,128)(2,1)S(1)} fusion(bf16[1280,512]{1,0:T(8,128)(2,1)} %value.1, s32[]{:T(128)S(6)} %select_n.16), kind=kLoop, calls=%fused_computation.8 | loop fusion | bytes 655364 | tf_op jit(solution)/shard_map/dynamic_slice | solution.py:443
  1.0 2.4 %collective-permute-start = (bf16[1280,128]{1,0:T(8,128)(2,1)S(1)}, bf16[1280,128]{1,0:T(8,128)(2,1)S(1)}, u32[]{:S(2)}, u32[]{:S(2)}) collective-permute-start(bf16[1280,128]{1,0:T(8,128)(2,1)S(1)} %constant_dynamic-slice_fusion), channel_id=1, source_target_pairs={{0,4},{4,12},{12,8},{8,0},{1,5},{5,13},{13,9},{9,1},{2,6},{6,14},{... | collective-permute-start | bytes 983048 | tf_op jit(solution)/shard_map/ppermute | solution.py:430
  3.4 1.3 %copy-done = bf16[1280,512]{1,0:T(8,128)(2,1)S(1)} copy-done((bf16[1280,512]{1,0:T(8,128)(2,1)S(1)}, bf16[1280,512]{1,0:T(8,128)(2,1)}, u32[]{:S(2)}) %copy-start) | copy-done | bytes 1310744
  4.8 1.0 %copy-done.5 = bf16[4,1,6,128,128]{4,3,2,1,0:T(8,128)(2,1)S(1)} copy-done((bf16[4,1,6,128,128]{4,3,2,1,0:T(8,128)(2,1)S(1)}, bf16[4,1,6,128,128]{4,3,2,1,0:T(8,128)(2,1)}, u32[]{:S(2)}) %copy-start.5) | copy-done | bytes 786456
  5.8 0.8 %dynamic-slice_bitcast_fusion = (bf16[6,128,128]{2,1,0:T(8,128)(2,1)S(1)}, bf16[6,128,128]{2,1,0:T(8,128)(2,1)}, bf16[6,128,128]{2,1,0:T(8,128)(2,1)S(1)}, bf16[6,128,128]{2,1,0:T(8,128)(2,1)}) fusion(bf16[4,1,6,128,128]{4,3,2,1,0:T(8,128)(2,1)S(1)} %copy-done.5, s32[]{:T(128)S(6)} %select_n.20, s32[]{:T(128)S(6)} %select_n.18, s32[]{:T(128)S(6)} %select_n.17, ...), kind=kLoop, calls=%fused_computation.4 | loop fusion | bytes 1572880 | tf_op jit(solution)/shard_map/jit(dynamic_index_in_dim)/squeeze | solution.py:445
  6.6 3.1 %collective-permute-done.own = bf16[1280,128]{1,0:T(8,128)(2,1)S(1)} collective-permute-done((bf16[1280,128]{1,0:T(8,128)(2,1)S(1)}, bf16[1280,128]{1,0:T(8,128)(2,1)S(1)}, u32[]{:S(2)}, u32[]{:S(2)}) %collective-permute-start) | collective-permute-done | bytes 327712 | tf_op jit(solution)/shard_map/ppermute | solution.py:430
  9.7 3.1 %collective-permute-start.1 = (bf16[1280,128]{1,0:T(8,128)(2,1)S(1)}, bf16[1280,128]{1,0:T(8,128)(2,1)S(1)}, u32[]{:S(2)}, u32[]{:S(2)}) collective-permute-start(bf16[1280,128]{1,0:T(8,128)(2,1)S(1)} %collective-permute-done.own), channel_id=1, source_target_pairs={{0,4},{4,12},{12,8},{8,0},{1,5},{5,13},{13,9},{9,1},{2,6},{6,14},{... | collective-permute-start | bytes 983048 | tf_op jit(solution)/shard_map/ppermute | solution.py:430
  12.8 1.2 %collective-permute-start.2 = (bf16[1280,128]{1,0:T(8,128)(2,1)S(1)}, bf16[1280,128]{1,0:T(8,128)(2,1)S(1)}, u32[]{:S(2)}, u32[]{:S(2)}) collective-permute-start(bf16[1280,128]{1,0:T(8,128)(2,1)S(1)} %collective-permute-done.own), channel_id=1, source_target_pairs={{0,16},{16,0},{1,17},{17,1},{2,18},{18,2},{3,19},{19,3},{4,20},{20... | collective-permute-start | bytes 983048 | tf_op jit(solution)/shard_map/ppermute | solution.py:426
  14.1 1.2 %collective-permute-start.3 = (bf16[1280,128]{1,0:T(8,128)(2,1)S(1)}, bf16[1280,128]{1,0:T(8,128)(2,1)S(1)}, u32[]{:S(2)}, u32[]{:S(2)}) collective-permute-start(bf16[1280,128]{1,0:T(8,128)(2,1)S(1)} %collective-permute-done.own), channel_id=1, source_target_pairs={{0,2},{2,0},{1,3},{3,1},{4,6},{6,4},{5,7},{7,5},{8,10},{10,8},{9,1... | collective-permute-start | bytes 983048 | tf_op jit(solution)/shard_map/ppermute | solution.py:422
  15.4 2.7 %make_plan.1 = (s32[7,24]{1,0:T(8,128)S(1)}, f32[1,1024]{1,0:T(1,128)S(1)}, f32[1024,128]{1,0:T(8,128)S(1)}) custom-call(s32[1,24,2]{2,1,0:T(8,128)S(1)} %copy.9.listed, s32[2,12]{1,0:T(2,128)S(1)} %copy-done.3, s32[1,2]{1,0:T(1,128)S(1)} %copy-done.4, f32[400]{0:T(512)S(1)} %copy-done.2, f32[1,2048]{1,0:T(1,128)S(1)} %bitcast.9), custom_call_target="tpu_custom_call" | custom-call | bytes 2097152 | tf_op jit(solution)/shard_map/make_plan/pallas_call | solution.py:77
  18.3 1.9 %collective-permute-done.2.by_y = bf16[1280,128]{1,0:T(8,128)(2,1)S(1)} collective-permute-done((bf16[1280,128]{1,0:T(8,128)(2,1)S(1)}, bf16[1280,128]{1,0:T(8,128)(2,1)S(1)}, u32[]{:S(2)}, u32[]{:S(2)}) %collective-permute-start.2) | collective-permute-done | bytes 327712 | tf_op jit(solution)/shard_map/ppermute | solution.py:426
  20.2 1.0 %collective-permute-done.3.by_x = bf16[1280,128]{1,0:T(8,128)(2,1)S(1)} collective-permute-done((bf16[1280,128]{1,0:T(8,128)(2,1)S(1)}, bf16[1280,128]{1,0:T(8,128)(2,1)S(1)}, u32[]{:S(2)}, u32[]{:S(2)}) %collective-permute-start.3) | collective-permute-done | bytes 327712 | tf_op jit(solution)/shard_map/ppermute | solution.py:422
  21.3 1.3 %collective-permute-start.4 = (bf16[1920,128]{1,0:T(8,128)(2,1)S(1)}, bf16[1920,128]{1,0:T(8,128)(2,1)S(1)}, u32[]{:S(2)}, u32[]{:S(2)}) collective-permute-start(bf16[1920,128]{1,0:T(8,128)(2,1)S(1)} %get-tuple-element.86), channel_id=1, source_target_pairs={{0,2},{2,0},{1,3},{3,1},{4,6},{6,4},{5,7},{7,5},{8,10},{10,8},{9,1... | collective-permute-start | bytes 1474568 | tf_op jit(solution)/shard_map/ppermute | solution.py:422
  22.9 1.2 %collective-permute-start.6 = (bf16[1280,128]{1,0:T(8,128)(2,1)S(1)}, bf16[1280,128]{1,0:T(8,128)(2,1)S(1)}, u32[]{:S(2)}, u32[]{:S(2)}) collective-permute-start(bf16[1280,128]{1,0:T(8,128)(2,1)S(1)} %collective-permute-done.1.own), channel_id=1, source_target_pairs={{0,4},{4,12},{12,8},{8,0},{1,5},{5,13},{13,9},{9,1},{2,6},{6,14},{... | collective-permute-start | bytes 983048 | tf_op jit(solution)/shard_map/ppermute | solution.py:430
  24.1 8.7 %collective-permute-done.7.refs_2_ = bf16[6,128,128]{2,1,0:T(8,128)(2,1)S(1)} collective-permute-done((bf16[6,128,128]{2,1,0:T(8,128)(2,1)S(1)}, bf16[6,128,128]{2,1,0:T(8,128)(2,1)S(1)}, u32[]{:S(2)}, u32[]{:S(2)}) %collective-permute-start.7) | collective-permute-done | bytes 196640 | tf_op jit(solution)/shard_map/ppermute | solution.py:430
  33.2 1.1 %collective-permute-start.9 = (bf16[1920,128]{1,0:T(8,128)(2,1)S(1)}, bf16[1920,128]{1,0:T(8,128)(2,1)S(1)}, u32[]{:S(2)}, u32[]{:S(2)}) collective-permute-start(bf16[1920,128]{1,0:T(8,128)(2,1)S(1)} %get-tuple-element.83), channel_id=1, source_target_pairs={{0,16},{16,0},{1,17},{17,1},{2,18},{18,2},{3,19},{19,3},{4,20},{20... | collective-permute-start | bytes 1474568 | tf_op jit(solution)/shard_map/ppermute | solution.py:426
  34.3 2.6 %collective-permute-start.11 = (bf16[6,128,128]{2,1,0:T(8,128)(2,1)S(1)}, bf16[6,128,128]{2,1,0:T(8,128)(2,1)S(1)}, u32[]{:S(2)}, u32[]{:S(2)}) collective-permute-start(bf16[6,128,128]{2,1,0:T(8,128)(2,1)S(1)} %get-tuple-element.64), channel_id=1, source_target_pairs={{0,8},{4,0},{12,4},{8,12},{1,9},{5,1},{13,5},{9,13},{2,10},{6,2},{... | collective-permute-start | bytes 589832 | tf_op jit(solution)/shard_map/ppermute | solution.py:430
  37.3 1.9 %shift_tiles.2.refs_1_ = bf16[12,144,256]{2,1,0:T(8,128)(2,1)S(1)} custom-call(s32[7,24]{1,0:T(8,128)S(1)} %get-tuple-element.50.refs_0_, bf16[6,128,128]{2,1,0:T(8,128)(2,1)S(1)} %get-tuple-element.61.refs_1_, bf16[6,128,128]{2,1,0:T(8,128)(2,1)S(1)} %collective-permute-done.7.refs_2_), custom_call_target="tpu_custom_call" | custom-call | bytes 8388608 | tf_op jit(solution)/shard_map/shift_tiles/pallas_call | solution.py:138
  39.2 9.1 %collective-permute-done.10.refs_1_ = bf16[6,128,128]{2,1,0:T(8,128)(2,1)S(1)} collective-permute-done((bf16[6,128,128]{2,1,0:T(8,128)(2,1)S(1)}, bf16[6,128,128]{2,1,0:T(8,128)(2,1)S(1)}, u32[]{:S(2)}, u32[]{:S(2)}) %collective-permute-start.10) | collective-permute-done | bytes 196640 | tf_op jit(solution)/shard_map/ppermute | solution.py:430
  48.7 1.8 %collective-permute-start.14 = (bf16[1280,512]{1,0:T(8,128)(2,1)S(1)}, bf16[1280,512]{1,0:T(8,128)(2,1)S(1)}, u32[]{:S(2)}, u32[]{:S(2)}) collective-permute-start(bf16[1280,512]{1,0:T(8,128)(2,1)S(1)} %choose.2.refs_3_), channel_id=1, source_target_pairs={{0,1},{1,0},{2,3},{3,2},{4,5},{5,4},{6,7},{7,6},{8,9},{9,8},{10,11... | collective-permute-start | bytes 3932168 | tf_op jit(solution)/shard_map/ppermute | solution.py:418
  50.6 1.3 %collective-permute-start.12 = (bf16[640,128]{1,0:T(8,128)(2,1)S(1)}, bf16[640,128]{1,0:T(8,128)(2,1)S(1)}, u32[]{:S(2)}, u32[]{:S(2)}) collective-permute-start(bf16[640,128]{1,0:T(8,128)(2,1)S(1)} %slice.22), channel_id=1, source_target_pairs={{0,2},{2,0},{1,3},{3,1},{4,6},{6,4},{5,7},{7,5},{8,10},{10,8},{9,1... | collective-permute-start | bytes 491528 | tf_op jit(solution)/shard_map/ppermute | solution.py:422
  52.2 1.9 %shift_tiles.3.refs_2_ = bf16[12,144,256]{2,1,0:T(8,128)(2,1)S(1)} custom-call(s32[7,24]{1,0:T(8,128)S(1)} %get-tuple-element.50.refs_0_, bf16[6,128,128]{2,1,0:T(8,128)(2,1)S(1)} %collective-permute-done.10.refs_1_, bf16[6,128,128]{2,1,0:T(8,128)(2,1)S(1)} %collective-permute-done.11.refs_2_), custom_call_target="tpu_custom_call" | custom-call | bytes 8388608 | tf_op jit(solution)/shard_map/shift_tiles/pallas_call | solution.py:138
  54.1 2.2 %first_product.2.middle.refs_2_ = bf16[1280,512]{1,0:T(8,128)(2,1)S(1)} custom-call(s32[7,24]{1,0:T(8,128)S(1)} %get-tuple-element.50.refs_0_, bf16[12,144,256]{2,1,0:T(8,128)(2,1)S(1)} %shift_tiles.2.refs_1_, bf16[12,144,256]{2,1,0:T(8,128)(2,1)S(1)} %shift_tiles.3.refs_2_, bf16[1280,512]{1,0:T(8,128)(2,1)S(1)} %choose.2.refs_3_, ...), custom_call_target="tpu_custom_call" | custom-call | flops 1811939328 | bytes 6291456 | tf_op jit(solution)/shard_map/first_product/pallas_call | solution.py:308
  56.5 0.9 %collective-permute-done.13.far_y = bf16[640,128]{1,0:T(8,128)(2,1)S(1)} collective-permute-done((bf16[640,128]{1,0:T(8,128)(2,1)S(1)}, bf16[640,128]{1,0:T(8,128)(2,1)S(1)}, u32[]{:S(2)}, u32[]{:S(2)}) %collective-permute-start.13) | collective-permute-done | bytes 163872 | tf_op jit(solution)/shard_map/ppermute | solution.py:426
  57.8 1.2 %collective-permute-start.15 = (bf16[1280,512]{1,0:T(8,128)(2,1)S(1)}, bf16[1280,512]{1,0:T(8,128)(2,1)S(1)}, u32[]{:S(2)}, u32[]{:S(2)}) collective-permute-start(bf16[1280,512]{1,0:T(8,128)(2,1)S(1)} %choose.3.refs_3_), channel_id=1, source_target_pairs={{0,1},{1,0},{2,3},{3,2},{4,5},{5,4},{6,7},{7,6},{8,9},{9,8},{10,11... | collective-permute-start | bytes 3932168 | tf_op jit(solution)/shard_map/ppermute | solution.py:418
  59.0 1.7 %send_product.3 = bf16[2,512,512]{2,1,0:T(8,128)(2,1)S(1)} custom-call(bf16[1280,512]{1,0:T(8,128)(2,1)S(1)} %first_product.2.middle.refs_2_, bf16[1280,512]{1,0:T(8,128)(2,1)S(1)} %stay.1.refs_0_.refs_4_, bf16[1280,512]{1,0:T(8,128)(2,1)S(1)} %assemble.3.refs_1_.refs_0_.refs_5_, bf16[1280,512]{1,0:T(8,128)(2,1)S(1)} %assemble.4.refs_2_.refs_1_.refs_6_, ...), custom_call_target="tpu_custom_call" | custom-call | flops 1342177280 | bytes 5242880 | tf_op jit(solution)/shard_map/send_product/pallas_call | solution.py:342
  60.8 0.8 %collective-permute-done.15.refs_4_ = bf16[1280,512]{1,0:T(8,128)(2,1)S(1)} collective-permute-done((bf16[1280,512]{1,0:T(8,128)(2,1)S(1)}, bf16[1280,512]{1,0:T(8,128)(2,1)S(1)}, u32[]{:S(2)}, u32[]{:S(2)}) %collective-permute-start.15) | collective-permute-done | bytes 1310752 | tf_op jit(solution)/shard_map/ppermute | solution.py:418
  61.6 2.2 %first_product.3.middle.refs_2_ = bf16[1280,512]{1,0:T(8,128)(2,1)S(1)} custom-call(s32[7,24]{1,0:T(8,128)S(1)} %get-tuple-element.50.refs_0_, bf16[12,144,256]{2,1,0:T(8,128)(2,1)S(1)} %shift_tiles.2.refs_1_, bf16[12,144,256]{2,1,0:T(8,128)(2,1)S(1)} %shift_tiles.3.refs_2_, bf16[1280,512]{1,0:T(8,128)(2,1)S(1)} %choose.3.refs_3_, ...), custom_call_target="tpu_custom_call" | custom-call | flops 1811939328 | bytes 6291456 | tf_op jit(solution)/shard_map/first_product/pallas_call | solution.py:308
  63.8 1.8 %send_product.2 = bf16[2,512,512]{2,1,0:T(8,128)(2,1)S(1)} custom-call(bf16[1280,512]{1,0:T(8,128)(2,1)S(1)} %first_product.3.middle.refs_2_, bf16[1280,512]{1,0:T(8,128)(2,1)S(1)} %stay.1.refs_0_.refs_4_, bf16[1280,512]{1,0:T(8,128)(2,1)S(1)} %assemble.3.refs_1_.refs_0_.refs_5_, bf16[1280,512]{1,0:T(8,128)(2,1)S(1)} %assemble.4.refs_2_.refs_1_.refs_6_, ...), custom_call_target="tpu_custom_call" | custom-call | flops 1342177280 | bytes 5242880 | tf_op jit(solution)/shard_map/send_product/pallas_call | solution.py:342
  65.6 0.4 collective-permute-start.16
  66.0 2.8 %keep_product.2.refs_8_ = bf16[1,1024,1024]{2,1,0:T(8,128)(2,1)} custom-call(f32[1,1024]{1,0:T(1,128)S(1)} %get-tuple-element.42.refs_0_, f32[1024,128]{1,0:T(8,128)S(1)} %get-tuple-element.43.refs_1_, bf16[1280,512]{1,0:T(8,128)(2,1)S(1)} %first_product.2.middle.refs_2_, bf16[2,512,512]{2,1,0:T(8,128)(2,1)S(1)} %collective-permute-done.17.refs_3_, ...), custom_call_target="tpu_custom_call" | custom-call | flops 1342177280 | bytes 6291456 | tf_op jit(solution)/shard_map/keep_product/pallas_call | solution.py:394
  68.8 2.6 %keep_product.3 = bf16[1,1024,1024]{2,1,0:T(8,128)(2,1)} custom-call(f32[1,1024]{1,0:T(1,128)S(1)} %get-tuple-element.42.refs_0_, f32[1024,128]{1,0:T(8,128)S(1)} %get-tuple-element.43.refs_1_, bf16[1280,512]{1,0:T(8,128)(2,1)S(1)} %first_product.3.middle.refs_2_, ...), custom_call_target="tpu_custom_call", output_to_operand_aliasing={{}: (8, {})} | custom-call | flops 1342177280 | bytes 6291456 | tf_op jit(solution)/shard_map/keep_product/pallas_call | solution.py:394
  (48 shorter events, 2.9 us)
Async XLA Ops:
  1.0 8.7 %collective-permute-start = (bf16[1280,128]{1,0:T(8,128)(2,1)S(1)}, bf16[1280,128]{1,0:T(8,128)(2,1)S(1)}, u32[]{:S(2)}, u32[]{:S(2)}) collective-permute-start(bf16[1280,128]{1,0:T(8,128)(2,1)S(1)} %constant_dynamic-slice_fusion), channel_id=1, source_target_pairs={{0,4},{4,12},{12,8},{8,0},{1,5},{5,13},{13,9},{9,1},{2,6},{6,14},{... | collective-permute-start | bytes 983048 | tf_op jit(solution)/shard_map/ppermute | solution.py:430
  3.4 1.3 %copy-start = (bf16[1280,512]{1,0:T(8,128)(2,1)S(1)}, bf16[1280,512]{1,0:T(8,128)(2,1)}, u32[]{:S(2)}) copy-start(bf16[1280,512]{1,0:T(8,128)(2,1)} %value.1) | copy-start | bytes 3932164
  4.7 1.1 %copy-start.5 = (bf16[4,1,6,128,128]{4,3,2,1,0:T(8,128)(2,1)S(1)}, bf16[4,1,6,128,128]{4,3,2,1,0:T(8,128)(2,1)}, u32[]{:S(2)}) copy-start(bf16[4,1,6,128,128]{4,3,2,1,0:T(8,128)(2,1)} %param.7) | copy-start | bytes 2359300
  4.8 10.5 %copy-start.8 = (s32[1,24,2]{1,2,0:T(2,128)S(1)}, s32[1,24,2]{1,2,0:T(2,128)}, u32[]{:S(2)}) copy-start(s32[1,24,2]{1,2,0:T(2,128)} %param.12) | copy-start | bytes 580
  4.8 10.6 %copy-start.1 = (f32[2048]{0:T(1024)S(1)}, f32[2048]{0:T(1024)}, u32[]{:S(2)}) copy-start(f32[2048]{0:T(1024)} %param.10) | copy-start | bytes 24580
  4.8 10.6 %copy-start.2 = (f32[400]{0:T(512)S(1)}, f32[400]{0:T(512)}, u32[]{:S(2)}) copy-start(f32[400]{0:T(512)} %eps_occ.1) | copy-start | bytes 4804
  4.8 10.6 %copy-start.3 = (s32[2,12]{1,0:T(2,128)S(1)}, s32[2,12]{1,0:T(2,128)}, u32[]{:S(2)}) copy-start(s32[2,12]{1,0:T(2,128)} %extra.1) | copy-start | bytes 292
  4.8 10.6 %copy-start.4 = (s32[1,2]{1,0:T(1,128)S(1)}, s32[1,2]{1,0:T(1,128)}, u32[]{:S(2)}) copy-start(s32[1,2]{1,0:T(1,128)} %pair_occ.1) | copy-start | bytes 28
  9.7 8.6 %collective-permute-start.1 = (bf16[1280,128]{1,0:T(8,128)(2,1)S(1)}, bf16[1280,128]{1,0:T(8,128)(2,1)S(1)}, u32[]{:S(2)}, u32[]{:S(2)}) collective-permute-start(bf16[1280,128]{1,0:T(8,128)(2,1)S(1)} %collective-permute-done.own), channel_id=1, source_target_pairs={{0,4},{4,12},{12,8},{8,0},{1,5},{5,13},{13,9},{9,1},{2,6},{6,14},{... | collective-permute-start | bytes 983048 | tf_op jit(solution)/shard_map/ppermute | solution.py:430
  12.8 7.4 %collective-permute-start.2 = (bf16[1280,128]{1,0:T(8,128)(2,1)S(1)}, bf16[1280,128]{1,0:T(8,128)(2,1)S(1)}, u32[]{:S(2)}, u32[]{:S(2)}) collective-permute-start(bf16[1280,128]{1,0:T(8,128)(2,1)S(1)} %collective-permute-done.own), channel_id=1, source_target_pairs={{0,16},{16,0},{1,17},{17,1},{2,18},{18,2},{3,19},{19,3},{4,20},{20... | collective-permute-start | bytes 983048 | tf_op jit(solution)/shard_map/ppermute | solution.py:426
  14.1 7.1 %collective-permute-start.3 = (bf16[1280,128]{1,0:T(8,128)(2,1)S(1)}, bf16[1280,128]{1,0:T(8,128)(2,1)S(1)}, u32[]{:S(2)}, u32[]{:S(2)}) collective-permute-start(bf16[1280,128]{1,0:T(8,128)(2,1)S(1)} %collective-permute-done.own), channel_id=1, source_target_pairs={{0,2},{2,0},{1,3},{3,1},{4,6},{6,4},{5,7},{7,5},{8,10},{10,8},{9,1... | collective-permute-start | bytes 983048 | tf_op jit(solution)/shard_map/ppermute | solution.py:422
  15.4 8.7 %copy-start.7 = (bf16[6,128,128]{2,1,0:T(8,128)(2,1)S(1)}, bf16[6,128,128]{2,1,0:T(8,128)(2,1)}, u32[]{:S(2)}) copy-start(bf16[6,128,128]{2,1,0:T(8,128)(2,1)} %get-tuple-element.54) | copy-start | bytes 589828
  21.3 13.0 %copy-start.6 = (bf16[6,128,128]{2,1,0:T(8,128)(2,1)S(1)}, bf16[6,128,128]{2,1,0:T(8,128)(2,1)}, u32[]{:S(2)}) copy-start(bf16[6,128,128]{2,1,0:T(8,128)(2,1)} %get-tuple-element.63) | copy-start | bytes 589828
  21.3 11.5 %collective-permute-start.4 = (bf16[1920,128]{1,0:T(8,128)(2,1)S(1)}, bf16[1920,128]{1,0:T(8,128)(2,1)S(1)}, u32[]{:S(2)}, u32[]{:S(2)}) collective-permute-start(bf16[1920,128]{1,0:T(8,128)(2,1)S(1)} %get-tuple-element.86), channel_id=1, source_target_pairs={{0,2},{2,0},{1,3},{3,1},{4,6},{6,4},{5,7},{7,5},{8,10},{10,8},{9,1... | collective-permute-start | bytes 1474568 | tf_op jit(solution)/shard_map/ppermute | solution.py:422
  22.6 10.2 %collective-permute-start.5 = (bf16[1920,128]{1,0:T(8,128)(2,1)S(1)}, bf16[1920,128]{1,0:T(8,128)(2,1)S(1)}, u32[]{:S(2)}, u32[]{:S(2)}) collective-permute-start(bf16[1920,128]{1,0:T(8,128)(2,1)S(1)} %get-tuple-element.85), channel_id=1, source_target_pairs={{0,16},{16,0},{1,17},{17,1},{2,18},{18,2},{3,19},{19,3},{4,20},{20... | collective-permute-start | bytes 1474568 | tf_op jit(solution)/shard_map/ppermute | solution.py:426
  22.9 9.9 %collective-permute-start.6 = (bf16[1280,128]{1,0:T(8,128)(2,1)S(1)}, bf16[1280,128]{1,0:T(8,128)(2,1)S(1)}, u32[]{:S(2)}, u32[]{:S(2)}) collective-permute-start(bf16[1280,128]{1,0:T(8,128)(2,1)S(1)} %collective-permute-done.1.own), channel_id=1, source_target_pairs={{0,4},{4,12},{12,8},{8,0},{1,5},{5,13},{13,9},{9,1},{2,6},{6,14},{... | collective-permute-start | bytes 983048 | tf_op jit(solution)/shard_map/ppermute | solution.py:430
  24.0 8.7 %collective-permute-start.7 = (bf16[6,128,128]{2,1,0:T(8,128)(2,1)S(1)}, bf16[6,128,128]{2,1,0:T(8,128)(2,1)S(1)}, u32[]{:S(2)}, u32[]{:S(2)}) collective-permute-start(bf16[6,128,128]{2,1,0:T(8,128)(2,1)S(1)} %copy-done.7), channel_id=1, source_target_pairs={{0,4},{4,12},{12,8},{8,0},{1,5},{5,13},{13,9},{9,1},{2,6},{6,14},{... | collective-permute-start | bytes 589832 | tf_op jit(solution)/shard_map/ppermute | solution.py:430
  32.9 15.4 %collective-permute-start.8 = (bf16[1920,128]{1,0:T(8,128)(2,1)S(1)}, bf16[1920,128]{1,0:T(8,128)(2,1)S(1)}, u32[]{:S(2)}, u32[]{:S(2)}) collective-permute-start(bf16[1920,128]{1,0:T(8,128)(2,1)S(1)} %get-tuple-element.84), channel_id=1, source_target_pairs={{0,2},{2,0},{1,3},{3,1},{4,6},{6,4},{5,7},{7,5},{8,10},{10,8},{9,1... | collective-permute-start | bytes 1474568 | tf_op jit(solution)/shard_map/ppermute | solution.py:422
  33.2 15.1 %collective-permute-start.9 = (bf16[1920,128]{1,0:T(8,128)(2,1)S(1)}, bf16[1920,128]{1,0:T(8,128)(2,1)S(1)}, u32[]{:S(2)}, u32[]{:S(2)}) collective-permute-start(bf16[1920,128]{1,0:T(8,128)(2,1)S(1)} %get-tuple-element.83), channel_id=1, source_target_pairs={{0,16},{16,0},{1,17},{17,1},{2,18},{18,2},{3,19},{19,3},{4,20},{20... | collective-permute-start | bytes 1474568 | tf_op jit(solution)/shard_map/ppermute | solution.py:426
  34.3 14.0 %collective-permute-start.10 = (bf16[6,128,128]{2,1,0:T(8,128)(2,1)S(1)}, bf16[6,128,128]{2,1,0:T(8,128)(2,1)S(1)}, u32[]{:S(2)}, u32[]{:S(2)}) collective-permute-start(bf16[6,128,128]{2,1,0:T(8,128)(2,1)S(1)} %copy-done.6), channel_id=1, source_target_pairs={{0,12},{4,8},{12,0},{8,4},{1,13},{5,9},{13,1},{9,5},{2,14},{6,10},... | collective-permute-start | bytes 589832 | tf_op jit(solution)/shard_map/ppermute | solution.py:430
  34.3 14.0 %collective-permute-start.11 = (bf16[6,128,128]{2,1,0:T(8,128)(2,1)S(1)}, bf16[6,128,128]{2,1,0:T(8,128)(2,1)S(1)}, u32[]{:S(2)}, u32[]{:S(2)}) collective-permute-start(bf16[6,128,128]{2,1,0:T(8,128)(2,1)S(1)} %get-tuple-element.64), channel_id=1, source_target_pairs={{0,8},{4,0},{12,4},{8,12},{1,9},{5,1},{13,5},{9,13},{2,10},{6,2},{... | collective-permute-start | bytes 589832 | tf_op jit(solution)/shard_map/ppermute | solution.py:430
  48.7 5.4 %collective-permute-start.14 = (bf16[1280,512]{1,0:T(8,128)(2,1)S(1)}, bf16[1280,512]{1,0:T(8,128)(2,1)S(1)}, u32[]{:S(2)}, u32[]{:S(2)}) collective-permute-start(bf16[1280,512]{1,0:T(8,128)(2,1)S(1)} %choose.2.refs_3_), channel_id=1, source_target_pairs={{0,1},{1,0},{2,3},{3,2},{4,5},{5,4},{6,7},{7,6},{8,9},{9,8},{10,11... | collective-permute-start | bytes 3932168 | tf_op jit(solution)/shard_map/ppermute | solution.py:418
  50.6 5.9 %collective-permute-start.12 = (bf16[640,128]{1,0:T(8,128)(2,1)S(1)}, bf16[640,128]{1,0:T(8,128)(2,1)S(1)}, u32[]{:S(2)}, u32[]{:S(2)}) collective-permute-start(bf16[640,128]{1,0:T(8,128)(2,1)S(1)} %slice.22), channel_id=1, source_target_pairs={{0,2},{2,0},{1,3},{3,1},{4,6},{6,4},{5,7},{7,5},{8,10},{10,8},{9,1... | collective-permute-start | bytes 491528 | tf_op jit(solution)/shard_map/ppermute | solution.py:422
  51.9 5.5 %collective-permute-start.13 = (bf16[640,128]{1,0:T(8,128)(2,1)S(1)}, bf16[640,128]{1,0:T(8,128)(2,1)S(1)}, u32[]{:S(2)}, u32[]{:S(2)}) collective-permute-start(bf16[640,128]{1,0:T(8,128)(2,1)S(1)} %slice.23), channel_id=1, source_target_pairs={{0,16},{16,0},{1,17},{17,1},{2,18},{18,2},{3,19},{19,3},{4,20},{20... | collective-permute-start | bytes 491528 | tf_op jit(solution)/shard_map/ppermute | solution.py:426
  57.8 3.8 %collective-permute-start.15 = (bf16[1280,512]{1,0:T(8,128)(2,1)S(1)}, bf16[1280,512]{1,0:T(8,128)(2,1)S(1)}, u32[]{:S(2)}, u32[]{:S(2)}) collective-permute-start(bf16[1280,512]{1,0:T(8,128)(2,1)S(1)} %choose.3.refs_3_), channel_id=1, source_target_pairs={{0,1},{1,0},{2,3},{3,2},{4,5},{5,4},{6,7},{7,6},{8,9},{9,8},{10,11... | collective-permute-start | bytes 3932168 | tf_op jit(solution)/shard_map/ppermute | solution.py:418
  60.7 5.3 %collective-permute-start.17 = (bf16[2,512,512]{2,1,0:T(8,128)(2,1)S(1)}, bf16[2,512,512]{2,1,0:T(8,128)(2,1)S(1)}, u32[]{:S(2)}, u32[]{:S(2)}) collective-permute-start(bf16[2,512,512]{2,1,0:T(8,128)(2,1)S(1)} %send_product.3), channel_id=1, source_target_pairs={{0,1},{1,0},{2,3},{3,2},{4,5},{5,4},{6,7},{7,6},{8,9},{9,8},{10,11... | collective-permute-start | bytes 3145736 | tf_op jit(solution)/shard_map/ppermute | solution.py:418
  65.6 3.2 %collective-permute-start.16 = (bf16[2,512,512]{2,1,0:T(8,128)(2,1)S(1)}, bf16[2,512,512]{2,1,0:T(8,128)(2,1)S(1)}, u32[]{:S(2)}, u32[]{:S(2)}) collective-permute-start(bf16[2,512,512]{2,1,0:T(8,128)(2,1)S(1)} %send_product.2), channel_id=1, source_target_pairs={{0,1},{1,0},{2,3},{3,2},{4,5},{5,4},{6,7},{7,6},{8,9},{9,8},{10,11... | collective-permute-start | bytes 3145736 | tf_op jit(solution)/shard_map/ppermute | solution.py:418

commit v7 on v6

--- a/solution.py
+++ b/solution.py
@@ -14,6 +14,7 @@
 COLS_WIN = 256
 GROUPS = 4
 UNROLL = 12
+STORES = 2
 SHIFT_UNROLL = 6
 RING = (0, 1, 3, 2)
 SWAP = ((0, 1), (1, 0))
@@ -321,9 +322,7 @@
     return result[0], [*shifted, *result[1:]]
 
 
-def send_kernel(ringed, middle, *refs):
-    groups = refs[:GROUPS]
-    out, held = refs[GROUPS:]
+def send_body(ringed, middle, groups, out, held):
     mine = GROUPS // 2
     for i in range(mine):
         wanted = (1 - lax.axis_index("rep")) * mine + i
@@ -333,6 +332,45 @@
         out[i] = lax.dot_general(
             held[i], middle[...], dims, preferred_element_type=F32
         ).astype(BF16)
+
+
+def send_kernel(ringed, middle, *refs):
+    send_body(ringed, middle, refs[:GROUPS], *refs[GROUPS:])
+
+
+def first_and_send_kernel(n_shifted, which, blocks, plan, *refs):
+    tiles, refs = refs[:n_shifted], refs[n_shifted:]
+    own, other, groups = refs[0], refs[1], refs[2 : 2 + GROUPS]
+    out, sent, held, total, left = refs[2 + GROUPS :]
+    first_kernel(1, n_shifted, 0, which, blocks, plan, *tiles, own, other, out, held, total)
+    send_body(blocks > 1, out, groups, sent, left)
+
+
+def first_and_send(plan, shifted, own, other, which, blocks, groups):
+    rows, width = own.shape
+    mine = GROUPS // 2
+    left = groups[0].shape[1]
+    n_tiles = plan.shape[1]
+    return pl.pallas_call(
+        functools.partial(first_and_send_kernel, len(shifted), which, blocks),
+        out_shape=(
+            jax.ShapeDtypeStruct((rows, width), BF16),
+            jax.ShapeDtypeStruct((mine, left, width), BF16),
+        ),
+        in_specs=[SMEM] + [VMEM] * (len(shifted) + 2 + GROUPS),
+        out_specs=(VMEM, VMEM),
+        scratch_shapes=[
+            pltpu.VMEM((2, rows, width), BF16),
+            pltpu.VMEM((rows + TILE, width), F32),
+            pltpu.VMEM((mine, rows, left), BF16),
+        ],
+        compiler_params=pltpu.CompilerParams(vmem_limit_bytes=20 * MIB),
+        cost_estimate=pl.CostEstimate(
+            flops=n_tiles * 4 * ROWS_WIN * COLS_WIN * width + 2 * mine * rows * left * width,
+            bytes_accessed=10 * MIB, transcendentals=0,
+        ),
+        name="first_and_send",
+    )(plan, *shifted, own, other, *groups)
 
 
 def send_product(middle, groups, ringed):
@@ -353,16 +391,20 @@
     )(middle, *groups)
 
 
-def keep_kernel(which, blocks, n_before, *refs):
+def keep_kernel(which, blocks, n_groups, n_before, *refs):
     by_col, by_row, middle, got = refs[:4]
-    groups = refs[4 : 4 + GROUPS]
-    out, held, ready, out_sems = refs[4 + GROUPS + n_before :]
+    groups = refs[4 : 4 + n_groups]
     mine = GROUPS // 2
+    if n_groups == 1:
+        held = groups[0]
+        out, ready, out_sems = refs[4 + n_groups + n_before :]
+    else:
+        out, held, ready, out_sems = refs[4 + n_groups + n_before :]
+        for i in range(mine):
+            wanted = lax.axis_index("rep") * mine + i
+            pick(ring_slot(wanted) if blocks > 1 else wanted, 0, groups, held.at[i])
     width = held.shape[2]
     columns = middle.shape[1]
-    for i in range(mine):
-        wanted = lax.axis_index("rep") * mine + i
-        pick(ring_slot(wanted) if blocks > 1 else wanted, 0, groups, held.at[i])
     if blocks > 1:
         block = column_block(which, blocks) - lax.axis_index("vir") * blocks
         column = pl.multiple_of(block * columns, LANES)
@@ -370,36 +412,44 @@
         column = 0
     dims = (((0,), (0,)), ((), ()))
     stores = []
+    part = width // STORES
     for i in range(mine):
-        total = lax.dot_general(held[i], middle[...], dims, preferred_element_type=F32)
-        total += got[i].astype(F32)
-        tall = by_row[i * width : (i + 1) * width, :]
-        tall = jnp.concatenate([tall] * (columns // LANES), axis=1)
-        ready[i] = (total / (by_col[:, pl.ds(column, columns)] - tall)).astype(BF16)
-        store = pltpu.make_async_copy(
-            ready.at[i], out.at[0, pl.ds(i * width, width), pl.ds(column, columns)], out_sems.at[i]
-        )
-        store.start()
-        stores.append(store)
+        for q in range(STORES):
+            some = slice(q * part, (q + 1) * part)
+            total = lax.dot_general(held[i, :, some], middle[...], dims, preferred_element_type=F32)
+            total += got[i, some].astype(F32)
+            row = i * width + q * part
+            tall = by_row[row : row + part, :]
+            tall = jnp.concatenate([tall] * (columns // LANES), axis=1)
+            ready[i, some] = (total / (by_col[:, pl.ds(column, columns)] - tall)).astype(BF16)
+            store = pltpu.make_async_copy(
+                ready.at[i, some], out.at[0, pl.ds(row, part), pl.ds(column, columns)],
+                out_sems.at[i * STORES + q],
+            )
+            store.start()
+            stores.append(store)
     for store in stores:
         store.wait()
 
 
 def keep_product(which, blocks, energies, middle, got, groups, before):
-    rows, width = groups[0].shape
-    columns = middle.shape[1]
-    mine = GROUPS // 2
+    rows, columns = middle.shape
+    mine, width, _ = got.shape
     extra = [] if before is None else [before]
     fixed = [*energies, middle, got, *groups]
-    return pl.pallas_call(
-        functools.partial(keep_kernel, which, blocks, len(extra)),
-        out_shape=jax.ShapeDtypeStruct((1, mine * width, blocks * columns), BF16),
+    out_shape = [jax.ShapeDtypeStruct((1, mine * width, blocks * columns), BF16)]
+    out_specs = [ANY]
+    if len(groups) > 1:
+        out_shape.append(jax.ShapeDtypeStruct((mine, rows, width), BF16))
+        out_specs.append(VMEM)
+    result = pl.pallas_call(
+        functools.partial(keep_kernel, which, blocks, len(groups), len(extra)),
+        out_shape=out_shape,
         in_specs=[VMEM] * len(fixed) + [ANY] * len(extra),
-        out_specs=ANY,
+        out_specs=out_specs,
         scratch_shapes=[
-            pltpu.VMEM((mine, rows, width), BF16),
             pltpu.VMEM((mine, width, columns), BF16),
-            pltpu.SemaphoreType.DMA((mine,)),
+            pltpu.SemaphoreType.DMA((mine * STORES,)),
         ],
         input_output_aliases={len(fixed): 0} if extra else {},
         compiler_params=pltpu.CompilerParams(vmem_limit_bytes=14 * MIB),
@@ -408,6 +458,7 @@
         ),
         name="keep_product",
     )(*fixed, *extra)
+    return result[0], [*result[1:]] or groups
 
 
 def ring_pairs(distance):
@@ -501,15 +552,19 @@
     for which in range(blocks):
         if ringed and which == 0:
             middle = early_middle
+            sent = send_product(middle, groups, ringed)
         else:
-            middle, shifted = first_product(plan, shifted, [], own, other, which, blocks)
-        sent = send_product(middle, groups, ringed)
+            middle, sent = first_and_send(
+                plan, shifted, own[0], other[0], which, blocks, groups
+            )
         middle, sent = lax.optimization_barrier((middle, sent))
         middles.append(middle)
         got.append(other_core(sent))
     out = None
     for which in range(blocks):
-        out = keep_product(which, blocks, energies, middles[which], got[which], groups, out)
+        out, groups = keep_product(
+            which, blocks, energies, middles[which], got[which], groups, out
+        )
     return out
 
 

time: 71.8 us -> 71.5 us (level)
    pallas_call x2 -> x3, Pallas kernels: 5.41 us -> 8.99 us  [the longest x2 5.05 us: keep_product(): pl.pallas_call(functools.partial(keep_kernel, which, blocks, len(groups),...]
    pallas_call x2 -> x1, Pallas kernels: 4.36 us -> 2.2 us  [first_product(): pl.pallas_call(functools.partial(first_kernel, len(own), len(shifted), le...]
    pallas_call x2 -> x1, Pallas kernels: 3.49 us -> 1.73 us  [send_product(): pl.pallas_call(functools.partial(send_kernel, ringed), out_shape=jax.Shap...]
where the time goes in v7:
time: 71.5 us; the launch traced here: 71.3 us
  waiting for transfers between devices  25.8 us (36%)
  Pallas kernels  20.6 us (29%)
  starting transfers between devices  20 us (28%)
  local copies, waits for them, and re-layouts  4.28 us (6%)
    ppermute x6, waiting for transfers between devices, to_z(): return lax.ppermute(value, 'ao', ring_pairs(distance))  21.1 us
    ppermute x6, starting transfers between devices, to_z(): return lax.ppermute(value, 'ao', ring_pairs(distance))  9.32 us
    pallas_call x2, Pallas kernels, keep_product(): pl.pallas_call(functools.partial(keep_kernel, which, blocks, len(groups),...  5.05 us
    ppermute x4, starting transfers between devices, to_x(): return lax.ppermute(value, 'vir', SWAP)  4.08 us
    pallas_call x1, Pallas kernels, first_and_send(): pl.pallas_call(functools.partial(first_and_send_kernel, len(shifted), whi...  3.94 us
    pallas_call x2, Pallas kernels, shift_tiles(): pl.pallas_call(functools.partial(shift_kernel, first, len(tiles)), out_sh...  3.83 us
    ppermute x4, starting transfers between devices, other_core(): return lax.ppermute(value, 'rep', SWAP)  3.58 us
    ppermute x4, starting transfers between devices, to_y(): return lax.ppermute(value, 'grp', SWAP)  2.99 us
  transfers between devices with their start and end apart: 18, of which 9 were waited for; matrix products, arithmetic and copies ran while one was open for 1% of the time, Pallas kernels for 25%

profile of v7, /device:TPU:9, one launch (start us, length us, event | category | flops | bytes accessed | tf_op | source)
XLA Modules:
  0.0 71.3 jit_solution(1520697548573479005)
XLA Ops:
  0.0 1.0 %constant_dynamic-slice_fusion = bf16[1280,128]{1,0:T(8,128)(2,1)S(1)} fusion(bf16[1280,512]{1,0:T(8,128)(2,1)} %value.1, s32[]{:T(128)S(6)} %select_n.16), kind=kLoop, calls=%fused_computation.8 | loop fusion | bytes 655364 | tf_op jit(solution)/shard_map/dynamic_slice | solution.py:494
  1.0 2.4 %collective-permute-start = (bf16[1280,128]{1,0:T(8,128)(2,1)S(1)}, bf16[1280,128]{1,0:T(8,128)(2,1)S(1)}, u32[]{:S(2)}, u32[]{:S(2)}) collective-permute-start(bf16[1280,128]{1,0:T(8,128)(2,1)S(1)} %constant_dynamic-slice_fusion), channel_id=1, source_target_pairs={{0,4},{4,12},{12,8},{8,0},{1,5},{5,13},{13,9},{9,1},{2,6},{6,14},{... | collective-permute-start | bytes 983048 | tf_op jit(solution)/shard_map/ppermute | solution.py:481
  3.4 1.3 %copy-done = bf16[1280,512]{1,0:T(8,128)(2,1)S(1)} copy-done((bf16[1280,512]{1,0:T(8,128)(2,1)S(1)}, bf16[1280,512]{1,0:T(8,128)(2,1)}, u32[]{:S(2)}) %copy-start) | copy-done | bytes 1310744
  4.8 1.0 %copy-done.5 = bf16[4,1,6,128,128]{4,3,2,1,0:T(8,128)(2,1)S(1)} copy-done((bf16[4,1,6,128,128]{4,3,2,1,0:T(8,128)(2,1)S(1)}, bf16[4,1,6,128,128]{4,3,2,1,0:T(8,128)(2,1)}, u32[]{:S(2)}) %copy-start.5) | copy-done | bytes 786456
  5.8 0.8 %dynamic-slice_bitcast_fusion = (bf16[6,128,128]{2,1,0:T(8,128)(2,1)S(1)}, bf16[6,128,128]{2,1,0:T(8,128)(2,1)}, bf16[6,128,128]{2,1,0:T(8,128)(2,1)S(1)}, bf16[6,128,128]{2,1,0:T(8,128)(2,1)}) fusion(bf16[4,1,6,128,128]{4,3,2,1,0:T(8,128)(2,1)S(1)} %copy-done.5, s32[]{:T(128)S(6)} %select_n.20, s32[]{:T(128)S(6)} %select_n.18, s32[]{:T(128)S(6)} %select_n.17, ...), kind=kLoop, calls=%fused_computation.4 | loop fusion | bytes 1572880 | tf_op jit(solution)/shard_map/jit(dynamic_index_in_dim)/squeeze | solution.py:496
  6.6 3.1 %collective-permute-done.own = bf16[1280,128]{1,0:T(8,128)(2,1)S(1)} collective-permute-done((bf16[1280,128]{1,0:T(8,128)(2,1)S(1)}, bf16[1280,128]{1,0:T(8,128)(2,1)S(1)}, u32[]{:S(2)}, u32[]{:S(2)}) %collective-permute-start) | collective-permute-done | bytes 327712 | tf_op jit(solution)/shard_map/ppermute | solution.py:481
  9.7 3.1 %collective-permute-start.1 = (bf16[1280,128]{1,0:T(8,128)(2,1)S(1)}, bf16[1280,128]{1,0:T(8,128)(2,1)S(1)}, u32[]{:S(2)}, u32[]{:S(2)}) collective-permute-start(bf16[1280,128]{1,0:T(8,128)(2,1)S(1)} %collective-permute-done.own), channel_id=1, source_target_pairs={{0,4},{4,12},{12,8},{8,0},{1,5},{5,13},{13,9},{9,1},{2,6},{6,14},{... | collective-permute-start | bytes 983048 | tf_op jit(solution)/shard_map/ppermute | solution.py:481
  12.8 1.2 %collective-permute-start.2 = (bf16[1280,128]{1,0:T(8,128)(2,1)S(1)}, bf16[1280,128]{1,0:T(8,128)(2,1)S(1)}, u32[]{:S(2)}, u32[]{:S(2)}) collective-permute-start(bf16[1280,128]{1,0:T(8,128)(2,1)S(1)} %collective-permute-done.own), channel_id=1, source_target_pairs={{0,16},{16,0},{1,17},{17,1},{2,18},{18,2},{3,19},{19,3},{4,20},{20... | collective-permute-start | bytes 983048 | tf_op jit(solution)/shard_map/ppermute | solution.py:477
  14.1 1.2 %collective-permute-start.3 = (bf16[1280,128]{1,0:T(8,128)(2,1)S(1)}, bf16[1280,128]{1,0:T(8,128)(2,1)S(1)}, u32[]{:S(2)}, u32[]{:S(2)}) collective-permute-start(bf16[1280,128]{1,0:T(8,128)(2,1)S(1)} %collective-permute-done.own), channel_id=1, source_target_pairs={{0,2},{2,0},{1,3},{3,1},{4,6},{6,4},{5,7},{7,5},{8,10},{10,8},{9,1... | collective-permute-start | bytes 983048 | tf_op jit(solution)/shard_map/ppermute | solution.py:473
  15.4 2.7 %make_plan.1 = (s32[7,24]{1,0:T(8,128)S(1)}, f32[1,1024]{1,0:T(1,128)S(1)}, f32[1024,128]{1,0:T(8,128)S(1)}) custom-call(s32[1,24,2]{2,1,0:T(8,128)S(1)} %copy.9.listed, s32[2,12]{1,0:T(2,128)S(1)} %copy-done.3, s32[1,2]{1,0:T(1,128)S(1)} %copy-done.4, f32[400]{0:T(512)S(1)} %copy-done.2, f32[1,2048]{1,0:T(1,128)S(1)} %bitcast.9), custom_call_target="tpu_custom_call" | custom-call | bytes 2097152 | tf_op jit(solution)/shard_map/make_plan/pallas_call | solution.py:78
  18.3 1.9 %collective-permute-done.2.by_y = bf16[1280,128]{1,0:T(8,128)(2,1)S(1)} collective-permute-done((bf16[1280,128]{1,0:T(8,128)(2,1)S(1)}, bf16[1280,128]{1,0:T(8,128)(2,1)S(1)}, u32[]{:S(2)}, u32[]{:S(2)}) %collective-permute-start.2) | collective-permute-done | bytes 327712 | tf_op jit(solution)/shard_map/ppermute | solution.py:477
  20.2 1.0 %collective-permute-done.3.by_x = bf16[1280,128]{1,0:T(8,128)(2,1)S(1)} collective-permute-done((bf16[1280,128]{1,0:T(8,128)(2,1)S(1)}, bf16[1280,128]{1,0:T(8,128)(2,1)S(1)}, u32[]{:S(2)}, u32[]{:S(2)}) %collective-permute-start.3) | collective-permute-done | bytes 327712 | tf_op jit(solution)/shard_map/ppermute | solution.py:473
  21.3 1.3 %collective-permute-start.4 = (bf16[1920,128]{1,0:T(8,128)(2,1)S(1)}, bf16[1920,128]{1,0:T(8,128)(2,1)S(1)}, u32[]{:S(2)}, u32[]{:S(2)}) collective-permute-start(bf16[1920,128]{1,0:T(8,128)(2,1)S(1)} %get-tuple-element.90), channel_id=1, source_target_pairs={{0,2},{2,0},{1,3},{3,1},{4,6},{6,4},{5,7},{7,5},{8,10},{10,8},{9,1... | collective-permute-start | bytes 1474568 | tf_op jit(solution)/shard_map/ppermute | solution.py:473
  22.9 1.2 %collective-permute-start.6 = (bf16[1280,128]{1,0:T(8,128)(2,1)S(1)}, bf16[1280,128]{1,0:T(8,128)(2,1)S(1)}, u32[]{:S(2)}, u32[]{:S(2)}) collective-permute-start(bf16[1280,128]{1,0:T(8,128)(2,1)S(1)} %collective-permute-done.1.own), channel_id=1, source_target_pairs={{0,4},{4,12},{12,8},{8,0},{1,5},{5,13},{13,9},{9,1},{2,6},{6,14},{... | collective-permute-start | bytes 983048 | tf_op jit(solution)/shard_map/ppermute | solution.py:481
  24.1 8.7 %collective-permute-done.7.refs_2_ = bf16[6,128,128]{2,1,0:T(8,128)(2,1)S(1)} collective-permute-done((bf16[6,128,128]{2,1,0:T(8,128)(2,1)S(1)}, bf16[6,128,128]{2,1,0:T(8,128)(2,1)S(1)}, u32[]{:S(2)}, u32[]{:S(2)}) %collective-permute-start.7) | collective-permute-done | bytes 196640 | tf_op jit(solution)/shard_map/ppermute | solution.py:481
  33.2 1.1 %collective-permute-start.9 = (bf16[1920,128]{1,0:T(8,128)(2,1)S(1)}, bf16[1920,128]{1,0:T(8,128)(2,1)S(1)}, u32[]{:S(2)}, u32[]{:S(2)}) collective-permute-start(bf16[1920,128]{1,0:T(8,128)(2,1)S(1)} %get-tuple-element.87), channel_id=1, source_target_pairs={{0,16},{16,0},{1,17},{17,1},{2,18},{18,2},{3,19},{19,3},{4,20},{20... | collective-permute-start | bytes 1474568 | tf_op jit(solution)/shard_map/ppermute | solution.py:477
  34.3 2.6 %collective-permute-start.11 = (bf16[6,128,128]{2,1,0:T(8,128)(2,1)S(1)}, bf16[6,128,128]{2,1,0:T(8,128)(2,1)S(1)}, u32[]{:S(2)}, u32[]{:S(2)}) collective-permute-start(bf16[6,128,128]{2,1,0:T(8,128)(2,1)S(1)} %get-tuple-element.66), channel_id=1, source_target_pairs={{0,8},{4,0},{12,4},{8,12},{1,9},{5,1},{13,5},{9,13},{2,10},{6,2},{... | collective-permute-start | bytes 589832 | tf_op jit(solution)/shard_map/ppermute | solution.py:481
  37.3 1.9 %shift_tiles.2.refs_1_.refs_0_ = bf16[12,144,256]{2,1,0:T(8,128)(2,1)S(1)} custom-call(s32[7,24]{1,0:T(8,128)S(1)} %get-tuple-element.52.refs_0_.plan, bf16[6,128,128]{2,1,0:T(8,128)(2,1)S(1)} %get-tuple-element.63.refs_1_, bf16[6,128,128]{2,1,0:T(8,128)(2,1)S(1)} %collective-permute-done.7.refs_2_), custom_call_target="tpu_custom_call" | custom-call | bytes 8388608 | tf_op jit(solution)/shard_map/shift_tiles/pallas_call | solution.py:139
  39.2 9.1 %collective-permute-done.10.refs_1_ = bf16[6,128,128]{2,1,0:T(8,128)(2,1)S(1)} collective-permute-done((bf16[6,128,128]{2,1,0:T(8,128)(2,1)S(1)}, bf16[6,128,128]{2,1,0:T(8,128)(2,1)S(1)}, u32[]{:S(2)}, u32[]{:S(2)}) %collective-permute-start.10) | collective-permute-done | bytes 196640 | tf_op jit(solution)/shard_map/ppermute | solution.py:481
  48.7 1.8 %collective-permute-start.14 = (bf16[1280,512]{1,0:T(8,128)(2,1)S(1)}, bf16[1280,512]{1,0:T(8,128)(2,1)S(1)}, u32[]{:S(2)}, u32[]{:S(2)}) collective-permute-start(bf16[1280,512]{1,0:T(8,128)(2,1)S(1)} %choose.2.refs_3_), channel_id=1, source_target_pairs={{0,1},{1,0},{2,3},{3,2},{4,5},{5,4},{6,7},{7,6},{8,9},{9,8},{10,11... | collective-permute-start | bytes 3932168 | tf_op jit(solution)/shard_map/ppermute | solution.py:469
  50.6 1.3 %collective-permute-start.12 = (bf16[640,128]{1,0:T(8,128)(2,1)S(1)}, bf16[640,128]{1,0:T(8,128)(2,1)S(1)}, u32[]{:S(2)}, u32[]{:S(2)}) collective-permute-start(bf16[640,128]{1,0:T(8,128)(2,1)S(1)} %slice.22), channel_id=1, source_target_pairs={{0,2},{2,0},{1,3},{3,1},{4,6},{6,4},{5,7},{7,5},{8,10},{10,8},{9,1... | collective-permute-start | bytes 491528 | tf_op jit(solution)/shard_map/ppermute | solution.py:473
  51.9 0.3 collective-permute-start.13
  52.2 1.9 %shift_tiles.3.refs_2_.refs_1_ = bf16[12,144,256]{2,1,0:T(8,128)(2,1)S(1)} custom-call(s32[7,24]{1,0:T(8,128)S(1)} %get-tuple-element.52.refs_0_.plan, bf16[6,128,128]{2,1,0:T(8,128)(2,1)S(1)} %collective-permute-done.10.refs_1_, bf16[6,128,128]{2,1,0:T(8,128)(2,1)S(1)} %collective-permute-done.11.refs_2_), custom_call_target="tpu_custom_call" | custom-call | bytes 8388608 | tf_op jit(solution)/shard_map/shift_tiles/pallas_call | solution.py:139
  54.1 2.2 %first_product.1.middle.refs_2_ = bf16[1280,512]{1,0:T(8,128)(2,1)S(1)} custom-call(s32[7,24]{1,0:T(8,128)S(1)} %get-tuple-element.52.refs_0_.plan, bf16[12,144,256]{2,1,0:T(8,128)(2,1)S(1)} %shift_tiles.2.refs_1_.refs_0_, bf16[12,144,256]{2,1,0:T(8,128)(2,1)S(1)} %shift_tiles.3.refs_2_.refs_1_, bf16[1280,512]{1,0:T(8,128)(2,1)S(1)} %choose.2.refs_3_, ...), custom_call_target="tpu_custom_call" | custom-call | flops 1811939328 | bytes 6291456 | tf_op jit(solution)/shard_map/first_product/pallas_call | solution.py:309
  56.5 0.9 %collective-permute-done.13.far_y = bf16[640,128]{1,0:T(8,128)(2,1)S(1)} collective-permute-done((bf16[640,128]{1,0:T(8,128)(2,1)S(1)}, bf16[640,128]{1,0:T(8,128)(2,1)S(1)}, u32[]{:S(2)}, u32[]{:S(2)}) %collective-permute-start.13) | collective-permute-done | bytes 163872 | tf_op jit(solution)/shard_map/ppermute | solution.py:477
  57.8 1.2 %collective-permute-start.15 = (bf16[1280,512]{1,0:T(8,128)(2,1)S(1)}, bf16[1280,512]{1,0:T(8,128)(2,1)S(1)}, u32[]{:S(2)}, u32[]{:S(2)}) collective-permute-start(bf16[1280,512]{1,0:T(8,128)(2,1)S(1)} %choose.3.refs_2_), channel_id=1, source_target_pairs={{0,1},{1,0},{2,3},{3,2},{4,5},{5,4},{6,7},{7,6},{8,9},{9,8},{10,11... | collective-permute-start | bytes 3932168 | tf_op jit(solution)/shard_map/ppermute | solution.py:469
  59.0 1.7 %send_product.1 = bf16[2,512,512]{2,1,0:T(8,128)(2,1)S(1)} custom-call(bf16[1280,512]{1,0:T(8,128)(2,1)S(1)} %first_product.1.middle.refs_2_, bf16[1280,512]{1,0:T(8,128)(2,1)S(1)} %stay.1.refs_0_.refs_4_, bf16[1280,512]{1,0:T(8,128)(2,1)S(1)} %assemble.3.refs_1_.refs_0_.refs_5_, bf16[1280,512]{1,0:T(8,128)(2,1)S(1)} %assemble.4.refs_2_.refs_1_.refs_6_, ...), custom_call_target="tpu_custom_call" | custom-call | flops 1342177280 | bytes 5242880 | tf_op jit(solution)/shard_map/send_product/pallas_call | solution.py:380
  60.8 0.8 %collective-permute-done.15.refs_3_ = bf16[1280,512]{1,0:T(8,128)(2,1)S(1)} collective-permute-done((bf16[1280,512]{1,0:T(8,128)(2,1)S(1)}, bf16[1280,512]{1,0:T(8,128)(2,1)S(1)}, u32[]{:S(2)}, u32[]{:S(2)}) %collective-permute-start.15) | collective-permute-done | bytes 1310752 | tf_op jit(solution)/shard_map/ppermute | solution.py:469
  61.6 3.9 %first_and_send.1 = (bf16[1280,512]{1,0:T(8,128)(2,1)S(1)}, bf16[2,512,512]{2,1,0:T(8,128)(2,1)S(1)}) custom-call(s32[7,24]{1,0:T(8,128)S(1)} %get-tuple-element.52.refs_0_.plan, bf16[12,144,256]{2,1,0:T(8,128)(2,1)S(1)} %shift_tiles.2.refs_1_.refs_0_, bf16[12,144,256]{2,1,0:T(8,128)(2,1)S(1)} %shift_tiles.3.refs_2_.refs_1_, ...), custom_call_target="tpu_custom_call" | custom-call | flops 3154116608 | bytes 10485760 | tf_op jit(solution)/shard_map/first_and_send/pallas_call | solution.py:354
  65.6 0.4 collective-permute-start.16
  66.0 2.7 %keep_product.2 = (bf16[1,1024,1024]{2,1,0:T(8,128)(2,1)}, bf16[2,1280,512]{2,1,0:T(8,128)(2,1)S(1)}) custom-call(f32[1,1024]{1,0:T(1,128)S(1)} %get-tuple-element.44.refs_0_, f32[1024,128]{1,0:T(8,128)S(1)} %get-tuple-element.45.refs_1_, bf16[1280,512]{1,0:T(8,128)(2,1)S(1)} %first_product.1.middle.refs_2_, ...), custom_call_target="tpu_custom_call" | custom-call | flops 1342177280 | bytes 6291456 | tf_op jit(solution)/shard_map/keep_product/pallas_call | solution.py:445
  68.8 2.3 %keep_product.3 = bf16[1,1024,1024]{2,1,0:T(8,128)(2,1)} custom-call(f32[1,1024]{1,0:T(1,128)S(1)} %get-tuple-element.44.refs_0_, f32[1024,128]{1,0:T(8,128)S(1)} %get-tuple-element.45.refs_1_, bf16[1280,512]{1,0:T(8,128)(2,1)S(1)} %get-tuple-element.76.refs_2_, ...), custom_call_target="tpu_custom_call", output_to_operand_aliasing={{}: (5, {})} | custom-call | flops 1342177280 | bytes 6291456 | tf_op jit(solution)/shard_map/keep_product/pallas_call | solution.py:445
  (47 shorter events, 2.6 us)
Async XLA Ops:
  1.0 8.7 %collective-permute-start = (bf16[1280,128]{1,0:T(8,128)(2,1)S(1)}, bf16[1280,128]{1,0:T(8,128)(2,1)S(1)}, u32[]{:S(2)}, u32[]{:S(2)}) collective-permute-start(bf16[1280,128]{1,0:T(8,128)(2,1)S(1)} %constant_dynamic-slice_fusion), channel_id=1, source_target_pairs={{0,4},{4,12},{12,8},{8,0},{1,5},{5,13},{13,9},{9,1},{2,6},{6,14},{... | collective-permute-start | bytes 983048 | tf_op jit(solution)/shard_map/ppermute | solution.py:481
  3.4 1.3 %copy-start = (bf16[1280,512]{1,0:T(8,128)(2,1)S(1)}, bf16[1280,512]{1,0:T(8,128)(2,1)}, u32[]{:S(2)}) copy-start(bf16[1280,512]{1,0:T(8,128)(2,1)} %value.1) | copy-start | bytes 3932164
  4.7 1.1 %copy-start.5 = (bf16[4,1,6,128,128]{4,3,2,1,0:T(8,128)(2,1)S(1)}, bf16[4,1,6,128,128]{4,3,2,1,0:T(8,128)(2,1)}, u32[]{:S(2)}) copy-start(bf16[4,1,6,128,128]{4,3,2,1,0:T(8,128)(2,1)} %param.7) | copy-start | bytes 2359300
  4.8 10.5 %copy-start.8 = (s32[1,24,2]{1,2,0:T(2,128)S(1)}, s32[1,24,2]{1,2,0:T(2,128)}, u32[]{:S(2)}) copy-start(s32[1,24,2]{1,2,0:T(2,128)} %param.12) | copy-start | bytes 580
  4.8 10.6 %copy-start.1 = (f32[2048]{0:T(1024)S(1)}, f32[2048]{0:T(1024)}, u32[]{:S(2)}) copy-start(f32[2048]{0:T(1024)} %param.10) | copy-start | bytes 24580
  4.8 10.6 %copy-start.2 = (f32[400]{0:T(512)S(1)}, f32[400]{0:T(512)}, u32[]{:S(2)}) copy-start(f32[400]{0:T(512)} %eps_occ.1) | copy-start | bytes 4804
  4.8 10.6 %copy-start.3 = (s32[2,12]{1,0:T(2,128)S(1)}, s32[2,12]{1,0:T(2,128)}, u32[]{:S(2)}) copy-start(s32[2,12]{1,0:T(2,128)} %extra.1) | copy-start | bytes 292
  4.8 10.6 %copy-start.4 = (s32[1,2]{1,0:T(1,128)S(1)}, s32[1,2]{1,0:T(1,128)}, u32[]{:S(2)}) copy-start(s32[1,2]{1,0:T(1,128)} %pair_occ.1) | copy-start | bytes 28
  9.7 8.6 %collective-permute-start.1 = (bf16[1280,128]{1,0:T(8,128)(2,1)S(1)}, bf16[1280,128]{1,0:T(8,128)(2,1)S(1)}, u32[]{:S(2)}, u32[]{:S(2)}) collective-permute-start(bf16[1280,128]{1,0:T(8,128)(2,1)S(1)} %collective-permute-done.own), channel_id=1, source_target_pairs={{0,4},{4,12},{12,8},{8,0},{1,5},{5,13},{13,9},{9,1},{2,6},{6,14},{... | collective-permute-start | bytes 983048 | tf_op jit(solution)/shard_map/ppermute | solution.py:481
  12.8 7.4 %collective-permute-start.2 = (bf16[1280,128]{1,0:T(8,128)(2,1)S(1)}, bf16[1280,128]{1,0:T(8,128)(2,1)S(1)}, u32[]{:S(2)}, u32[]{:S(2)}) collective-permute-start(bf16[1280,128]{1,0:T(8,128)(2,1)S(1)} %collective-permute-done.own), channel_id=1, source_target_pairs={{0,16},{16,0},{1,17},{17,1},{2,18},{18,2},{3,19},{19,3},{4,20},{20... | collective-permute-start | bytes 983048 | tf_op jit(solution)/shard_map/ppermute | solution.py:477
  14.1 7.1 %collective-permute-start.3 = (bf16[1280,128]{1,0:T(8,128)(2,1)S(1)}, bf16[1280,128]{1,0:T(8,128)(2,1)S(1)}, u32[]{:S(2)}, u32[]{:S(2)}) collective-permute-start(bf16[1280,128]{1,0:T(8,128)(2,1)S(1)} %collective-permute-done.own), channel_id=1, source_target_pairs={{0,2},{2,0},{1,3},{3,1},{4,6},{6,4},{5,7},{7,5},{8,10},{10,8},{9,1... | collective-permute-start | bytes 983048 | tf_op jit(solution)/shard_map/ppermute | solution.py:473
  15.4 8.7 %copy-start.7 = (bf16[6,128,128]{2,1,0:T(8,128)(2,1)S(1)}, bf16[6,128,128]{2,1,0:T(8,128)(2,1)}, u32[]{:S(2)}) copy-start(bf16[6,128,128]{2,1,0:T(8,128)(2,1)} %get-tuple-element.56) | copy-start | bytes 589828
  21.3 13.0 %copy-start.6 = (bf16[6,128,128]{2,1,0:T(8,128)(2,1)S(1)}, bf16[6,128,128]{2,1,0:T(8,128)(2,1)}, u32[]{:S(2)}) copy-start(bf16[6,128,128]{2,1,0:T(8,128)(2,1)} %get-tuple-element.65) | copy-start | bytes 589828
  21.3 11.5 %collective-permute-start.4 = (bf16[1920,128]{1,0:T(8,128)(2,1)S(1)}, bf16[1920,128]{1,0:T(8,128)(2,1)S(1)}, u32[]{:S(2)}, u32[]{:S(2)}) collective-permute-start(bf16[1920,128]{1,0:T(8,128)(2,1)S(1)} %get-tuple-element.90), channel_id=1, source_target_pairs={{0,2},{2,0},{1,3},{3,1},{4,6},{6,4},{5,7},{7,5},{8,10},{10,8},{9,1... | collective-permute-start | bytes 1474568 | tf_op jit(solution)/shard_map/ppermute | solution.py:473
  22.6 10.2 %collective-permute-start.5 = (bf16[1920,128]{1,0:T(8,128)(2,1)S(1)}, bf16[1920,128]{1,0:T(8,128)(2,1)S(1)}, u32[]{:S(2)}, u32[]{:S(2)}) collective-permute-start(bf16[1920,128]{1,0:T(8,128)(2,1)S(1)} %get-tuple-element.89), channel_id=1, source_target_pairs={{0,16},{16,0},{1,17},{17,1},{2,18},{18,2},{3,19},{19,3},{4,20},{20... | collective-permute-start | bytes 1474568 | tf_op jit(solution)/shard_map/ppermute | solution.py:477
  22.9 9.9 %collective-permute-start.6 = (bf16[1280,128]{1,0:T(8,128)(2,1)S(1)}, bf16[1280,128]{1,0:T(8,128)(2,1)S(1)}, u32[]{:S(2)}, u32[]{:S(2)}) collective-permute-start(bf16[1280,128]{1,0:T(8,128)(2,1)S(1)} %collective-permute-done.1.own), channel_id=1, source_target_pairs={{0,4},{4,12},{12,8},{8,0},{1,5},{5,13},{13,9},{9,1},{2,6},{6,14},{... | collective-permute-start | bytes 983048 | tf_op jit(solution)/shard_map/ppermute | solution.py:481
  24.0 8.7 %collective-permute-start.7 = (bf16[6,128,128]{2,1,0:T(8,128)(2,1)S(1)}, bf16[6,128,128]{2,1,0:T(8,128)(2,1)S(1)}, u32[]{:S(2)}, u32[]{:S(2)}) collective-permute-start(bf16[6,128,128]{2,1,0:T(8,128)(2,1)S(1)} %copy-done.7), channel_id=1, source_target_pairs={{0,4},{4,12},{12,8},{8,0},{1,5},{5,13},{13,9},{9,1},{2,6},{6,14},{... | collective-permute-start | bytes 589832 | tf_op jit(solution)/shard_map/ppermute | solution.py:481
  32.9 15.4 %collective-permute-start.8 = (bf16[1920,128]{1,0:T(8,128)(2,1)S(1)}, bf16[1920,128]{1,0:T(8,128)(2,1)S(1)}, u32[]{:S(2)}, u32[]{:S(2)}) collective-permute-start(bf16[1920,128]{1,0:T(8,128)(2,1)S(1)} %get-tuple-element.88), channel_id=1, source_target_pairs={{0,2},{2,0},{1,3},{3,1},{4,6},{6,4},{5,7},{7,5},{8,10},{10,8},{9,1... | collective-permute-start | bytes 1474568 | tf_op jit(solution)/shard_map/ppermute | solution.py:473
  33.2 15.1 %collective-permute-start.9 = (bf16[1920,128]{1,0:T(8,128)(2,1)S(1)}, bf16[1920,128]{1,0:T(8,128)(2,1)S(1)}, u32[]{:S(2)}, u32[]{:S(2)}) collective-permute-start(bf16[1920,128]{1,0:T(8,128)(2,1)S(1)} %get-tuple-element.87), channel_id=1, source_target_pairs={{0,16},{16,0},{1,17},{17,1},{2,18},{18,2},{3,19},{19,3},{4,20},{20... | collective-permute-start | bytes 1474568 | tf_op jit(solution)/shard_map/ppermute | solution.py:477
  34.3 14.0 %collective-permute-start.10 = (bf16[6,128,128]{2,1,0:T(8,128)(2,1)S(1)}, bf16[6,128,128]{2,1,0:T(8,128)(2,1)S(1)}, u32[]{:S(2)}, u32[]{:S(2)}) collective-permute-start(bf16[6,128,128]{2,1,0:T(8,128)(2,1)S(1)} %copy-done.6), channel_id=1, source_target_pairs={{0,12},{4,8},{12,0},{8,4},{1,13},{5,9},{13,1},{9,5},{2,14},{6,10},... | collective-permute-start | bytes 589832 | tf_op jit(solution)/shard_map/ppermute | solution.py:481
  34.3 14.0 %collective-permute-start.11 = (bf16[6,128,128]{2,1,0:T(8,128)(2,1)S(1)}, bf16[6,128,128]{2,1,0:T(8,128)(2,1)S(1)}, u32[]{:S(2)}, u32[]{:S(2)}) collective-permute-start(bf16[6,128,128]{2,1,0:T(8,128)(2,1)S(1)} %get-tuple-element.66), channel_id=1, source_target_pairs={{0,8},{4,0},{12,4},{8,12},{1,9},{5,1},{13,5},{9,13},{2,10},{6,2},{... | collective-permute-start | bytes 589832 | tf_op jit(solution)/shard_map/ppermute | solution.py:481
  48.7 5.4 %collective-permute-start.14 = (bf16[1280,512]{1,0:T(8,128)(2,1)S(1)}, bf16[1280,512]{1,0:T(8,128)(2,1)S(1)}, u32[]{:S(2)}, u32[]{:S(2)}) collective-permute-start(bf16[1280,512]{1,0:T(8,128)(2,1)S(1)} %choose.2.refs_3_), channel_id=1, source_target_pairs={{0,1},{1,0},{2,3},{3,2},{4,5},{5,4},{6,7},{7,6},{8,9},{9,8},{10,11... | collective-permute-start | bytes 3932168 | tf_op jit(solution)/shard_map/ppermute | solution.py:469
  50.6 5.9 %collective-permute-start.12 = (bf16[640,128]{1,0:T(8,128)(2,1)S(1)}, bf16[640,128]{1,0:T(8,128)(2,1)S(1)}, u32[]{:S(2)}, u32[]{:S(2)}) collective-permute-start(bf16[640,128]{1,0:T(8,128)(2,1)S(1)} %slice.22), channel_id=1, source_target_pairs={{0,2},{2,0},{1,3},{3,1},{4,6},{6,4},{5,7},{7,5},{8,10},{10,8},{9,1... | collective-permute-start | bytes 491528 | tf_op jit(solution)/shard_map/ppermute | solution.py:473
  51.9 5.5 %collective-permute-start.13 = (bf16[640,128]{1,0:T(8,128)(2,1)S(1)}, bf16[640,128]{1,0:T(8,128)(2,1)S(1)}, u32[]{:S(2)}, u32[]{:S(2)}) collective-permute-start(bf16[640,128]{1,0:T(8,128)(2,1)S(1)} %slice.23), channel_id=1, source_target_pairs={{0,16},{16,0},{1,17},{17,1},{2,18},{18,2},{3,19},{19,3},{4,20},{20... | collective-permute-start | bytes 491528 | tf_op jit(solution)/shard_map/ppermute | solution.py:477
  57.8 3.8 %collective-permute-start.15 = (bf16[1280,512]{1,0:T(8,128)(2,1)S(1)}, bf16[1280,512]{1,0:T(8,128)(2,1)S(1)}, u32[]{:S(2)}, u32[]{:S(2)}) collective-permute-start(bf16[1280,512]{1,0:T(8,128)(2,1)S(1)} %choose.3.refs_2_), channel_id=1, source_target_pairs={{0,1},{1,0},{2,3},{3,2},{4,5},{5,4},{6,7},{7,6},{8,9},{9,8},{10,11... | collective-permute-start | bytes 3932168 | tf_op jit(solution)/shard_map/ppermute | solution.py:469
  60.7 5.3 %collective-permute-start.17 = (bf16[2,512,512]{2,1,0:T(8,128)(2,1)S(1)}, bf16[2,512,512]{2,1,0:T(8,128)(2,1)S(1)}, u32[]{:S(2)}, u32[]{:S(2)}) collective-permute-start(bf16[2,512,512]{2,1,0:T(8,128)(2,1)S(1)} %send_product.1), channel_id=1, source_target_pairs={{0,1},{1,0},{2,3},{3,2},{4,5},{5,4},{6,7},{7,6},{8,9},{9,8},{10,11... | collective-permute-start | bytes 3145736 | tf_op jit(solution)/shard_map/ppermute | solution.py:469
  65.6 3.2 %collective-permute-start.16 = (bf16[2,512,512]{2,1,0:T(8,128)(2,1)S(1)}, bf16[2,512,512]{2,1,0:T(8,128)(2,1)S(1)}, u32[]{:S(2)}, u32[]{:S(2)}) collective-permute-start(bf16[2,512,512]{2,1,0:T(8,128)(2,1)S(1)} %get-tuple-element.77), channel_id=1, source_target_pairs={{0,1},{1,0},{2,3},{3,2},{4,5},{5,4},{6,7},{7,6},{8,9},{9,8},{10,11... | collective-permute-start | bytes 3145736 | tf_op jit(solution)/shard_map/ppermute | solution.py:469

commit v8 on v7

--- a/solution.py
+++ b/solution.py
@@ -233,6 +233,26 @@
 
 def choose_kernel(which, blocks, *refs):
     pick(ring_slot(column_block(which, blocks)), which, refs[:-1], refs[-1])
+
+
+def last_kernel(blocks, *refs):
+    pieces, groups, (out, chosen, sems) = refs[:5], refs[5:7], refs[7:]
+    assemble_kernel(*pieces, out, sems)
+    pick(ring_slot(column_block(1, blocks)), 1, (*groups, out), chosen)
+
+
+def assemble_last(blocks, pieces, groups):
+    shape = jax.ShapeDtypeStruct(groups[0].shape, BF16)
+    return pl.pallas_call(
+        functools.partial(last_kernel, blocks),
+        out_shape=(shape, shape),
+        in_specs=[ANY] * 5 + [VMEM] * 2,
+        out_specs=(VMEM, VMEM),
+        scratch_shapes=[pltpu.SemaphoreType.DMA((5,))],
+        compiler_params=pltpu.CompilerParams(vmem_limit_bytes=10 * MIB),
+        cost_estimate=pl.CostEstimate(flops=0, bytes_accessed=4 * MIB, transcendentals=0),
+        name="assemble_last",
+    )(*pieces, *groups)
 
 
 def choose(which, blocks, groups):
@@ -514,8 +534,8 @@
         plan, [early, late], [], [first], [other_core(first)], 0, blocks
     )
     x4, y4, middle = together((to_x(y3[:half]), to_y(x3[half:rows]), middle))
-    group3 = assemble(z3, x3, y3, x4, y4)
-    return [group0, group1, group2, group3], middle, shifted, plan
+    group3, second = assemble_last(blocks, [z3, x3, y3, x4, y4], [group1, group2])
+    return [group0, group1, group2, group3], second, middle, shifted, plan
 
 
 def exchange_any(half_ints, coeff):
@@ -539,14 +559,14 @@
         eps_vir.reshape(1, -1), rows, full_width // lax.axis_size("rep"), b_width,
     )
     if ringed:
-        groups, early_middle, shifted, plan = exchange_small(half_ints, coeff, plan, shift_tiles)
+        groups, second, early_middle, shifted, plan = exchange_small(half_ints, coeff, plan, shift_tiles)
         blocks = b_width // width
     else:
         gathered, groups, tiles = exchange_any(half_ints, coeff)
         own, blocks = [lax.dynamic_slice_in_dim(gathered, vir * b_width, b_width, 1)], 1
         shifted = [shift_tiles(plan, 0, [tiles])]
     if ringed:
-        own = [choose(1, blocks, groups[1:])]
+        own = [second]
     other = [other_core(g) for g in own]
     middles, got = [], []
     for which in range(blocks):

time: 71.5 us -> 71.4 us (level)
  no operation moved by 1% of the time
where the time goes in v8:
time: 71.4 us; the launch traced here: 71.2 us
  waiting for transfers between devices  25.8 us (36%)
  Pallas kernels  20.6 us (29%)
  starting transfers between devices  20 us (28%)
  local copies, waits for them, and re-layouts  4.27 us (6%)
    ppermute x6, waiting for transfers between devices, to_z(): return lax.ppermute(value, 'ao', ring_pairs(distance))  21.1 us
    ppermute x6, starting transfers between devices, to_z(): return lax.ppermute(value, 'ao', ring_pairs(distance))  9.32 us
    pallas_call x2, Pallas kernels, keep_product(): pl.pallas_call(functools.partial(keep_kernel, which, blocks, len(groups),...  5.05 us
    ppermute x4, starting transfers between devices, to_x(): return lax.ppermute(value, 'vir', SWAP)  4.08 us
    pallas_call x1, Pallas kernels, first_and_send(): pl.pallas_call(functools.partial(first_and_send_kernel, len(shifted), whi...  3.95 us
    pallas_call x2, Pallas kernels, shift_tiles(): pl.pallas_call(functools.partial(shift_kernel, first, len(tiles)), out_sh...  3.83 us
    ppermute x4, starting transfers between devices, other_core(): return lax.ppermute(value, 'rep', SWAP)  3.57 us
    ppermute x4, starting transfers between devices, to_y(): return lax.ppermute(value, 'grp', SWAP)  2.99 us
  transfers between devices with their start and end apart: 18, of which 9 were waited for; matrix products, arithmetic and copies ran while one was open for 1% of the time, Pallas kernels for 25%

profile of v8, /device:TPU:9, one launch (start us, length us, event | category | flops | bytes accessed | tf_op | source)
XLA Modules:
  0.0 71.2 jit_solution(8335077241010241136)
XLA Ops:
  0.0 1.0 %constant_dynamic-slice_fusion = bf16[1280,128]{1,0:T(8,128)(2,1)S(1)} fusion(bf16[1280,512]{1,0:T(8,128)(2,1)} %value.1, s32[]{:T(128)S(6)} %select_n.16), kind=kLoop, calls=%fused_computation.8 | loop fusion | bytes 655364 | tf_op jit(solution)/shard_map/dynamic_slice | solution.py:514
  1.0 2.4 %collective-permute-start = (bf16[1280,128]{1,0:T(8,128)(2,1)S(1)}, bf16[1280,128]{1,0:T(8,128)(2,1)S(1)}, u32[]{:S(2)}, u32[]{:S(2)}) collective-permute-start(bf16[1280,128]{1,0:T(8,128)(2,1)S(1)} %constant_dynamic-slice_fusion), channel_id=1, source_target_pairs={{0,4},{4,12},{12,8},{8,0},{1,5},{5,13},{13,9},{9,1},{2,6},{6,14},{... | collective-permute-start | bytes 983048 | tf_op jit(solution)/shard_map/ppermute | solution.py:501
  3.4 1.3 %copy-done = bf16[1280,512]{1,0:T(8,128)(2,1)S(1)} copy-done((bf16[1280,512]{1,0:T(8,128)(2,1)S(1)}, bf16[1280,512]{1,0:T(8,128)(2,1)}, u32[]{:S(2)}) %copy-start) | copy-done | bytes 1310744
  4.8 1.0 %copy-done.5 = bf16[4,1,6,128,128]{4,3,2,1,0:T(8,128)(2,1)S(1)} copy-done((bf16[4,1,6,128,128]{4,3,2,1,0:T(8,128)(2,1)S(1)}, bf16[4,1,6,128,128]{4,3,2,1,0:T(8,128)(2,1)}, u32[]{:S(2)}) %copy-start.5) | copy-done | bytes 786456
  5.8 0.8 %dynamic-slice_bitcast_fusion = (bf16[6,128,128]{2,1,0:T(8,128)(2,1)S(1)}, bf16[6,128,128]{2,1,0:T(8,128)(2,1)}, bf16[6,128,128]{2,1,0:T(8,128)(2,1)S(1)}, bf16[6,128,128]{2,1,0:T(8,128)(2,1)}) fusion(bf16[4,1,6,128,128]{4,3,2,1,0:T(8,128)(2,1)S(1)} %copy-done.5, s32[]{:T(128)S(6)} %select_n.20, s32[]{:T(128)S(6)} %select_n.18, s32[]{:T(128)S(6)} %select_n.17, ...), kind=kLoop, calls=%fused_computation.4 | loop fusion | bytes 1572880 | tf_op jit(solution)/shard_map/jit(dynamic_index_in_dim)/squeeze | solution.py:516
  6.6 3.1 %collective-permute-done.own = bf16[1280,128]{1,0:T(8,128)(2,1)S(1)} collective-permute-done((bf16[1280,128]{1,0:T(8,128)(2,1)S(1)}, bf16[1280,128]{1,0:T(8,128)(2,1)S(1)}, u32[]{:S(2)}, u32[]{:S(2)}) %collective-permute-start) | collective-permute-done | bytes 327712 | tf_op jit(solution)/shard_map/ppermute | solution.py:501
  9.7 3.1 %collective-permute-start.1 = (bf16[1280,128]{1,0:T(8,128)(2,1)S(1)}, bf16[1280,128]{1,0:T(8,128)(2,1)S(1)}, u32[]{:S(2)}, u32[]{:S(2)}) collective-permute-start(bf16[1280,128]{1,0:T(8,128)(2,1)S(1)} %collective-permute-done.own), channel_id=1, source_target_pairs={{0,4},{4,12},{12,8},{8,0},{1,5},{5,13},{13,9},{9,1},{2,6},{6,14},{... | collective-permute-start | bytes 983048 | tf_op jit(solution)/shard_map/ppermute | solution.py:501
  12.8 1.2 %collective-permute-start.2 = (bf16[1280,128]{1,0:T(8,128)(2,1)S(1)}, bf16[1280,128]{1,0:T(8,128)(2,1)S(1)}, u32[]{:S(2)}, u32[]{:S(2)}) collective-permute-start(bf16[1280,128]{1,0:T(8,128)(2,1)S(1)} %collective-permute-done.own), channel_id=1, source_target_pairs={{0,16},{16,0},{1,17},{17,1},{2,18},{18,2},{3,19},{19,3},{4,20},{20... | collective-permute-start | bytes 983048 | tf_op jit(solution)/shard_map/ppermute | solution.py:497
  14.1 1.2 %collective-permute-start.3 = (bf16[1280,128]{1,0:T(8,128)(2,1)S(1)}, bf16[1280,128]{1,0:T(8,128)(2,1)S(1)}, u32[]{:S(2)}, u32[]{:S(2)}) collective-permute-start(bf16[1280,128]{1,0:T(8,128)(2,1)S(1)} %collective-permute-done.own), channel_id=1, source_target_pairs={{0,2},{2,0},{1,3},{3,1},{4,6},{6,4},{5,7},{7,5},{8,10},{10,8},{9,1... | collective-permute-start | bytes 983048 | tf_op jit(solution)/shard_map/ppermute | solution.py:493
  15.4 2.7 %make_plan.1 = (s32[7,24]{1,0:T(8,128)S(1)}, f32[1,1024]{1,0:T(1,128)S(1)}, f32[1024,128]{1,0:T(8,128)S(1)}) custom-call(s32[1,24,2]{2,1,0:T(8,128)S(1)} %copy.9.listed, s32[2,12]{1,0:T(2,128)S(1)} %copy-done.3, s32[1,2]{1,0:T(1,128)S(1)} %copy-done.4, f32[400]{0:T(512)S(1)} %copy-done.2, f32[1,2048]{1,0:T(1,128)S(1)} %bitcast.9), custom_call_target="tpu_custom_call" | custom-call | bytes 2097152 | tf_op jit(solution)/shard_map/make_plan/pallas_call | solution.py:78
  18.3 1.9 %collective-permute-done.2.by_y = bf16[1280,128]{1,0:T(8,128)(2,1)S(1)} collective-permute-done((bf16[1280,128]{1,0:T(8,128)(2,1)S(1)}, bf16[1280,128]{1,0:T(8,128)(2,1)S(1)}, u32[]{:S(2)}, u32[]{:S(2)}) %collective-permute-start.2) | collective-permute-done | bytes 327712 | tf_op jit(solution)/shard_map/ppermute | solution.py:497
  20.2 1.0 %collective-permute-done.3.by_x = bf16[1280,128]{1,0:T(8,128)(2,1)S(1)} collective-permute-done((bf16[1280,128]{1,0:T(8,128)(2,1)S(1)}, bf16[1280,128]{1,0:T(8,128)(2,1)S(1)}, u32[]{:S(2)}, u32[]{:S(2)}) %collective-permute-start.3) | collective-permute-done | bytes 327712 | tf_op jit(solution)/shard_map/ppermute | solution.py:493
  21.3 1.3 %collective-permute-start.4 = (bf16[1920,128]{1,0:T(8,128)(2,1)S(1)}, bf16[1920,128]{1,0:T(8,128)(2,1)S(1)}, u32[]{:S(2)}, u32[]{:S(2)}) collective-permute-start(bf16[1920,128]{1,0:T(8,128)(2,1)S(1)} %get-tuple-element.94), channel_id=1, source_target_pairs={{0,2},{2,0},{1,3},{3,1},{4,6},{6,4},{5,7},{7,5},{8,10},{10,8},{9,1... | collective-permute-start | bytes 1474568 | tf_op jit(solution)/shard_map/ppermute | solution.py:493
  22.9 1.2 %collective-permute-start.6 = (bf16[1280,128]{1,0:T(8,128)(2,1)S(1)}, bf16[1280,128]{1,0:T(8,128)(2,1)S(1)}, u32[]{:S(2)}, u32[]{:S(2)}) collective-permute-start(bf16[1280,128]{1,0:T(8,128)(2,1)S(1)} %collective-permute-done.1.own), channel_id=1, source_target_pairs={{0,4},{4,12},{12,8},{8,0},{1,5},{5,13},{13,9},{9,1},{2,6},{6,14},{... | collective-permute-start | bytes 983048 | tf_op jit(solution)/shard_map/ppermute | solution.py:501
  24.1 8.7 %collective-permute-done.7.refs_2_ = bf16[6,128,128]{2,1,0:T(8,128)(2,1)S(1)} collective-permute-done((bf16[6,128,128]{2,1,0:T(8,128)(2,1)S(1)}, bf16[6,128,128]{2,1,0:T(8,128)(2,1)S(1)}, u32[]{:S(2)}, u32[]{:S(2)}) %collective-permute-start.7) | collective-permute-done | bytes 196640 | tf_op jit(solution)/shard_map/ppermute | solution.py:501
  33.2 1.1 %collective-permute-start.9 = (bf16[1920,128]{1,0:T(8,128)(2,1)S(1)}, bf16[1920,128]{1,0:T(8,128)(2,1)S(1)}, u32[]{:S(2)}, u32[]{:S(2)}) collective-permute-start(bf16[1920,128]{1,0:T(8,128)(2,1)S(1)} %get-tuple-element.91), channel_id=1, source_target_pairs={{0,16},{16,0},{1,17},{17,1},{2,18},{18,2},{3,19},{19,3},{4,20},{20... | collective-permute-start | bytes 1474568 | tf_op jit(solution)/shard_map/ppermute | solution.py:497
  34.3 2.6 %collective-permute-start.11 = (bf16[6,128,128]{2,1,0:T(8,128)(2,1)S(1)}, bf16[6,128,128]{2,1,0:T(8,128)(2,1)S(1)}, u32[]{:S(2)}, u32[]{:S(2)}) collective-permute-start(bf16[6,128,128]{2,1,0:T(8,128)(2,1)S(1)} %get-tuple-element.68), channel_id=1, source_target_pairs={{0,8},{4,0},{12,4},{8,12},{1,9},{5,1},{13,5},{9,13},{2,10},{6,2},{... | collective-permute-start | bytes 589832 | tf_op jit(solution)/shard_map/ppermute | solution.py:501
  37.3 1.9 %shift_tiles.2.refs_1_.refs_0_ = bf16[12,144,256]{2,1,0:T(8,128)(2,1)S(1)} custom-call(s32[7,24]{1,0:T(8,128)S(1)} %get-tuple-element.54.refs_0_.plan, bf16[6,128,128]{2,1,0:T(8,128)(2,1)S(1)} %get-tuple-element.65.refs_1_, bf16[6,128,128]{2,1,0:T(8,128)(2,1)S(1)} %collective-permute-done.7.refs_2_), custom_call_target="tpu_custom_call" | custom-call | bytes 8388608 | tf_op jit(solution)/shard_map/shift_tiles/pallas_call | solution.py:139
  39.2 9.1 %collective-permute-done.10.refs_1_ = bf16[6,128,128]{2,1,0:T(8,128)(2,1)S(1)} collective-permute-done((bf16[6,128,128]{2,1,0:T(8,128)(2,1)S(1)}, bf16[6,128,128]{2,1,0:T(8,128)(2,1)S(1)}, u32[]{:S(2)}, u32[]{:S(2)}) %collective-permute-start.10) | collective-permute-done | bytes 196640 | tf_op jit(solution)/shard_map/ppermute | solution.py:501
  48.7 1.8 %collective-permute-start.14 = (bf16[1280,512]{1,0:T(8,128)(2,1)S(1)}, bf16[1280,512]{1,0:T(8,128)(2,1)S(1)}, u32[]{:S(2)}, u32[]{:S(2)}) collective-permute-start(bf16[1280,512]{1,0:T(8,128)(2,1)S(1)} %choose.1.refs_3_), channel_id=1, source_target_pairs={{0,1},{1,0},{2,3},{3,2},{4,5},{5,4},{6,7},{7,6},{8,9},{9,8},{10,11... | collective-permute-start | bytes 3932168 | tf_op jit(solution)/shard_map/ppermute | solution.py:489
  50.6 1.3 %collective-permute-start.12 = (bf16[640,128]{1,0:T(8,128)(2,1)S(1)}, bf16[640,128]{1,0:T(8,128)(2,1)S(1)}, u32[]{:S(2)}, u32[]{:S(2)}) collective-permute-start(bf16[640,128]{1,0:T(8,128)(2,1)S(1)} %slice.22), channel_id=1, source_target_pairs={{0,2},{2,0},{1,3},{3,1},{4,6},{6,4},{5,7},{7,5},{8,10},{10,8},{9,1... | collective-permute-start | bytes 491528 | tf_op jit(solution)/shard_map/ppermute | solution.py:493
  52.2 1.9 %shift_tiles.3.refs_2_.refs_1_ = bf16[12,144,256]{2,1,0:T(8,128)(2,1)S(1)} custom-call(s32[7,24]{1,0:T(8,128)S(1)} %get-tuple-element.54.refs_0_.plan, bf16[6,128,128]{2,1,0:T(8,128)(2,1)S(1)} %collective-permute-done.10.refs_1_, bf16[6,128,128]{2,1,0:T(8,128)(2,1)S(1)} %collective-permute-done.11.refs_2_), custom_call_target="tpu_custom_call" | custom-call | bytes 8388608 | tf_op jit(solution)/shard_map/shift_tiles/pallas_call | solution.py:139
  54.1 2.2 %first_product.1.middle.refs_2_ = bf16[1280,512]{1,0:T(8,128)(2,1)S(1)} custom-call(s32[7,24]{1,0:T(8,128)S(1)} %get-tuple-element.54.refs_0_.plan, bf16[12,144,256]{2,1,0:T(8,128)(2,1)S(1)} %shift_tiles.2.refs_1_.refs_0_, bf16[12,144,256]{2,1,0:T(8,128)(2,1)S(1)} %shift_tiles.3.refs_2_.refs_1_, bf16[1280,512]{1,0:T(8,128)(2,1)S(1)} %choose.1.refs_3_, ...), custom_call_target="tpu_custom_call" | custom-call | flops 1811939328 | bytes 6291456 | tf_op jit(solution)/shard_map/first_product/pallas_call | solution.py:329
  56.5 0.9 %collective-permute-done.13.refs_4_ = bf16[640,128]{1,0:T(8,128)(2,1)S(1)} collective-permute-done((bf16[640,128]{1,0:T(8,128)(2,1)S(1)}, bf16[640,128]{1,0:T(8,128)(2,1)S(1)}, u32[]{:S(2)}, u32[]{:S(2)}) %collective-permute-start.13) | collective-permute-done | bytes 163872 | tf_op jit(solution)/shard_map/ppermute | solution.py:497
  57.4 0.4 assemble_last.1
  57.8 1.2 %collective-permute-start.15 = (bf16[1280,512]{1,0:T(8,128)(2,1)S(1)}, bf16[1280,512]{1,0:T(8,128)(2,1)S(1)}, u32[]{:S(2)}, u32[]{:S(2)}) collective-permute-start(bf16[1280,512]{1,0:T(8,128)(2,1)S(1)} %get-tuple-element.78.refs_2_), channel_id=1, source_target_pairs={{0,1},{1,0},{2,3},{3,2},{4,5},{5,4},{6,7},{7,6},{8,9},{9,8},{10,11... | collective-permute-start | bytes 3932168 | tf_op jit(solution)/shard_map/ppermute | solution.py:489
  58.9 1.7 %send_product.1 = bf16[2,512,512]{2,1,0:T(8,128)(2,1)S(1)} custom-call(bf16[1280,512]{1,0:T(8,128)(2,1)S(1)} %first_product.1.middle.refs_2_, bf16[1280,512]{1,0:T(8,128)(2,1)S(1)} %stay.1.refs_0_.refs_4_, bf16[1280,512]{1,0:T(8,128)(2,1)S(1)} %assemble.2.refs_1_.refs_5_, bf16[1280,512]{1,0:T(8,128)(2,1)S(1)} %assemble.3.refs_2_.refs_6_, ...), custom_call_target="tpu_custom_call" | custom-call | flops 1342177280 | bytes 5242880 | tf_op jit(solution)/shard_map/send_product/pallas_call | solution.py:400
  60.8 0.8 %collective-permute-done.15.refs_3_ = bf16[1280,512]{1,0:T(8,128)(2,1)S(1)} collective-permute-done((bf16[1280,512]{1,0:T(8,128)(2,1)S(1)}, bf16[1280,512]{1,0:T(8,128)(2,1)S(1)}, u32[]{:S(2)}, u32[]{:S(2)}) %collective-permute-start.15) | collective-permute-done | bytes 1310752 | tf_op jit(solution)/shard_map/ppermute | solution.py:489
  61.6 3.9 %first_and_send.1 = (bf16[1280,512]{1,0:T(8,128)(2,1)S(1)}, bf16[2,512,512]{2,1,0:T(8,128)(2,1)S(1)}) custom-call(s32[7,24]{1,0:T(8,128)S(1)} %get-tuple-element.54.refs_0_.plan, bf16[12,144,256]{2,1,0:T(8,128)(2,1)S(1)} %shift_tiles.2.refs_1_.refs_0_, bf16[12,144,256]{2,1,0:T(8,128)(2,1)S(1)} %shift_tiles.3.refs_2_.refs_1_, ...), custom_call_target="tpu_custom_call" | custom-call | flops 3154116608 | bytes 10485760 | tf_op jit(solution)/shard_map/first_and_send/pallas_call | solution.py:374
  65.6 0.4 collective-permute-start.16
  66.0 2.7 %keep_product.2 = (bf16[1,1024,1024]{2,1,0:T(8,128)(2,1)}, bf16[2,1280,512]{2,1,0:T(8,128)(2,1)S(1)}) custom-call(f32[1,1024]{1,0:T(1,128)S(1)} %get-tuple-element.46.refs_0_, f32[1024,128]{1,0:T(8,128)S(1)} %get-tuple-element.47.refs_1_, bf16[1280,512]{1,0:T(8,128)(2,1)S(1)} %first_product.1.middle.refs_2_, ...), custom_call_target="tpu_custom_call" | custom-call | flops 1342177280 | bytes 6291456 | tf_op jit(solution)/shard_map/keep_product/pallas_call | solution.py:465
  68.7 2.3 %keep_product.3 = bf16[1,1024,1024]{2,1,0:T(8,128)(2,1)} custom-call(f32[1,1024]{1,0:T(1,128)S(1)} %get-tuple-element.46.refs_0_, f32[1024,128]{1,0:T(8,128)S(1)} %get-tuple-element.47.refs_1_, bf16[1280,512]{1,0:T(8,128)(2,1)S(1)} %get-tuple-element.80.refs_2_, ...), custom_call_target="tpu_custom_call", output_to_operand_aliasing={{}: (5, {})} | custom-call | flops 1342177280 | bytes 6291456 | tf_op jit(solution)/shard_map/keep_product/pallas_call | solution.py:465
  (46 shorter events, 2.5 us)
Async XLA Ops:
  1.0 8.7 %collective-permute-start = (bf16[1280,128]{1,0:T(8,128)(2,1)S(1)}, bf16[1280,128]{1,0:T(8,128)(2,1)S(1)}, u32[]{:S(2)}, u32[]{:S(2)}) collective-permute-start(bf16[1280,128]{1,0:T(8,128)(2,1)S(1)} %constant_dynamic-slice_fusion), channel_id=1, source_target_pairs={{0,4},{4,12},{12,8},{8,0},{1,5},{5,13},{13,9},{9,1},{2,6},{6,14},{... | collective-permute-start | bytes 983048 | tf_op jit(solution)/shard_map/ppermute | solution.py:501
  3.4 1.3 %copy-start = (bf16[1280,512]{1,0:T(8,128)(2,1)S(1)}, bf16[1280,512]{1,0:T(8,128)(2,1)}, u32[]{:S(2)}) copy-start(bf16[1280,512]{1,0:T(8,128)(2,1)} %value.1) | copy-start | bytes 3932164
  4.7 1.1 %copy-start.5 = (bf16[4,1,6,128,128]{4,3,2,1,0:T(8,128)(2,1)S(1)}, bf16[4,1,6,128,128]{4,3,2,1,0:T(8,128)(2,1)}, u32[]{:S(2)}) copy-start(bf16[4,1,6,128,128]{4,3,2,1,0:T(8,128)(2,1)} %param.7) | copy-start | bytes 2359300
  4.8 10.5 %copy-start.8 = (s32[1,24,2]{1,2,0:T(2,128)S(1)}, s32[1,24,2]{1,2,0:T(2,128)}, u32[]{:S(2)}) copy-start(s32[1,24,2]{1,2,0:T(2,128)} %param.12) | copy-start | bytes 580
  4.8 10.6 %copy-start.1 = (f32[2048]{0:T(1024)S(1)}, f32[2048]{0:T(1024)}, u32[]{:S(2)}) copy-start(f32[2048]{0:T(1024)} %param.10) | copy-start | bytes 24580
  4.8 10.6 %copy-start.2 = (f32[400]{0:T(512)S(1)}, f32[400]{0:T(512)}, u32[]{:S(2)}) copy-start(f32[400]{0:T(512)} %eps_occ.1) | copy-start | bytes 4804
  4.8 10.6 %copy-start.3 = (s32[2,12]{1,0:T(2,128)S(1)}, s32[2,12]{1,0:T(2,128)}, u32[]{:S(2)}) copy-start(s32[2,12]{1,0:T(2,128)} %extra.1) | copy-start | bytes 292
  4.8 10.6 %copy-start.4 = (s32[1,2]{1,0:T(1,128)S(1)}, s32[1,2]{1,0:T(1,128)}, u32[]{:S(2)}) copy-start(s32[1,2]{1,0:T(1,128)} %pair_occ.1) | copy-start | bytes 28
  9.7 8.6 %collective-permute-start.1 = (bf16[1280,128]{1,0:T(8,128)(2,1)S(1)}, bf16[1280,128]{1,0:T(8,128)(2,1)S(1)}, u32[]{:S(2)}, u32[]{:S(2)}) collective-permute-start(bf16[1280,128]{1,0:T(8,128)(2,1)S(1)} %collective-permute-done.own), channel_id=1, source_target_pairs={{0,4},{4,12},{12,8},{8,0},{1,5},{5,13},{13,9},{9,1},{2,6},{6,14},{... | collective-permute-start | bytes 983048 | tf_op jit(solution)/shard_map/ppermute | solution.py:501
  12.8 7.4 %collective-permute-start.2 = (bf16[1280,128]{1,0:T(8,128)(2,1)S(1)}, bf16[1280,128]{1,0:T(8,128)(2,1)S(1)}, u32[]{:S(2)}, u32[]{:S(2)}) collective-permute-start(bf16[1280,128]{1,0:T(8,128)(2,1)S(1)} %collective-permute-done.own), channel_id=1, source_target_pairs={{0,16},{16,0},{1,17},{17,1},{2,18},{18,2},{3,19},{19,3},{4,20},{20... | collective-permute-start | bytes 983048 | tf_op jit(solution)/shard_map/ppermute | solution.py:497
  14.1 7.1 %collective-permute-start.3 = (bf16[1280,128]{1,0:T(8,128)(2,1)S(1)}, bf16[1280,128]{1,0:T(8,128)(2,1)S(1)}, u32[]{:S(2)}, u32[]{:S(2)}) collective-permute-start(bf16[1280,128]{1,0:T(8,128)(2,1)S(1)} %collective-permute-done.own), channel_id=1, source_target_pairs={{0,2},{2,0},{1,3},{3,1},{4,6},{6,4},{5,7},{7,5},{8,10},{10,8},{9,1... | collective-permute-start | bytes 983048 | tf_op jit(solution)/shard_map/ppermute | solution.py:493
  15.4 8.7 %copy-start.7 = (bf16[6,128,128]{2,1,0:T(8,128)(2,1)S(1)}, bf16[6,128,128]{2,1,0:T(8,128)(2,1)}, u32[]{:S(2)}) copy-start(bf16[6,128,128]{2,1,0:T(8,128)(2,1)} %get-tuple-element.58) | copy-start | bytes 589828
  21.3 13.0 %copy-start.6 = (bf16[6,128,128]{2,1,0:T(8,128)(2,1)S(1)}, bf16[6,128,128]{2,1,0:T(8,128)(2,1)}, u32[]{:S(2)}) copy-start(bf16[6,128,128]{2,1,0:T(8,128)(2,1)} %get-tuple-element.67) | copy-start | bytes 589828
  21.3 11.5 %collective-permute-start.4 = (bf16[1920,128]{1,0:T(8,128)(2,1)S(1)}, bf16[1920,128]{1,0:T(8,128)(2,1)S(1)}, u32[]{:S(2)}, u32[]{:S(2)}) collective-permute-start(bf16[1920,128]{1,0:T(8,128)(2,1)S(1)} %get-tuple-element.94), channel_id=1, source_target_pairs={{0,2},{2,0},{1,3},{3,1},{4,6},{6,4},{5,7},{7,5},{8,10},{10,8},{9,1... | collective-permute-start | bytes 1474568 | tf_op jit(solution)/shard_map/ppermute | solution.py:493
  22.6 10.2 %collective-permute-start.5 = (bf16[1920,128]{1,0:T(8,128)(2,1)S(1)}, bf16[1920,128]{1,0:T(8,128)(2,1)S(1)}, u32[]{:S(2)}, u32[]{:S(2)}) collective-permute-start(bf16[1920,128]{1,0:T(8,128)(2,1)S(1)} %get-tuple-element.93), channel_id=1, source_target_pairs={{0,16},{16,0},{1,17},{17,1},{2,18},{18,2},{3,19},{19,3},{4,20},{20... | collective-permute-start | bytes 1474568 | tf_op jit(solution)/shard_map/ppermute | solution.py:497
  22.9 9.9 %collective-permute-start.6 = (bf16[1280,128]{1,0:T(8,128)(2,1)S(1)}, bf16[1280,128]{1,0:T(8,128)(2,1)S(1)}, u32[]{:S(2)}, u32[]{:S(2)}) collective-permute-start(bf16[1280,128]{1,0:T(8,128)(2,1)S(1)} %collective-permute-done.1.own), channel_id=1, source_target_pairs={{0,4},{4,12},{12,8},{8,0},{1,5},{5,13},{13,9},{9,1},{2,6},{6,14},{... | collective-permute-start | bytes 983048 | tf_op jit(solution)/shard_map/ppermute | solution.py:501
  24.0 8.7 %collective-permute-start.7 = (bf16[6,128,128]{2,1,0:T(8,128)(2,1)S(1)}, bf16[6,128,128]{2,1,0:T(8,128)(2,1)S(1)}, u32[]{:S(2)}, u32[]{:S(2)}) collective-permute-start(bf16[6,128,128]{2,1,0:T(8,128)(2,1)S(1)} %copy-done.7), channel_id=1, source_target_pairs={{0,4},{4,12},{12,8},{8,0},{1,5},{5,13},{13,9},{9,1},{2,6},{6,14},{... | collective-permute-start | bytes 589832 | tf_op jit(solution)/shard_map/ppermute | solution.py:501
  32.9 15.4 %collective-permute-start.8 = (bf16[1920,128]{1,0:T(8,128)(2,1)S(1)}, bf16[1920,128]{1,0:T(8,128)(2,1)S(1)}, u32[]{:S(2)}, u32[]{:S(2)}) collective-permute-start(bf16[1920,128]{1,0:T(8,128)(2,1)S(1)} %get-tuple-element.92), channel_id=1, source_target_pairs={{0,2},{2,0},{1,3},{3,1},{4,6},{6,4},{5,7},{7,5},{8,10},{10,8},{9,1... | collective-permute-start | bytes 1474568 | tf_op jit(solution)/shard_map/ppermute | solution.py:493
  33.2 15.1 %collective-permute-start.9 = (bf16[1920,128]{1,0:T(8,128)(2,1)S(1)}, bf16[1920,128]{1,0:T(8,128)(2,1)S(1)}, u32[]{:S(2)}, u32[]{:S(2)}) collective-permute-start(bf16[1920,128]{1,0:T(8,128)(2,1)S(1)} %get-tuple-element.91), channel_id=1, source_target_pairs={{0,16},{16,0},{1,17},{17,1},{2,18},{18,2},{3,19},{19,3},{4,20},{20... | collective-permute-start | bytes 1474568 | tf_op jit(solution)/shard_map/ppermute | solution.py:497
  34.3 14.0 %collective-permute-start.10 = (bf16[6,128,128]{2,1,0:T(8,128)(2,1)S(1)}, bf16[6,128,128]{2,1,0:T(8,128)(2,1)S(1)}, u32[]{:S(2)}, u32[]{:S(2)}) collective-permute-start(bf16[6,128,128]{2,1,0:T(8,128)(2,1)S(1)} %copy-done.6), channel_id=1, source_target_pairs={{0,12},{4,8},{12,0},{8,4},{1,13},{5,9},{13,1},{9,5},{2,14},{6,10},... | collective-permute-start | bytes 589832 | tf_op jit(solution)/shard_map/ppermute | solution.py:501
  34.3 14.0 %collective-permute-start.11 = (bf16[6,128,128]{2,1,0:T(8,128)(2,1)S(1)}, bf16[6,128,128]{2,1,0:T(8,128)(2,1)S(1)}, u32[]{:S(2)}, u32[]{:S(2)}) collective-permute-start(bf16[6,128,128]{2,1,0:T(8,128)(2,1)S(1)} %get-tuple-element.68), channel_id=1, source_target_pairs={{0,8},{4,0},{12,4},{8,12},{1,9},{5,1},{13,5},{9,13},{2,10},{6,2},{... | collective-permute-start | bytes 589832 | tf_op jit(solution)/shard_map/ppermute | solution.py:501
  48.7 5.4 %collective-permute-start.14 = (bf16[1280,512]{1,0:T(8,128)(2,1)S(1)}, bf16[1280,512]{1,0:T(8,128)(2,1)S(1)}, u32[]{:S(2)}, u32[]{:S(2)}) collective-permute-start(bf16[1280,512]{1,0:T(8,128)(2,1)S(1)} %choose.1.refs_3_), channel_id=1, source_target_pairs={{0,1},{1,0},{2,3},{3,2},{4,5},{5,4},{6,7},{7,6},{8,9},{9,8},{10,11... | collective-permute-start | bytes 3932168 | tf_op jit(solution)/shard_map/ppermute | solution.py:489
  50.6 5.9 %collective-permute-start.12 = (bf16[640,128]{1,0:T(8,128)(2,1)S(1)}, bf16[640,128]{1,0:T(8,128)(2,1)S(1)}, u32[]{:S(2)}, u32[]{:S(2)}) collective-permute-start(bf16[640,128]{1,0:T(8,128)(2,1)S(1)} %slice.22), channel_id=1, source_target_pairs={{0,2},{2,0},{1,3},{3,1},{4,6},{6,4},{5,7},{7,5},{8,10},{10,8},{9,1... | collective-permute-start | bytes 491528 | tf_op jit(solution)/shard_map/ppermute | solution.py:493
  51.9 5.5 %collective-permute-start.13 = (bf16[640,128]{1,0:T(8,128)(2,1)S(1)}, bf16[640,128]{1,0:T(8,128)(2,1)S(1)}, u32[]{:S(2)}, u32[]{:S(2)}) collective-permute-start(bf16[640,128]{1,0:T(8,128)(2,1)S(1)} %slice.23), channel_id=1, source_target_pairs={{0,16},{16,0},{1,17},{17,1},{2,18},{18,2},{3,19},{19,3},{4,20},{20... | collective-permute-start | bytes 491528 | tf_op jit(solution)/shard_map/ppermute | solution.py:497
  57.8 3.8 %collective-permute-start.15 = (bf16[1280,512]{1,0:T(8,128)(2,1)S(1)}, bf16[1280,512]{1,0:T(8,128)(2,1)S(1)}, u32[]{:S(2)}, u32[]{:S(2)}) collective-permute-start(bf16[1280,512]{1,0:T(8,128)(2,1)S(1)} %get-tuple-element.78.refs_2_), channel_id=1, source_target_pairs={{0,1},{1,0},{2,3},{3,2},{4,5},{5,4},{6,7},{7,6},{8,9},{9,8},{10,11... | collective-permute-start | bytes 3932168 | tf_op jit(solution)/shard_map/ppermute | solution.py:489
  60.7 5.3 %collective-permute-start.17 = (bf16[2,512,512]{2,1,0:T(8,128)(2,1)S(1)}, bf16[2,512,512]{2,1,0:T(8,128)(2,1)S(1)}, u32[]{:S(2)}, u32[]{:S(2)}) collective-permute-start(bf16[2,512,512]{2,1,0:T(8,128)(2,1)S(1)} %send_product.1), channel_id=1, source_target_pairs={{0,1},{1,0},{2,3},{3,2},{4,5},{5,4},{6,7},{7,6},{8,9},{9,8},{10,11... | collective-permute-start | bytes 3145736 | tf_op jit(solution)/shard_map/ppermute | solution.py:489
  65.6 3.2 %collective-permute-start.16 = (bf16[2,512,512]{2,1,0:T(8,128)(2,1)S(1)}, bf16[2,512,512]{2,1,0:T(8,128)(2,1)S(1)}, u32[]{:S(2)}, u32[]{:S(2)}) collective-permute-start(bf16[2,512,512]{2,1,0:T(8,128)(2,1)S(1)} %get-tuple-element.81), channel_id=1, source_target_pairs={{0,1},{1,0},{2,3},{3,2},{4,5},{5,4},{6,7},{7,6},{8,9},{9,8},{10,11... | collective-permute-start | bytes 3145736 | tf_op jit(solution)/shard_map/ppermute | solution.py:489
